TPU v7x, 256 devices: a whole 4x4x8 slice. The times are simulated.
256 devices in a mesh: rep: 32 (over z_hi, x, core), fsdp: 8 (over y, z_lo).
Axes of the slice: x: 4, y: 4, z: 8 (z_hi: 4, z_lo: 2; z = z_hi * 2 + z_lo), core: 2. Of those that a mesh axis runs over, the one named last changes fastest.
Arguments:
- local_weights: bfloat16 [32, 5120, 512], P('rep', 'fsdp'), may hold values from -6 to 6
- global_weights: float32 [5120, 512], P('fsdp'), may hold values from -6 to 6
- momentum: float32 [5120, 512], P('fsdp'), may hold values from -6 to 6
- tokens: bfloat16 [131072, 5120], P(('rep', 'fsdp')), may hold values from -0.375 to 0.375
- key_grad: bfloat16 [131072, 512], P(('rep', 'fsdp')), may hold values from -6 to 6
Outputs:
- new_global: float32 [5120, 512], P('fsdp')
- new_momentum: float32 [5120, 512], P('fsdp')
- inner_keys: bfloat16 [131072, 512], P(('rep', 'fsdp'))
- weight_grad: bfloat16 [32, 5120, 512], P('rep', 'fsdp')
All inputs are finite; a program needn't handle non-finite values.
Results may differ from a plain program's by a relative error of at most 0.0049.
Values may be sent and summed in bfloat16 or wider, within the bound.
No kernel may reach another device: no remote copies, remote signals or barrier semaphores. Data moves between devices by JAX's collectives and lax.ppermute only.
A program may use at most 128 MiB of HBM per device.

v0:
```python
import jax
import jax.numpy as jnp
from jax import lax
from jax.sharding import PartitionSpec as P

momentum_rate = 0.9
outer_rate = 0.7


def per_device(local_weights, global_weights, momentum, tokens, key_grad):
    replicas = lax.axis_size("rep")
    outer_grad = global_weights - local_weights[0].astype(jnp.float32)
    summed = lax.psum(outer_grad, "rep")
    average = summed / replicas
    new_momentum = momentum_rate * momentum + average
    new_global = global_weights - outer_rate * (average + momentum_rate * new_momentum)
    start_weights = new_global.astype(jnp.bfloat16)
    columns = tokens
    inner_keys = jnp.dot(
        columns,
        lax.all_gather(start_weights, "fsdp", axis=0, tiled=True),
        preferred_element_type=jnp.float32,
    ).astype(jnp.bfloat16)
    columns = tokens
    grad_rows = lax.psum_scatter(
        lax.dot_general(
            columns, key_grad, (((0,), (0,)), ((), ())), preferred_element_type=jnp.float32
        ),
        "fsdp",
        scatter_dimension=0,
        tiled=True,
    )
    weight_grad = grad_rows.astype(jnp.bfloat16)[None]
    return (new_global, new_momentum, inner_keys, weight_grad)


def solution(mesh):
    placed = (
        P("rep", "fsdp", None),
        P("fsdp", None),
        P("fsdp", None),
        P(("rep", "fsdp"), None),
        P(("rep", "fsdp"), None),
    )
    return jax.shard_map(
        per_device,
        mesh=mesh,
        in_specs=placed,
        out_specs=(
            P("fsdp", None),
            P("fsdp", None),
            P(("rep", "fsdp"), None),
            P("rep", "fsdp", None),
        ),
        check_vma=False,
    )
```

profile of v0, /device:TPU:1, one launch (start us, length us, event | category | flops | bytes accessed | tf_op | source)
XLA Modules:
  0.0 642.0 jit_solution(12402348356338065704)
XLA Ops:
  7.2 0.0 copy-start
  7.2 0.0 all-reduce.2.cloned.1.call-start
  7.2 0.0 copy-start.2
  7.2 2.9 convert_subtract_fusion
  10.1 0.0 copy-start.1
  10.1 0.0 all-reduce.2.cloned.1.call-update
  10.1 0.0 all-gather.2.cloned.1.call-start
  10.2 293.2 %all-reduce.2.cloned.1.call-done = f32[640,512]{1,0:T(8,128)} async-done(((f32[640,512]{1,0:T(8,128)}), f32[640,512]{1,0:T(8,128)}) %all-reduce.2.cloned.1.call-update) | async-done | bytes 1310736 | tf_op jit(solution)/shard_map/psum | solution.py:13
  303.4 0.0 copy-done.2
  303.4 0.0 copy-done.1
  303.4 3.5 fusion.1
  306.9 0.0 all-gather.2.cloned.1.call-update
  306.9 0.0 reduce-scatter.2.cloned.1.call-start
  307.0 0.0 copy-done
  307.0 8.2 %fusion.2 = f32[5120,512]{1,0:T(8,128)} fusion(bf16[512,5120]{1,0:T(8,128)(2,1)} %param.8, bf16[512,512]{1,0:T(8,128)(2,1)S(1)} %copy-done), kind=kOutput, calls=%fused_computation.7 | convolution fusion | flops 2684354560 | bytes 16252928 | tf_op jit(solution)/shard_map/dot_general | solution.py:26
  315.2 0.0 reduce-scatter.2.cloned.1.call-update
  315.2 103.5 %all-gather.2.cloned.1.call-done = bf16[5120,512]{1,0:T(8,128)(2,1)} async-done(((bf16[640,512]{1,0:T(8,128)(2,1)}), bf16[5120,512]{1,0:T(8,128)(2,1)}) %all-gather.2.cloned.1.call-update) | async-done | bytes 5242896 | tf_op jit(solution)/shard_map/all_gather | solution.py:21
  418.7 7.0 %fusion = bf16[512,512]{0,1:T(8,128)(2,1)S(1)} fusion(bf16[5120,512]{1,0:T(8,128)(2,1)} %all-gather.2.cloned.1.call-done, bf16[512,5120]{1,0:T(8,128)(2,1)} %param.8), kind=kOutput, calls=%fused_computation.4 | convolution fusion | flops 2684616704 | bytes 11010048 | tf_op jit(solution)/shard_map/dot_general | solution.py:19
  425.7 1.0 copy.9
  426.7 206.6 %reduce-scatter.2.cloned.1.call-done = f32[640,512]{1,0:T(8,128)} async-done(((f32[5120,512]{1,0:T(8,128)}), f32[640,512]{1,0:T(8,128)}) %reduce-scatter.2.cloned.1.call-update) | async-done | bytes 1310736 | tf_op jit(solution)/shard_map/reduce_scatter | solution.py:25
  633.3 2.2 convert_bitcast_fusion
Async XLA Ops:
  7.2 299.8 %copy-start = (bf16[512,512]{1,0:T(8,128)(2,1)S(1)}, bf16[512,512]{1,0:T(8,128)(2,1)}, u32[]{:S(2)}) copy-start(bf16[512,512]{1,0:T(8,128)(2,1)} %param.9) | copy-start | bytes 1572868
  7.2 296.2 %all-reduce.2.cloned.1.call-start = ((), (), s32[]{:S(2)}) async-start(), calls=%async_computation.1 | async-start | bytes 2621440 | tf_op jit(solution)/shard_map/psum | solution.py:13
  7.2 296.1 %copy-start.2 = (f32[640,512]{1,0:T(8,128)S(1)}, f32[640,512]{1,0:T(8,128)}, u32[]{:S(2)}) copy-start(f32[640,512]{1,0:T(8,128)} %param.7) | copy-start | bytes 3932164
  10.1 293.3 %copy-start.1 = (f32[640,512]{1,0:T(8,128)S(1)}, f32[640,512]{1,0:T(8,128)}, u32[]{:S(2)}) copy-start(f32[640,512]{1,0:T(8,128)} %param.6) | copy-start | bytes 3932164
  10.1 408.6 %all-gather.2.cloned.1.call-start = ((), (), s32[]{:S(2)}) async-start(), calls=%async_computation.2 | async-start | bytes 5898240 | tf_op jit(solution)/shard_map/all_gather | solution.py:21
  306.9 326.3 %reduce-scatter.2.cloned.1.call-start = ((), (), s32[]{:S(2)}) async-start(), calls=%async_computation.3 | async-start | bytes 11796480 | tf_op jit(solution)/shard_map/reduce_scatter | solution.py:25
Sparse Core Ops, SparseCore 0:
  11.2 292.1 all-reduce.1
  307.1 111.5 all-gather.1
  421.4 211.8 reduce-scatter.1
where the time goes:
time: 642 us
  waiting for transfers between devices  603 us (94%)
  matrix products  15.1 us (2%)
  between operations  13.8 us (2%)
  other arithmetic  8.64 us (1%)
    psum x1, waiting for transfers between devices, per_device(): summed = lax.psum(outer_grad, 'rep')  293 us
    reduce_scatter x1, waiting for transfers between devices, per_device(): lax.psum_scatter(lax.dot_general(columns, key_grad, (((0,), (0,)), ((), (...  207 us
    all_gather x1, waiting for transfers between devices, per_device(): lax.all_gather(start_weights, 'fsdp', axis=0, tiled=True)  103 us
  transfers between devices with their start and end apart: 3, of which 3 were waited for; matrix products, arithmetic and copies ran while one was open for 3% of the time, Pallas kernels for 0%

commit v1 on v0

v1 whole, which is shorter than its diff:
```python
import jax
import jax.numpy as jnp
from jax import lax
from jax.experimental import pallas as pl
from jax.experimental.pallas import tpu as pltpu
from jax.sharding import PartitionSpec as P

momentum_rate = 0.9
outer_rate = 0.7

F32, BF16 = jnp.float32, jnp.bfloat16
AXES = ("rep", "fsdp")
SIZES = (4, 4, 2, 4, 2)
REPLICAS = 32
D, KW, SHARD = 5120, 512, 640
TOK = 512
ROWS, COLS = 160, 256
FIRST = 256
LATER = SHARD - FIRST


def shift(value, zh=0, x=0, core=0, y=0, zl=0):
    steps = (zh, x, core, y, zl)

    def index(place):
        n = 0
        for p, size in zip(place, SIZES):
            n = n * size + p
        return n

    pairs = []
    for a in range(4):
        for b in range(4):
            for c in range(2):
                for d in range(4):
                    for e in range(2):
                        place = (a, b, c, d, e)
                        to = tuple((p + s) % n for p, s, n in zip(place, steps, SIZES))
                        pairs.append((index(place), index(to)))
    return lax.ppermute(value, AXES, pairs)


def grad_kernel(order, tokens, key_grad, f0, f1, f2, f3, mine, other):
    step = pl.program_id(0)
    part = lax.dot_general(
        tokens[...], key_grad[...], (((0,), (0,)), ((), ())), preferred_element_type=F32
    ).astype(BF16)
    for k, ref in enumerate((f0, f1, f2, f3)):

        @pl.when(step // 2 == k)
        def _(ref=ref):
            ref[0] = part[:FIRST]

    @pl.when(step % 2 == 0)
    def _():
        mine[0] = part[FIRST:]

    @pl.when(step % 2 == 1)
    def _():
        other[0] = part[FIRST:]


def grad_parts(order, tokens, key_grad):
    def first(k):
        return pl.BlockSpec((1, FIRST, KW), lambda s, o: (jnp.clip(s - 2 * k, 0, 1), 0, 0))

    later = pl.BlockSpec((1, LATER, KW), lambda s, o: (s // 2, 0, 0))
    return pl.pallas_call(
        grad_kernel,
        grid_spec=pltpu.PrefetchScalarGridSpec(
            num_scalar_prefetch=1,
            grid=(8,),
            in_specs=[
                pl.BlockSpec((TOK, SHARD), lambda s, o: (0, o[s])),
                pl.BlockSpec((TOK, KW), lambda s, o: (0, 0)),
            ],
            out_specs=[first(0), first(1), first(2), first(3), later, later],
        ),
        out_shape=[jax.ShapeDtypeStruct((2, FIRST, KW), BF16)] * 4
        + [jax.ShapeDtypeStruct((4, LATER, KW), BF16)] * 2,
        compiler_params=pltpu.CompilerParams(vmem_limit_bytes=32 << 20),
        cost_estimate=pl.CostEstimate(flops=2 * TOK * D * KW, bytes_accessed=11 << 20, transcendentals=0),
    )(order, tokens, key_grad)


def pair_kernel(order, g, l0, l1, own, p1, p2, p3):
    step = pl.program_id(0)
    total = 2.0 * g[...] - l0[...].astype(F32) - l1[...].astype(F32)

    @pl.when(step == 0)
    def _():
        own[...] = total

    for k, ref in enumerate((p1, p2, p3)):

        @pl.when(step == k + 1)
        def _(ref=ref):
            ref[...] = total.astype(BF16)


def pair_sums(order, g, l0, l1):
    block = pl.BlockSpec((ROWS, COLS), lambda s, o: (o[16 + s], o[24]))
    out = pl.BlockSpec((ROWS, COLS), lambda s, o: (0, 0))
    return pl.pallas_call(
        pair_kernel,
        grid_spec=pltpu.PrefetchScalarGridSpec(
            num_scalar_prefetch=1, grid=(4,), in_specs=[block] * 3, out_specs=[out] * 4
        ),
        out_shape=[jax.ShapeDtypeStruct((ROWS, COLS), F32)]
        + [jax.ShapeDtypeStruct((ROWS, COLS), BF16)] * 3,
    )(order, g, l0, l1)


def step_kernel(order, own, r1, r2, r3, g, m, average, start):
    avg = (own[...] + r1[...].astype(F32) + r2[...].astype(F32) + r3[...].astype(F32)) / REPLICAS
    new_m = momentum_rate * m[...] + avg
    new_g = g[...] - outer_rate * (avg + momentum_rate * new_m)
    average[...] = avg
    start[...] = new_g.astype(BF16)


def outer_step(order, own, r1, r2, r3, g, m):
    here = pl.BlockSpec((ROWS, COLS), lambda s, o: (0, 0))
    block = pl.BlockSpec((ROWS, COLS), lambda s, o: (o[16], o[24]))
    return pl.pallas_call(
        step_kernel,
        grid_spec=pltpu.PrefetchScalarGridSpec(
            num_scalar_prefetch=1, grid=(1,), in_specs=[here] * 4 + [block] * 2, out_specs=[here] * 2
        ),
        out_shape=[
            jax.ShapeDtypeStruct((ROWS, COLS), F32),
            jax.ShapeDtypeStruct((ROWS, COLS), BF16),
        ],
    )(order, own, r1, r2, r3, g, m)


def update_kernel(order, average, g, m, new_global, new_momentum):
    avg = average[0]
    new_m = momentum_rate * m[...] + avg
    new_momentum[...] = new_m
    new_global[...] = g[...] - outer_rate * (avg + momentum_rate * new_m)


def update(order, average, g, m):
    block = pl.BlockSpec(
        (ROWS, COLS), lambda h, s, o: (o[20 + s], (o[24] + h) % 2)
    )
    return pl.pallas_call(
        update_kernel,
        grid_spec=pltpu.PrefetchScalarGridSpec(
            num_scalar_prefetch=1,
            grid=(2, 4),
            in_specs=[
                pl.BlockSpec((1, ROWS, COLS), lambda h, s, o: (h * 4 + s, 0, 0)),
                block,
                block,
            ],
            out_specs=[block] * 2,
        ),
        out_shape=[jax.ShapeDtypeStruct((SHARD, KW), F32)] * 2,
    )(order, average, g, m)


def keys_kernel(order, tokens, tokens_other, w0, w1, w2, w3, keys, keys_other, weights, total, total_other):
    step = pl.program_id(0)
    for k, ref in enumerate((w0, w1, w2, w3)):
        weights[pl.ds(pl.multiple_of(order[20 + k] * ROWS, ROWS), ROWS), :] = ref[0]

    @pl.when(step == 0)
    def _():
        total[...] = jnp.zeros_like(total)
        total_other[...] = jnp.zeros_like(total_other)

    total[...] += jnp.dot(tokens[...], weights[...], preferred_element_type=F32)
    total_other[...] += jnp.dot(tokens_other[...], weights[...], preferred_element_type=F32)

    @pl.when(step == 7)
    def _():
        keys[...] = total[...].astype(BF16)
        keys_other[...] = total_other[...].astype(BF16)


def keys_of(order, tokens, tokens_other, blocks):
    rows = pl.BlockSpec((TOK, SHARD), lambda s, o: (0, o[8 + s]))
    block = pl.BlockSpec((1, ROWS, COLS), lambda s, o: (s, 0, 0))
    out = pl.BlockSpec((TOK, COLS), lambda s, o: (0, 0))
    return pl.pallas_call(
        keys_kernel,
        grid_spec=pltpu.PrefetchScalarGridSpec(
            num_scalar_prefetch=1,
            grid=(8,),
            in_specs=[rows] * 2 + [block] * 4,
            out_specs=[out] * 2,
            scratch_shapes=[
                pltpu.VMEM((SHARD, COLS), BF16),
                pltpu.VMEM((TOK, COLS), F32),
                pltpu.VMEM((TOK, COLS), F32),
            ],
        ),
        out_shape=[jax.ShapeDtypeStruct((TOK, COLS), BF16)] * 2,
        compiler_params=pltpu.CompilerParams(vmem_limit_bytes=32 << 20),
        cost_estimate=pl.CostEstimate(flops=2 * TOK * D * KW, bytes_accessed=14 << 20, transcendentals=0),
    )(order, tokens, tokens_other, *blocks)


def per_device(local_weights, global_weights, momentum, tokens, key_grad):
    g, m, local = global_weights, momentum, local_weights[0]
    rep, fsdp = lax.axis_index("rep"), lax.axis_index("fsdp")
    core, x, y, zl = rep % 2, rep // 2 % 4, fsdp // 2, fsdp % 2
    four, two = jnp.arange(4), jnp.arange(2)
    order = jnp.concatenate(
        [
            (((y + four) % 4)[:, None] * 2 + (zl + two)[None] % 2).reshape(8),
            (((y - four) % 4)[:, None] * 2 + (zl + two)[None] % 2).reshape(8),
            (x + four) % 4,
            (x - four) % 4,
            core[None],
        ]
    ).astype(jnp.int32)

    local_other = shift(local, core=1)
    tokens_other = shift(tokens, core=1)

    f0, f1, f2, f3, mine, other = grad_parts(order, tokens, key_grad)

    own, p1, p2, p3 = pair_sums(order, g, local, local_other)
    r1, r2, r3 = (shift(p, x=k + 1) for k, p in enumerate((p1, p2, p3)))

    f1, f2, f3 = (shift(f, y=k + 1) for k, f in enumerate((f1, f2, f3)))
    got = shift(other, zl=1)

    chips = own + r1.astype(F32) + r2.astype(F32) + r3.astype(F32)
    sent = chips.astype(BF16)
    q1, q2, q3 = (shift(sent, zh=k) for k in (1, 2, 3))
    average, start = outer_step(order, chips, q1, q2, q3, g, m)

    pair = jnp.stack([start, shift(start, zl=1)])
    shards = jnp.concatenate([pair] + [shift(pair, y=k) for k in (1, 2, 3)])
    blocks = [shards] + [shift(shards, x=k) for k in (1, 2, 3)]

    half = jnp.stack([average] + [shift(average, x=k) for k in (1, 2, 3)])
    whole = jnp.concatenate([half, shift(half, core=1)])
    new_global, new_momentum = update(order, whole, g, m)

    f_sum = f0.astype(F32) + f1.astype(F32) + f2.astype(F32) + f3.astype(F32)
    f_got = shift(f_sum[1].astype(BF16), zl=1)
    l_sum = mine.astype(F32) + got.astype(F32)
    l_got = [shift(l_sum[k].astype(BF16), y=k) for k in (1, 2, 3)]
    weight_grad = jnp.concatenate(
        [
            f_sum[0] + f_got.astype(F32),
            l_sum[0] + l_got[0].astype(F32) + l_got[1].astype(F32) + l_got[2].astype(F32),
        ]
    ).astype(BF16)[None]

    keys, keys_other = keys_of(order, tokens, tokens_other, blocks)
    keys_got = shift(keys_other, core=1)
    inner_keys = jnp.where(
        core == 0,
        jnp.concatenate([keys, keys_got], axis=1),
        jnp.concatenate([keys_got, keys], axis=1),
    )
    return (new_global, new_momentum, inner_keys, weight_grad)


def solution(mesh):
    placed = (
        P("rep", "fsdp", None),
        P("fsdp", None),
        P("fsdp", None),
        P(("rep", "fsdp"), None),
        P(("rep", "fsdp"), None),
    )
    return jax.shard_map(
        per_device,
        mesh=mesh,
        in_specs=placed,
        out_specs=(
            P("fsdp", None),
            P("fsdp", None),
            P(("rep", "fsdp"), None),
            P("rep", "fsdp", None),
        ),
        check_vma=False,
    )
```

time: 642 us -> 186 us (0.29)
  waiting for transfers between devices: 603 us -> 77.3 us
  starting transfers between devices: 0.12 us -> 53.2 us
  Pallas kernels: 0 us -> 29.5 us
  matrix products: 15.1 us -> 0 us
  between operations: 13.8 us -> 0.8 us
  local copies, waits for them, and re-layouts: 1.02 us -> 13.2 us
    psum x1 -> x0, waiting for transfers between devices: 293 us -> none  [per_device(): summed = lax.psum(outer_grad, 'rep')]
    reduce_scatter x1 -> x0, waiting for transfers between devices: 207 us -> none  [per_device(): lax.psum_scatter(lax.dot_general(columns, key_grad, (((0,), (0,)), ((), (...]
    all_gather x1 -> x0, waiting for transfers between devices: 103 us -> none  [per_device(): lax.all_gather(start_weights, 'fsdp', axis=0, tiled=True)]
    ppermute x0 -> x28, waiting for transfers between devices: none -> 77.3 us  [shift(): return lax.ppermute(value, AXES, pairs)]
    ppermute x0 -> x28, starting transfers between devices: none -> 53.2 us  [shift(): return lax.ppermute(value, AXES, pairs)]
    pallas_call x0 -> x5, Pallas kernels: none -> 29.5 us  [the longest x1 8.82 us: keys_of(): pl.pallas_call(keys_kernel, grid_spec=pltpu.PrefetchScalarGridSpec(num_sc...]
    dot_general x2 -> x0, matrix products: 15.1 us -> none  [the longest x1 8.16 us: per_device(): lax.dot_general(columns, key_grad, (((0,), (0,)), ((), ())), preferred_el...]
    unnamed x7 -> x30, local copies, waits for them, and re-layouts: 1.02 us -> 11.3 us
  transfers between devices with their start and end apart: 3 -> 28, of which waited for: 3 -> 11; matrix products, arithmetic and copies ran while one was open for 3% -> 9% of each run, Pallas kernels for 0% -> 16%
where the time goes in v1:
time: 186 us; the launch traced here: 185 us
  waiting for transfers between devices  77.3 us (42%)
  starting transfers between devices  53.2 us (29%)
  Pallas kernels  29.5 us (16%)
  local copies, waits for them, and re-layouts  13.2 us (7%)
  other arithmetic  10.8 us (6%)
    ppermute x28, waiting for transfers between devices, shift(): return lax.ppermute(value, AXES, pairs)  77.3 us
    ppermute x28, starting transfers between devices, shift(): return lax.ppermute(value, AXES, pairs)  53.2 us
    unnamed x30, local copies, waits for them, and re-layouts  11.3 us
    pallas_call x1, Pallas kernels, keys_of(): pl.pallas_call(keys_kernel, grid_spec=pltpu.PrefetchScalarGridSpec(num_sc...  8.82 us
    pallas_call x1, Pallas kernels, update(): pl.pallas_call(update_kernel, grid_spec=pltpu.PrefetchScalarGridSpec(num_...  7.17 us
    pallas_call x1, Pallas kernels, grad_parts(): pl.pallas_call(grad_kernel, grid_spec=pltpu.PrefetchScalarGridSpec(num_sc...  7.14 us
    pallas_call x1, Pallas kernels, pair_sums(): pl.pallas_call(pair_kernel, grid_spec=pltpu.PrefetchScalarGridSpec(num_sc...  3.79 us
  transfers between devices with their start and end apart: 28, of which 11 were waited for; matrix products, arithmetic and copies ran while one was open for 9% of the time, Pallas kernels for 16%

profile of v1, /device:TPU:1, one launch (start us, length us, event | category | flops | bytes accessed | tf_op | source)
XLA Modules:
  0.0 184.9 jit_solution(17944494685861296354)
XLA Ops:
  0.6 3.3 %collective-permute-start.11 = (bf16[512,5120]{1,0:T(8,128)(2,1)}, bf16[512,5120]{1,0:T(8,128)(2,1)}, u32[]{:S(2)}, u32[]{:S(2)}) collective-permute-start(bf16[512,5120]{1,0:T(8,128)(2,1)} %tokens.3), channel_id=1, source_target_pairs={{0,8},{1,9},{2,10},{3,11},{4,12},{5,13},{6,14},{7,15},{8,0},{9,1},... | collective-permute-start | bytes 15728648 | tf_op jit(solution)/shard_map/ppermute | solution.py:40
  4.0 0.1 broadcast_add_fusion
  4.1 0.1 add.154
  4.1 0.1 add.158
  4.2 0.1 concatenate.32.order
  4.3 2.5 %copy-done = bf16[512,5120]{1,0:T(8,128)(2,1)S(1)} copy-done((bf16[512,5120]{1,0:T(8,128)(2,1)S(1)}, bf16[512,5120]{1,0:T(8,128)(2,1)}, u32[]{:S(2)}) %copy-start) | copy-done | bytes 5242904
  6.8 1.0 copy-done.4
  7.9 7.1 %shard_map.88 = (bf16[2,256,512]{2,1,0:T(8,128)(2,1)S(1)}, bf16[2,256,512]{2,1,0:T(8,128)(2,1)S(1)}, bf16[2,256,512]{2,1,0:T(8,128)(2,1)S(1)}, bf16[2,256,512]{2...) custom-call(s32[25]{0:T(128)S(1)} %concatenate.32.order, ...), custom_call_target="tpu_custom_call" | custom-call | flops 2684354560 | bytes 11534336 | tf_op jit(solution)/shard_map/pallas_call | solution.py:68
  15.0 2.2 %collective-permute-start.21 = (bf16[2,256,512]{2,1,0:T(8,128)(2,1)S(1)}, bf16[2,256,512]{2,1,0:T(8,128)(2,1)S(1)}, u32[]{:S(2)}, u32[]{:S(2)}) collective-permute-start(bf16[2,256,512]{2,1,0:T(8,128)(2,1)S(1)} %get-tuple-element.32), channel_id=1, source_target_pairs={{0,4},{1,5},{2,6},{3,7},{4,0},{5,1},{6,2},{7,3},{8,12},{9,13},{10,... | collective-permute-start | bytes 1572872 | tf_op jit(solution)/shard_map/ppermute | solution.py:40
  17.2 1.1 collective-permute-start.22
  18.3 0.9 collective-permute-start
  19.2 11.0 %collective-permute-done.20 = bf16[2,256,512]{2,1,0:T(8,128)(2,1)S(1)} collective-permute-done((bf16[2,256,512]{2,1,0:T(8,128)(2,1)S(1)}, bf16[2,256,512]{2,1,0:T(8,128)(2,1)S(1)}, u32[]{:S(2)}, u32[]{:S(2)}) %collective-permute-start.20) | collective-permute-done | bytes 524320 | tf_op jit(solution)/shard_map/ppermute | solution.py:40
  30.1 10.3 %collective-permute-done.21 = bf16[2,256,512]{2,1,0:T(8,128)(2,1)S(1)} collective-permute-done((bf16[2,256,512]{2,1,0:T(8,128)(2,1)S(1)}, bf16[2,256,512]{2,1,0:T(8,128)(2,1)S(1)}, u32[]{:S(2)}, u32[]{:S(2)}) %collective-permute-start.21) | collective-permute-done | bytes 524320 | tf_op jit(solution)/shard_map/ppermute | solution.py:40
  40.5 0.7 collective-permute-done.22
  41.2 0.3 convert_add_fusion.1
  41.5 3.8 %shard_map.84 = (f32[160,256]{1,0:T(8,128)}, bf16[160,256]{1,0:T(8,128)(2,1)}, bf16[160,256]{1,0:T(8,128)(2,1)}, bf16[160,256]{1,0:T(8,128)(2,1)}) custom-call(s32[25]{0:T(128)} %copy-done.2, f32[640,512]{1,0:T(8,128)} %g.5, bf16[640,512]{1,0:T(8,128)(2,1)} %bitcast.50, bf16[640,512]{1,0:T(8,128)(2,1)} %collective-permute-done.l1), custom_call_target="tpu_custom_call" | custom-call | tf_op jit(solution)/shard_map/pallas_call | solution.py:104
  45.3 0.4 collective-permute-start.1
  45.7 2.5 %collective-permute-start.2 = (bf16[160,256]{1,0:T(8,128)(2,1)}, bf16[160,256]{1,0:T(8,128)(2,1)S(1)}, u32[]{:S(2)}, u32[]{:S(2)}) collective-permute-start(bf16[160,256]{1,0:T(8,128)(2,1)} %get-tuple-element.22), channel_id=1, source_target_pairs={{0,32},{1,33},{2,34},{3,35},{4,36},{5,37},{6,38},{7,39},{8,40},{9,... | collective-permute-start | bytes 245768 | tf_op jit(solution)/shard_map/ppermute | solution.py:40
  48.2 1.1 collective-permute-start.3
  49.4 1.7 collective-permute-start.23
  51.1 0.1 collective-permute-start.24
  51.2 0.3 collective-permute-done.2
  51.5 0.6 collective-permute-done.3
  52.1 1.6 fusion.17
  53.7 3.5 %collective-permute-start.4 = (bf16[160,256]{1,0:T(8,128)(2,1)S(1)}, bf16[160,256]{1,0:T(8,128)(2,1)S(1)}, u32[]{:S(2)}, u32[]{:S(2)}) collective-permute-start(bf16[160,256]{1,0:T(8,128)(2,1)S(1)} %get-tuple-element.36), channel_id=1, source_target_pairs={{0,64},{1,65},{2,66},{3,67},{4,68},{5,69},{6,70},{7,71},{8,72},{9,... | collective-permute-start | bytes 245768 | tf_op jit(solution)/shard_map/ppermute | solution.py:40
  57.2 5.1 %collective-permute-start.5 = (bf16[160,256]{1,0:T(8,128)(2,1)S(1)}, bf16[160,256]{1,0:T(8,128)(2,1)S(1)}, u32[]{:S(2)}, u32[]{:S(2)}) collective-permute-start(bf16[160,256]{1,0:T(8,128)(2,1)S(1)} %get-tuple-element.36), channel_id=1, source_target_pairs={{0,128},{1,129},{2,130},{3,131},{4,132},{5,133},{6,134},{7,135},{8... | collective-permute-start | bytes 245768 | tf_op jit(solution)/shard_map/ppermute | solution.py:40
  62.3 2.4 %collective-permute-start.6 = (bf16[160,256]{1,0:T(8,128)(2,1)S(1)}, bf16[160,256]{1,0:T(8,128)(2,1)S(1)}, u32[]{:S(2)}, u32[]{:S(2)}) collective-permute-start(bf16[160,256]{1,0:T(8,128)(2,1)S(1)} %get-tuple-element.36), channel_id=1, source_target_pairs={{0,192},{1,193},{2,194},{3,195},{4,196},{5,197},{6,198},{7,199},{8... | collective-permute-start | bytes 245768 | tf_op jit(solution)/shard_map/ppermute | solution.py:40
  64.7 0.8 fusion.7
  65.5 32.3 %collective-permute-done.4.r1 = bf16[160,256]{1,0:T(8,128)(2,1)S(1)} collective-permute-done((bf16[160,256]{1,0:T(8,128)(2,1)S(1)}, bf16[160,256]{1,0:T(8,128)(2,1)S(1)}, u32[]{:S(2)}, u32[]{:S(2)}) %collective-permute-start.4) | collective-permute-done | bytes 81952 | tf_op jit(solution)/shard_map/ppermute | solution.py:40
  97.8 3.3 %collective-permute-done.5.r2 = bf16[160,256]{1,0:T(8,128)(2,1)S(1)} collective-permute-done((bf16[160,256]{1,0:T(8,128)(2,1)S(1)}, bf16[160,256]{1,0:T(8,128)(2,1)S(1)}, u32[]{:S(2)}, u32[]{:S(2)}) %collective-permute-start.5) | collective-permute-done | bytes 81952 | tf_op jit(solution)/shard_map/ppermute | solution.py:40
  101.1 0.6 copy-done.9
  101.8 2.6 %shard_map.85 = (f32[160,256]{1,0:T(8,128)}, bf16[160,256]{1,0:T(8,128)(2,1)}) custom-call(s32[25]{0:T(128)} %copy-done.2, f32[160,256]{1,0:T(8,128)} %get-tuple-element.37.own, bf16[160,256]{1,0:T(8,128)(2,1)} %copy-done.8, bf16[160,256]{1,0:T(8,128)(2,1)} %copy-done.9, bf16[160,256]{1,0:T(8,128)(2,1)} %copy-done.10, f32[640,512]{1,0:T(8,128)} %g.5, ...), custom_call_target="tpu_custom_call" | custom-call | tf_op jit(solution)/shard_map/pallas_call | solution.py:125
  104.4 1.7 constant_dynamic-update-slice_fusion.4
  106.0 0.9 constant_dynamic-update-slice_fusion.9
  106.9 0.3 collective-permute-start.7
  107.2 1.0 collective-permute-start.8
  108.3 1.5 collective-permute-start.9
  109.7 0.9 pad_maximum_fusion.2
  110.6 3.6 %collective-permute-done.7 = f32[160,256]{1,0:T(8,128)S(1)} collective-permute-done((f32[160,256]{1,0:T(8,128)}, f32[160,256]{1,0:T(8,128)S(1)}, u32[]{:S(2)}, u32[]{:S(2)}) %collective-permute-start.7) | collective-permute-done | bytes 163872 | tf_op jit(solution)/shard_map/ppermute | solution.py:40
  114.3 0.2 collective-permute-start.13
  114.4 0.7 constant_dynamic-update-slice_fusion.3
  115.1 3.6 %collective-permute-start.14 = (bf16[2,160,256]{2,1,0:T(8,128)(2,1)S(1)}, bf16[2,160,256]{2,1,0:T(8,128)(2,1)S(1)}, u32[]{:S(2)}, u32[]{:S(2)}) collective-permute-start(bf16[2,160,256]{2,1,0:T(8,128)(2,1)S(1)} %pad_maximum_fusion.2), channel_id=1, source_target_pairs={{0,4},{1,5},{2,6},{3,7},{4,0},{5,1},{6,2},{7,3},{8,12},{9,13},{10,... | collective-permute-start | bytes 491528 | tf_op jit(solution)/shard_map/ppermute | solution.py:40
  118.8 0.7 constant_dynamic-update-slice_fusion.2
  119.4 0.1 collective-permute-start.15
  119.6 0.1 collective-permute-done.13
  119.6 5.5 %collective-permute-start.10 = (f32[4,160,256]{2,1,0:T(8,128)S(1)}, f32[4,160,256]{2,1,0:T(8,128)S(1)}, u32[]{:S(2)}, u32[]{:S(2)}) collective-permute-start(f32[4,160,256]{2,1,0:T(8,128)S(1)} %pad_maximum_fusion), channel_id=1, source_target_pairs={{0,8},{1,9},{2,10},{3,11},{4,12},{5,13},{6,14},{7,15},{8,0},{9,1},... | collective-permute-start | bytes 1966088 | tf_op jit(solution)/shard_map/ppermute | solution.py:40
  125.2 0.1 collective-permute-start.16
  125.3 0.6 collective-permute-start.17
  125.8 2.1 %collective-permute-start.18 = (bf16[8,160,256]{2,1,0:T(8,128)(2,1)S(1)}, bf16[8,160,256]{2,1,0:T(8,128)(2,1)}, u32[]{:S(2)}, u32[]{:S(2)}) collective-permute-start(bf16[8,160,256]{2,1,0:T(8,128)(2,1)S(1)} %constant_dynamic-update-slice_fusion.5.w0), channel_id=1, source_target_pairs={{0,48},{1,49},{2,50},{3,51},{4,52},{5,53},{6,54},{7,55},{8,56},{9,... | collective-permute-start | bytes 1966088 | tf_op jit(solution)/shard_map/ppermute | solution.py:40
  127.9 3.7 %convert_add_fusion = (f32[4,384,512]{2,1,0:T(8,128)}, bf16[4,384,512]{2,1,0:T(8,128)(2,1)S(1)}) fusion(bf16[4,384,512]{2,1,0:T(8,128)(2,1)} %collective-permute-done.24, bf16[4,384,512]{2,1,0:T(8,128)(2,1)S(1)} %get-tuple-element.34), kind=kLoop, calls=%fused_computation | loop fusion | flops 3145728 | bytes 7864320 | tf_op jit(solution)/shard_map/add | solution.py:247
  131.6 0.8 slice_bitcast_fusion.4
  132.4 0.7 collective-permute-start.25
  133.1 7.6 %collective-permute-done.16.w1 = bf16[8,160,256]{2,1,0:T(8,128)(2,1)S(1)} collective-permute-done((bf16[8,160,256]{2,1,0:T(8,128)(2,1)S(1)}, bf16[8,160,256]{2,1,0:T(8,128)(2,1)S(1)}, u32[]{:S(2)}, u32[]{:S(2)}) %collective-permute-start.16) | collective-permute-done | bytes 655392 | tf_op jit(solution)/shard_map/ppermute | solution.py:40
  140.7 2.6 %collective-permute-start.26 = (bf16[384,512]{1,0:T(8,128)(2,1)S(1)}, bf16[384,512]{1,0:T(8,128)(2,1)}, u32[]{:S(2)}, u32[]{:S(2)}) collective-permute-start(bf16[384,512]{1,0:T(8,128)(2,1)S(1)} %get-tuple-element.42), channel_id=1, source_target_pairs={{0,4},{1,5},{2,6},{3,7},{4,0},{5,1},{6,2},{7,3},{8,12},{9,13},{10,... | collective-permute-start | bytes 1179656 | tf_op jit(solution)/shard_map/ppermute | solution.py:40
  143.3 7.3 %collective-permute-done.17.w2 = bf16[8,160,256]{2,1,0:T(8,128)(2,1)S(1)} collective-permute-done((bf16[8,160,256]{2,1,0:T(8,128)(2,1)S(1)}, bf16[8,160,256]{2,1,0:T(8,128)(2,1)S(1)}, u32[]{:S(2)}, u32[]{:S(2)}) %collective-permute-start.17) | collective-permute-done | bytes 655392 | tf_op jit(solution)/shard_map/ppermute | solution.py:40
  150.7 0.7 constant_dynamic-update-slice_fusion.1
  151.3 0.9 constant_dynamic-update-slice_fusion.average
  152.2 7.2 %shard_map.86 = (f32[640,512]{1,0:T(8,128)}, f32[640,512]{1,0:T(8,128)}) custom-call(s32[25]{0:T(128)} %copy-done.2, f32[8,160,256]{2,1,0:T(8,128)} %constant_dynamic-update-slice_fusion.average, f32[640,512]{1,0:T(8,128)} %g.5, f32[640,512]{1,0:T(8,128)} %m.3), custom_call_target="tpu_custom_call" | custom-call | tf_op jit(solution)/shard_map/pallas_call | solution.py:148
  159.4 2.5 %copy-done.1 = bf16[512,5120]{1,0:T(8,128)(2,1)S(1)} copy-done((bf16[512,5120]{1,0:T(8,128)(2,1)S(1)}, bf16[512,5120]{1,0:T(8,128)(2,1)}, u32[]{:S(2)}) %copy-start.1) | copy-done | bytes 5242904
  161.9 8.8 %shard_map.87 = (bf16[512,256]{1,0:T(8,128)(2,1)S(1)}, bf16[512,256]{1,0:T(8,128)(2,1)S(1)}) custom-call(s32[25]{0:T(128)S(1)} %copy-done.3, bf16[512,5120]{1,0:T(8,128)(2,1)S(1)} %copy-done.1, bf16[512,5120]{1,0:T(8,128)(2,1)} %collective-permute-done.11.tokens_other, bf16[8,160,256]{2,1,0:T(8,128)(2,1)S(1)} %constant_dynamic-update-slice_fusion.5.w0, ...), custom_call_target="tpu_custom_call" | custom-call | flops 2684354560 | bytes 14680064 | tf_op jit(solution)/shard_map/pallas_call | solution.py:187
  170.7 10.7 %collective-permute-start.19 = (bf16[512,256]{1,0:T(8,128)(2,1)S(1)}, bf16[512,256]{1,0:T(8,128)(2,1)S(1)}, u32[]{:S(2)}, u32[]{:S(2)}) collective-permute-start(bf16[512,256]{1,0:T(8,128)(2,1)S(1)} %get-tuple-element.29), channel_id=1, source_target_pairs={{0,8},{1,9},{2,10},{3,11},{4,12},{5,13},{6,14},{7,15},{8,0},{9,1},... | collective-permute-start | bytes 786440 | tf_op jit(solution)/shard_map/ppermute | solution.py:40
  181.5 1.6 fusion.6
  183.1 0.9 pad_maximum_fusion.1
  184.0 0.9 maximum_select_fusion
  (47 shorter events, 0.3 us)
Async XLA Ops:
  0.6 158.7 %collective-permute-start.11 = (bf16[512,5120]{1,0:T(8,128)(2,1)}, bf16[512,5120]{1,0:T(8,128)(2,1)}, u32[]{:S(2)}, u32[]{:S(2)}) collective-permute-start(bf16[512,5120]{1,0:T(8,128)(2,1)} %tokens.3), channel_id=1, source_target_pairs={{0,8},{1,9},{2,10},{3,11},{4,12},{5,13},{6,14},{7,15},{8,0},{9,1},... | collective-permute-start | bytes 15728648 | tf_op jit(solution)/shard_map/ppermute | solution.py:40
  4.3 2.5 %copy-start = (bf16[512,5120]{1,0:T(8,128)(2,1)S(1)}, bf16[512,5120]{1,0:T(8,128)(2,1)}, u32[]{:S(2)}) copy-start(bf16[512,5120]{1,0:T(8,128)(2,1)} %tokens.3) | copy-start | bytes 15728644
  6.8 1.0 copy-start.4
  7.9 7.1 %copy-start.2 = (s32[25]{0:T(128)}, s32[25]{0:T(128)S(1)}, u32[]{:S(2)}) copy-start(s32[25]{0:T(128)S(1)} %concatenate.32.order) | copy-start | bytes 304
  7.9 10.4 %copy-start.7 = (bf16[1,640,512]{2,1,0:T(8,128)(2,1)S(1)}, bf16[1,640,512]{2,1,0:T(8,128)(2,1)}, u32[]{:S(2)}) copy-start(bf16[1,640,512]{2,1,0:T(8,128)(2,1)} %param.5) | copy-start | bytes 1966084
  15.0 15.1 %collective-permute-start.20 = (bf16[2,256,512]{2,1,0:T(8,128)(2,1)S(1)}, bf16[2,256,512]{2,1,0:T(8,128)(2,1)S(1)}, u32[]{:S(2)}, u32[]{:S(2)}) collective-permute-start(bf16[2,256,512]{2,1,0:T(8,128)(2,1)S(1)} %get-tuple-element.31), channel_id=1, source_target_pairs={{0,2},{1,3},{2,4},{3,5},{4,6},{5,7},{6,0},{7,1},{8,10},{9,11},{10,... | collective-permute-start | bytes 1572872 | tf_op jit(solution)/shard_map/ppermute | solution.py:40
  15.0 25.5 %collective-permute-start.21 = (bf16[2,256,512]{2,1,0:T(8,128)(2,1)S(1)}, bf16[2,256,512]{2,1,0:T(8,128)(2,1)S(1)}, u32[]{:S(2)}, u32[]{:S(2)}) collective-permute-start(bf16[2,256,512]{2,1,0:T(8,128)(2,1)S(1)} %get-tuple-element.32), channel_id=1, source_target_pairs={{0,4},{1,5},{2,6},{3,7},{4,0},{5,1},{6,2},{7,3},{8,12},{9,13},{10,... | collective-permute-start | bytes 1572872 | tf_op jit(solution)/shard_map/ppermute | solution.py:40
  17.2 24.0 %collective-permute-start.22 = (bf16[2,256,512]{2,1,0:T(8,128)(2,1)S(1)}, bf16[2,256,512]{2,1,0:T(8,128)(2,1)S(1)}, u32[]{:S(2)}, u32[]{:S(2)}) collective-permute-start(bf16[2,256,512]{2,1,0:T(8,128)(2,1)S(1)} %get-tuple-element.33), channel_id=1, source_target_pairs={{0,6},{1,7},{2,0},{3,1},{4,2},{5,3},{6,4},{7,5},{8,14},{9,15},{10,... | collective-permute-start | bytes 1572872 | tf_op jit(solution)/shard_map/ppermute | solution.py:40
  18.3 23.2 %collective-permute-start = (bf16[640,512]{1,0:T(8,128)(2,1)S(1)}, bf16[640,512]{1,0:T(8,128)(2,1)}, u32[]{:S(2)}, u32[]{:S(2)}) collective-permute-start(bf16[640,512]{1,0:T(8,128)(2,1)S(1)} %bitcast.51), channel_id=1, source_target_pairs={{0,8},{1,9},{2,10},{3,11},{4,12},{5,13},{6,14},{7,15},{8,0},{9,1},... | collective-permute-start | bytes 1966088 | tf_op jit(solution)/shard_map/ppermute | solution.py:40
  45.3 5.8 %collective-permute-start.1 = (bf16[160,256]{1,0:T(8,128)(2,1)}, bf16[160,256]{1,0:T(8,128)(2,1)S(1)}, u32[]{:S(2)}, u32[]{:S(2)}) collective-permute-start(bf16[160,256]{1,0:T(8,128)(2,1)} %get-tuple-element.21), channel_id=1, source_target_pairs={{0,16},{1,17},{2,18},{3,19},{4,20},{5,21},{6,22},{7,23},{8,24},{9,... | collective-permute-start | bytes 245768 | tf_op jit(solution)/shard_map/ppermute | solution.py:40
  45.7 5.8 %collective-permute-start.2 = (bf16[160,256]{1,0:T(8,128)(2,1)}, bf16[160,256]{1,0:T(8,128)(2,1)S(1)}, u32[]{:S(2)}, u32[]{:S(2)}) collective-permute-start(bf16[160,256]{1,0:T(8,128)(2,1)} %get-tuple-element.22), channel_id=1, source_target_pairs={{0,32},{1,33},{2,34},{3,35},{4,36},{5,37},{6,38},{7,39},{8,40},{9,... | collective-permute-start | bytes 245768 | tf_op jit(solution)/shard_map/ppermute | solution.py:40
  48.2 3.9 %collective-permute-start.3 = (bf16[160,256]{1,0:T(8,128)(2,1)}, bf16[160,256]{1,0:T(8,128)(2,1)S(1)}, u32[]{:S(2)}, u32[]{:S(2)}) collective-permute-start(bf16[160,256]{1,0:T(8,128)(2,1)} %get-tuple-element.23), channel_id=1, source_target_pairs={{0,48},{1,49},{2,50},{3,51},{4,52},{5,53},{6,54},{7,55},{8,56},{9,... | collective-permute-start | bytes 245768 | tf_op jit(solution)/shard_map/ppermute | solution.py:40
  49.4 12.9 %collective-permute-start.23 = (bf16[256,512]{1,0:T(8,128)(2,1)S(1)}, bf16[256,512]{1,0:T(8,128)(2,1)S(1)}, u32[]{:S(2)}, u32[]{:S(2)}) collective-permute-start(bf16[256,512]{1,0:T(8,128)(2,1)S(1)} %fusion.8), channel_id=1, source_target_pairs={{0,1},{1,0},{2,3},{3,2},{4,5},{5,4},{6,7},{7,6},{8,9},{9,8},{10,11... | collective-permute-start | bytes 786440 | tf_op jit(solution)/shard_map/ppermute | solution.py:40
  51.1 74.7 %collective-permute-start.24 = (bf16[4,384,512]{2,1,0:T(8,128)(2,1)}, bf16[4,384,512]{2,1,0:T(8,128)(2,1)}, u32[]{:S(2)}, u32[]{:S(2)}) collective-permute-start(bf16[4,384,512]{2,1,0:T(8,128)(2,1)} %get-tuple-element.35), channel_id=1, source_target_pairs={{0,1},{1,0},{2,3},{3,2},{4,5},{5,4},{6,7},{7,6},{8,9},{9,8},{10,11... | collective-permute-start | bytes 4718600 | tf_op jit(solution)/shard_map/ppermute | solution.py:40
  53.7 44.1 %collective-permute-start.4 = (bf16[160,256]{1,0:T(8,128)(2,1)S(1)}, bf16[160,256]{1,0:T(8,128)(2,1)S(1)}, u32[]{:S(2)}, u32[]{:S(2)}) collective-permute-start(bf16[160,256]{1,0:T(8,128)(2,1)S(1)} %get-tuple-element.36), channel_id=1, source_target_pairs={{0,64},{1,65},{2,66},{3,67},{4,68},{5,69},{6,70},{7,71},{8,72},{9,... | collective-permute-start | bytes 245768 | tf_op jit(solution)/shard_map/ppermute | solution.py:40
  57.2 43.9 %collective-permute-start.5 = (bf16[160,256]{1,0:T(8,128)(2,1)S(1)}, bf16[160,256]{1,0:T(8,128)(2,1)S(1)}, u32[]{:S(2)}, u32[]{:S(2)}) collective-permute-start(bf16[160,256]{1,0:T(8,128)(2,1)S(1)} %get-tuple-element.36), channel_id=1, source_target_pairs={{0,128},{1,129},{2,130},{3,131},{4,132},{5,133},{6,134},{7,135},{8... | collective-permute-start | bytes 245768 | tf_op jit(solution)/shard_map/ppermute | solution.py:40
  62.3 38.8 %collective-permute-start.6 = (bf16[160,256]{1,0:T(8,128)(2,1)S(1)}, bf16[160,256]{1,0:T(8,128)(2,1)S(1)}, u32[]{:S(2)}, u32[]{:S(2)}) collective-permute-start(bf16[160,256]{1,0:T(8,128)(2,1)S(1)} %get-tuple-element.36), channel_id=1, source_target_pairs={{0,192},{1,193},{2,194},{3,195},{4,196},{5,197},{6,198},{7,199},{8... | collective-permute-start | bytes 245768 | tf_op jit(solution)/shard_map/ppermute | solution.py:40
  97.8 3.3 %copy-start.8 = (bf16[160,256]{1,0:T(8,128)(2,1)}, bf16[160,256]{1,0:T(8,128)(2,1)S(1)}, u32[]{:S(2)}) copy-start(bf16[160,256]{1,0:T(8,128)(2,1)S(1)} %collective-permute-done.4.r1) | copy-start | bytes 245764
  101.1 0.6 copy-start.9
  101.1 0.6 copy-start.10
  104.4 15.1 %copy-start.6 = (f32[160,256]{1,0:T(8,128)S(1)}, f32[160,256]{1,0:T(8,128)}, u32[]{:S(2)}) copy-start(f32[160,256]{1,0:T(8,128)} %get-tuple-element.24) | copy-start | bytes 491524
  104.4 3.9 %collective-permute-start.12 = (bf16[160,256]{1,0:T(8,128)(2,1)}, bf16[160,256]{1,0:T(8,128)(2,1)S(1)}, u32[]{:S(2)}, u32[]{:S(2)}) collective-permute-start(bf16[160,256]{1,0:T(8,128)(2,1)} %get-tuple-element.27), channel_id=1, source_target_pairs={{0,1},{1,0},{2,3},{3,2},{4,5},{5,4},{6,7},{7,6},{8,9},{9,8},{10,11... | collective-permute-start | bytes 245768 | tf_op jit(solution)/shard_map/ppermute | solution.py:40
  106.9 7.3 %collective-permute-start.7 = (f32[160,256]{1,0:T(8,128)}, f32[160,256]{1,0:T(8,128)S(1)}, u32[]{:S(2)}, u32[]{:S(2)}) collective-permute-start(f32[160,256]{1,0:T(8,128)} %get-tuple-element.24), channel_id=1, source_target_pairs={{0,16},{1,17},{2,18},{3,19},{4,20},{5,21},{6,22},{7,23},{8,24},{9,... | collective-permute-start | bytes 491528 | tf_op jit(solution)/shard_map/ppermute | solution.py:40
  107.2 7.9 %collective-permute-start.8 = (f32[160,256]{1,0:T(8,128)}, f32[160,256]{1,0:T(8,128)S(1)}, u32[]{:S(2)}, u32[]{:S(2)}) collective-permute-start(f32[160,256]{1,0:T(8,128)} %get-tuple-element.24), channel_id=1, source_target_pairs={{0,32},{1,33},{2,34},{3,35},{4,36},{5,37},{6,38},{7,39},{8,40},{9,... | collective-permute-start | bytes 491528 | tf_op jit(solution)/shard_map/ppermute | solution.py:40
  108.3 11.2 %collective-permute-start.9 = (f32[160,256]{1,0:T(8,128)}, f32[160,256]{1,0:T(8,128)S(1)}, u32[]{:S(2)}, u32[]{:S(2)}) collective-permute-start(f32[160,256]{1,0:T(8,128)} %get-tuple-element.24), channel_id=1, source_target_pairs={{0,48},{1,49},{2,50},{3,51},{4,52},{5,53},{6,54},{7,55},{8,56},{9,... | collective-permute-start | bytes 491528 | tf_op jit(solution)/shard_map/ppermute | solution.py:40
  114.3 5.4 %collective-permute-start.13 = (bf16[2,160,256]{2,1,0:T(8,128)(2,1)S(1)}, bf16[2,160,256]{2,1,0:T(8,128)(2,1)S(1)}, u32[]{:S(2)}, u32[]{:S(2)}) collective-permute-start(bf16[2,160,256]{2,1,0:T(8,128)(2,1)S(1)} %pad_maximum_fusion.2), channel_id=1, source_target_pairs={{0,2},{1,3},{2,4},{3,5},{4,6},{5,7},{6,0},{7,1},{8,10},{9,11},{10,... | collective-permute-start | bytes 491528 | tf_op jit(solution)/shard_map/ppermute | solution.py:40
  115.1 10.0 %collective-permute-start.14 = (bf16[2,160,256]{2,1,0:T(8,128)(2,1)S(1)}, bf16[2,160,256]{2,1,0:T(8,128)(2,1)S(1)}, u32[]{:S(2)}, u32[]{:S(2)}) collective-permute-start(bf16[2,160,256]{2,1,0:T(8,128)(2,1)S(1)} %pad_maximum_fusion.2), channel_id=1, source_target_pairs={{0,4},{1,5},{2,6},{3,7},{4,0},{5,1},{6,2},{7,3},{8,12},{9,13},{10,... | collective-permute-start | bytes 491528 | tf_op jit(solution)/shard_map/ppermute | solution.py:40
  119.4 5.7 %collective-permute-start.15 = (bf16[2,160,256]{2,1,0:T(8,128)(2,1)S(1)}, bf16[2,160,256]{2,1,0:T(8,128)(2,1)S(1)}, u32[]{:S(2)}, u32[]{:S(2)}) collective-permute-start(bf16[2,160,256]{2,1,0:T(8,128)(2,1)S(1)} %pad_maximum_fusion.2), channel_id=1, source_target_pairs={{0,6},{1,7},{2,0},{3,1},{4,2},{5,3},{6,4},{7,5},{8,14},{9,15},{10,... | collective-permute-start | bytes 491528 | tf_op jit(solution)/shard_map/ppermute | solution.py:40
  119.6 12.8 %collective-permute-start.10 = (f32[4,160,256]{2,1,0:T(8,128)S(1)}, f32[4,160,256]{2,1,0:T(8,128)S(1)}, u32[]{:S(2)}, u32[]{:S(2)}) collective-permute-start(f32[4,160,256]{2,1,0:T(8,128)S(1)} %pad_maximum_fusion), channel_id=1, source_target_pairs={{0,8},{1,9},{2,10},{3,11},{4,12},{5,13},{6,14},{7,15},{8,0},{9,1},... | collective-permute-start | bytes 1966088 | tf_op jit(solution)/shard_map/ppermute | solution.py:40
  125.2 15.6 %collective-permute-start.16 = (bf16[8,160,256]{2,1,0:T(8,128)(2,1)S(1)}, bf16[8,160,256]{2,1,0:T(8,128)(2,1)S(1)}, u32[]{:S(2)}, u32[]{:S(2)}) collective-permute-start(bf16[8,160,256]{2,1,0:T(8,128)(2,1)S(1)} %constant_dynamic-update-slice_fusion.5.w0), channel_id=1, source_target_pairs={{0,16},{1,17},{2,18},{3,19},{4,20},{5,21},{6,22},{7,23},{8,24},{9,... | collective-permute-start | bytes 1966088 | tf_op jit(solution)/shard_map/ppermute | solution.py:40
  125.3 25.4 %collective-permute-start.17 = (bf16[8,160,256]{2,1,0:T(8,128)(2,1)S(1)}, bf16[8,160,256]{2,1,0:T(8,128)(2,1)S(1)}, u32[]{:S(2)}, u32[]{:S(2)}) collective-permute-start(bf16[8,160,256]{2,1,0:T(8,128)(2,1)S(1)} %constant_dynamic-update-slice_fusion.5.w0), channel_id=1, source_target_pairs={{0,32},{1,33},{2,34},{3,35},{4,36},{5,37},{6,38},{7,39},{8,40},{9,... | collective-permute-start | bytes 1966088 | tf_op jit(solution)/shard_map/ppermute | solution.py:40
  125.8 33.5 %collective-permute-start.18 = (bf16[8,160,256]{2,1,0:T(8,128)(2,1)S(1)}, bf16[8,160,256]{2,1,0:T(8,128)(2,1)}, u32[]{:S(2)}, u32[]{:S(2)}) collective-permute-start(bf16[8,160,256]{2,1,0:T(8,128)(2,1)S(1)} %constant_dynamic-update-slice_fusion.5.w0), channel_id=1, source_target_pairs={{0,48},{1,49},{2,50},{3,51},{4,52},{5,53},{6,54},{7,55},{8,56},{9,... | collective-permute-start | bytes 1966088 | tf_op jit(solution)/shard_map/ppermute | solution.py:40
  132.4 49.0 %collective-permute-start.25 = (bf16[384,512]{1,0:T(8,128)(2,1)}, bf16[384,512]{1,0:T(8,128)(2,1)S(1)}, u32[]{:S(2)}, u32[]{:S(2)}) collective-permute-start(bf16[384,512]{1,0:T(8,128)(2,1)} %get-tuple-element.40), channel_id=1, source_target_pairs={{0,2},{1,3},{2,4},{3,5},{4,6},{5,7},{6,0},{7,1},{8,10},{9,11},{10,... | collective-permute-start | bytes 1179656 | tf_op jit(solution)/shard_map/ppermute | solution.py:40
  140.7 40.7 %collective-permute-start.26 = (bf16[384,512]{1,0:T(8,128)(2,1)S(1)}, bf16[384,512]{1,0:T(8,128)(2,1)}, u32[]{:S(2)}, u32[]{:S(2)}) collective-permute-start(bf16[384,512]{1,0:T(8,128)(2,1)S(1)} %get-tuple-element.42), channel_id=1, source_target_pairs={{0,4},{1,5},{2,6},{3,7},{4,0},{5,1},{6,2},{7,3},{8,12},{9,13},{10,... | collective-permute-start | bytes 1179656 | tf_op jit(solution)/shard_map/ppermute | solution.py:40
  150.6 30.8 %collective-permute-start.27 = (bf16[384,512]{1,0:T(8,128)(2,1)S(1)}, bf16[384,512]{1,0:T(8,128)(2,1)}, u32[]{:S(2)}, u32[]{:S(2)}) collective-permute-start(bf16[384,512]{1,0:T(8,128)(2,1)S(1)} %get-tuple-element.41), channel_id=1, source_target_pairs={{0,6},{1,7},{2,0},{3,1},{4,2},{5,3},{6,4},{7,5},{8,14},{9,15},{10,... | collective-permute-start | bytes 1179656 | tf_op jit(solution)/shard_map/ppermute | solution.py:40
  152.2 7.2 %copy-start.3 = (s32[25]{0:T(128)S(1)}, s32[25]{0:T(128)}, u32[]{:S(2)}) copy-start(s32[25]{0:T(128)} %copy-done.2) | copy-start | bytes 304
  159.4 2.5 %copy-start.1 = (bf16[512,5120]{1,0:T(8,128)(2,1)S(1)}, bf16[512,5120]{1,0:T(8,128)(2,1)}, u32[]{:S(2)}) copy-start(bf16[512,5120]{1,0:T(8,128)(2,1)} %tokens.3) | copy-start | bytes 15728644
  170.7 12.4 %copy-start.5 = (bf16[1,256,512]{2,1,0:T(8,128)(2,1)S(1)}, bf16[1,256,512]{2,1,0:T(8,128)(2,1)}, u32[]{:S(2)}) copy-start(bf16[1,256,512]{2,1,0:T(8,128)(2,1)} %fusion.7) | copy-start | bytes 786436
  170.7 13.3 %collective-permute-start.19 = (bf16[512,256]{1,0:T(8,128)(2,1)S(1)}, bf16[512,256]{1,0:T(8,128)(2,1)S(1)}, u32[]{:S(2)}, u32[]{:S(2)}) collective-permute-start(bf16[512,256]{1,0:T(8,128)(2,1)S(1)} %get-tuple-element.29), channel_id=1, source_target_pairs={{0,8},{1,9},{2,10},{3,11},{4,12},{5,13},{6,14},{7,15},{8,0},{9,1},... | collective-permute-start | bytes 786440 | tf_op jit(solution)/shard_map/ppermute | solution.py:40

commit v2 on v1

v2 whole, which is shorter than its diff:
```python
import jax
import jax.numpy as jnp
from jax import lax
from jax.experimental import pallas as pl
from jax.experimental.pallas import tpu as pltpu
from jax.sharding import PartitionSpec as P

momentum_rate = 0.9
outer_rate = 0.7

F32, BF16 = jnp.float32, jnp.bfloat16
AXES = ("rep", "fsdp")
SIZES = (4, 4, 2, 4, 2)
REPLICAS = 32
D, KW, SHARD = 5120, 512, 640
TOK = 512
ROWS, COLS = 160, 256
HALF = SHARD // 2


def shift(value, zh=0, x=0, core=0, y=0, zl=0):
    steps = (zh, x, core, y, zl)

    def index(place):
        n = 0
        for p, size in zip(place, SIZES):
            n = n * size + p
        return n

    pairs = []
    for a in range(4):
        for b in range(4):
            for c in range(2):
                for d in range(4):
                    for e in range(2):
                        place = (a, b, c, d, e)
                        to = tuple((p + s) % n for p, s, n in zip(place, steps, SIZES))
                        pairs.append((index(place), index(to)))
    return lax.ppermute(value, AXES, pairs)


def after(value, *others):
    return lax.optimization_barrier((value, *others))[0]


def share(tokens, key_grad):
    return lax.dot_general(
        tokens[...], key_grad[...], (((0,), (0,)), ((), ())), preferred_element_type=F32
    ).astype(BF16)


def far_kernel(order, tokens, key_grad, low, high):
    part = share(tokens, key_grad)
    for z in range(2):
        low[z] = part[z * SHARD : z * SHARD + HALF]
        high[z] = part[z * SHARD + HALF : (z + 1) * SHARD]


def far_part(order, tokens, key_grad):
    return pl.pallas_call(
        far_kernel,
        grid_spec=pltpu.PrefetchScalarGridSpec(
            num_scalar_prefetch=1,
            grid=(1,),
            in_specs=[
                pl.BlockSpec((TOK, 2 * SHARD), lambda s, o: (0, o[2])),
                pl.BlockSpec((TOK, KW), lambda s, o: (0, 0)),
            ],
            out_specs=[pl.BlockSpec((2, HALF, KW), lambda s, o: (0, 0, 0))] * 2,
        ),
        out_shape=[jax.ShapeDtypeStruct((2, HALF, KW), BF16)] * 2,
        compiler_params=pltpu.CompilerParams(vmem_limit_bytes=32 << 20),
        cost_estimate=pl.CostEstimate(flops=TOK * D * KW // 2, bytes_accessed=3 << 20, transcendentals=0),
    )(order, tokens, key_grad)


def near_kernel(order, tokens, key_grad, up, down, here):
    step = pl.program_id(0)
    part = share(tokens, key_grad).reshape(2, SHARD, KW)
    for k, ref in enumerate((up, down, here)):

        @pl.when(step == k)
        def _(ref=ref):
            ref[...] = part


def near_parts(order, tokens, key_grad):
    out = pl.BlockSpec((2, SHARD, KW), lambda s, o: (0, 0, 0))
    return pl.pallas_call(
        near_kernel,
        grid_spec=pltpu.PrefetchScalarGridSpec(
            num_scalar_prefetch=1,
            grid=(3,),
            in_specs=[
                pl.BlockSpec((TOK, 2 * SHARD), lambda s, o: (0, o[8 + s])),
                pl.BlockSpec((TOK, KW), lambda s, o: (0, 0)),
            ],
            out_specs=[out] * 3,
        ),
        out_shape=[jax.ShapeDtypeStruct((2, SHARD, KW), BF16)] * 3,
        compiler_params=pltpu.CompilerParams(vmem_limit_bytes=48 << 20),
        cost_estimate=pl.CostEstimate(flops=3 * TOK * D * KW // 2, bytes_accessed=8 << 20, transcendentals=0),
    )(order, tokens, key_grad)


def pair_kernel(order, g, l0, l1, own, p1, p2, p3):
    for k, ref in enumerate((own, p1, p2, p3)):
        rows = pl.ds(pl.multiple_of(order[16 + k] * ROWS, ROWS), ROWS)
        total = 2.0 * g[rows, :] - l0[rows, :].astype(F32) - l1[rows, :].astype(F32)
        ref[...] = total.astype(ref.dtype)


def pair_sums(order, g, l0, l1):
    block = pl.BlockSpec((SHARD, COLS), lambda s, o: (0, o[24]))
    out = pl.BlockSpec((ROWS, COLS), lambda s, o: (0, 0))
    return pl.pallas_call(
        pair_kernel,
        grid_spec=pltpu.PrefetchScalarGridSpec(
            num_scalar_prefetch=1, grid=(1,), in_specs=[block] * 3, out_specs=[out] * 4
        ),
        out_shape=[jax.ShapeDtypeStruct((ROWS, COLS), F32)]
        + [jax.ShapeDtypeStruct((ROWS, COLS), BF16)] * 3,
    )(order, g, l0, l1)


def step_kernel(order, own, r1, r2, r3, g, m, average, start):
    avg = (own[...] + r1[...].astype(F32) + r2[...].astype(F32) + r3[...].astype(F32)) / REPLICAS
    new_m = momentum_rate * m[...] + avg
    new_g = g[...] - outer_rate * (avg + momentum_rate * new_m)
    average[...] = avg
    start[...] = new_g.astype(BF16)


def outer_step(order, own, r1, r2, r3, g, m):
    here = pl.BlockSpec((ROWS, COLS), lambda s, o: (0, 0))
    block = pl.BlockSpec((ROWS, COLS), lambda s, o: (o[16], o[24]))
    return pl.pallas_call(
        step_kernel,
        grid_spec=pltpu.PrefetchScalarGridSpec(
            num_scalar_prefetch=1, grid=(1,), in_specs=[here] * 4 + [block] * 2, out_specs=[here] * 2
        ),
        out_shape=[
            jax.ShapeDtypeStruct((ROWS, COLS), F32),
            jax.ShapeDtypeStruct((ROWS, COLS), BF16),
        ],
    )(order, own, r1, r2, r3, g, m)


def join_kernel(*refs):
    *parts, out = refs
    at = 0
    for ref in parts:
        n = ref.shape[0]
        out[at : at + n] = ref[...]
        at += n


def join(*parts):
    n = sum(p.shape[0] for p in parts)
    return pl.pallas_call(
        join_kernel,
        out_shape=jax.ShapeDtypeStruct((n, *parts[0].shape[1:]), parts[0].dtype),
    )(*parts)


def update_kernel(average, g, m, new_global, new_momentum):
    for h in range(2):
        cols = slice(h * COLS, (h + 1) * COLS)
        new_m = momentum_rate * m[:, cols] + average[h]
        new_momentum[:, cols] = new_m
        new_global[:, cols] = g[:, cols] - outer_rate * (average[h] + momentum_rate * new_m)


def update(average, g, m):
    block = pl.BlockSpec((ROWS, KW), lambda s: (s, 0))
    return pl.pallas_call(
        update_kernel,
        grid=(4,),
        in_specs=[pl.BlockSpec((2, ROWS, COLS), lambda s: (s, 0, 0)), block, block],
        out_specs=[block] * 2,
        out_shape=[jax.ShapeDtypeStruct((SHARD, KW), F32)] * 2,
    )(average, g, m)


def keys_kernel(order, tokens, w0, w1, w2, w3, keys, weights):
    @pl.when(pl.program_id(0) == 0)
    def _():
        for d in range(4):
            for z in range(2):
                for k, ref in enumerate((w0, w1, w2, w3)):
                    at = order[4 + d] * (2 * SHARD) + order[12 + z] * SHARD + order[20 + k] * ROWS
                    weights[pl.ds(pl.multiple_of(at, ROWS), ROWS), :] = ref[2 * d + z]

    keys[0] = jnp.dot(tokens[0], weights[...], preferred_element_type=F32).astype(BF16)


def keys_of(order, tokens, blocks):
    part = 4
    rows = pl.BlockSpec((1, TOK // part, D), lambda s, o: (s // part, s % part, 0))
    whole = pl.BlockSpec((8, ROWS, COLS), lambda s, o: (0, 0, 0))
    return pl.pallas_call(
        keys_kernel,
        grid_spec=pltpu.PrefetchScalarGridSpec(
            num_scalar_prefetch=1,
            grid=(2 * part,),
            in_specs=[rows] + [whole] * 4,
            out_specs=pl.BlockSpec((1, TOK // part, COLS), lambda s, o: (s // part, s % part, 0)),
            scratch_shapes=[pltpu.VMEM((D, COLS), BF16)],
        ),
        out_shape=jax.ShapeDtypeStruct((2, TOK, COLS), BF16),
        compiler_params=pltpu.CompilerParams(vmem_limit_bytes=32 << 20),
        cost_estimate=pl.CostEstimate(flops=2 * TOK * D * KW, bytes_accessed=14 << 20, transcendentals=0),
    )(order, tokens, *blocks)


def per_device(local_weights, global_weights, momentum, tokens, key_grad):
    g, m, local = global_weights, momentum, local_weights[0]
    rep, fsdp = lax.axis_index("rep"), lax.axis_index("fsdp")
    core, x, y, zl = rep % 2, rep // 2 % 4, fsdp // 2, fsdp % 2
    four = jnp.arange(4)
    order = jnp.concatenate(
        [
            (y + four) % 4,
            (y - four) % 4,
            (y + jnp.array([1, 3, 0, 0])) % 4,
            (zl + four) % 2,
            (x + four) % 4,
            (x - four) % 4,
            core[None],
        ]
    ).astype(jnp.int32)

    local_other = shift(local, core=1)
    pairs = lax.all_gather(tokens, "rep", axis_index_groups=[[2 * k, 2 * k + 1] for k in range(16)])

    low, high = far_part(order, tokens, key_grad)
    low, high = shift(low, y=1), shift(high, y=-1)

    own, p1, p2, p3 = pair_sums(order, g, local, local_other)
    r1, r2, r3 = (shift(p, x=k + 1) for k, p in enumerate((p1, p2, p3)))

    up, down, here = near_parts(order, after(tokens, p1), key_grad)

    chips = own + r1.astype(F32) + r2.astype(F32) + r3.astype(F32)
    sent = chips.astype(BF16)
    q1, q2, q3 = (shift(sent, zh=k) for k in (1, 2, 3))

    low, high = after(low, sent), after(high, sent)
    up = jnp.concatenate([up[:, :HALF] + low, up[:, HALF:]], axis=1)
    down = jnp.concatenate([down[:, :HALF], down[:, HALF:] + high], axis=1)
    up, down = shift(up, y=1), shift(down, y=-1)

    average, start = outer_step(order, chips, q1, q2, q3, g, m)

    pair = join(start[None], shift(start, zl=1)[None])
    shards = join(pair, *(shift(pair, y=k) for k in (1, 2, 3)))
    blocks = [shards] + [shift(shards, x=k) for k in (1, 2, 3)]

    whole = lax.all_gather(
        average, "rep", axis_index_groups=[[8 * k + j for j in range(8)] for k in range(4)]
    )
    new_global, new_momentum = update(whole, g, m)

    rows = here.astype(F32) + up.astype(F32) + down.astype(F32)
    got = shift(lax.dynamic_index_in_dim(rows, 1 - zl, 0, False).astype(BF16), zl=1)
    weight_grad = (lax.dynamic_index_in_dim(rows, zl, 0, False) + got.astype(F32)).astype(BF16)[None]

    keys = keys_of(order, pairs, blocks)
    keys_got = shift(lax.dynamic_index_in_dim(keys, 1 - core, 0, False), core=1)
    keys = lax.dynamic_index_in_dim(keys, core, 0, False)
    inner_keys = jnp.where(
        core == 0,
        jnp.concatenate([keys, keys_got], axis=1),
        jnp.concatenate([keys_got, keys], axis=1),
    )
    return (new_global, new_momentum, inner_keys, weight_grad)


def solution(mesh):
    placed = (
        P("rep", "fsdp", None),
        P("fsdp", None),
        P("fsdp", None),
        P(("rep", "fsdp"), None),
        P(("rep", "fsdp"), None),
    )
    return jax.shard_map(
        per_device,
        mesh=mesh,
        in_specs=placed,
        out_specs=(
            P("fsdp", None),
            P("fsdp", None),
            P(("rep", "fsdp"), None),
            P("rep", "fsdp", None),
        ),
        check_vma=False,
    )
```

time: 186 us -> 135 us (0.73)
  waiting for transfers between devices: 77.3 us -> 36.8 us
  starting transfers between devices: 53.2 us -> 32.7 us
  between operations: 0.8 us -> 14.2 us
  Pallas kernels: 29.5 us -> 25.4 us
  other arithmetic: 10.8 us -> 12.9 us
    ppermute x28 -> x20, waiting for transfers between devices: 77.3 us -> 36.1 us  [shift(): return lax.ppermute(value, AXES, pairs)]
    ppermute x28 -> x20, starting transfers between devices: 53.2 us -> 32.6 us  [shift(): return lax.ppermute(value, AXES, pairs)]
    pallas_call x1, Pallas kernels: 8.82 us -> 4.97 us  [keys_of(): pl.pallas_call(keys_kernel, grid_spec=pltpu.PrefetchScalarGridSpec(num_sc...]
    broadcast_in_dim x0 -> x1, other arithmetic: none -> 2.57 us  [per_device(): (lax.dynamic_index_in_dim(rows, zl, 0, False) + got.astype(F32)).astype(B...]
    add x3 -> x2, other arithmetic: 4.02 us -> 5.06 us  [the longest x1 3.83 us: per_device(): rows = here.astype(F32) + up.astype(F32) + down.astype(F32)]
    unnamed x30 -> x36, local copies, waits for them, and re-layouts: 11.3 us -> 10.2 us
    pallas_call x2 -> x5, Pallas kernels: 14.3 us -> 15.1 us  [the longest x1 5.79 us: near_parts(): pl.pallas_call(near_kernel, grid_spec=pltpu.PrefetchScalarGridSpec(num_sc...]
  transfers between devices with their start and end apart: 28 -> 22, of which waited for: 11 -> 8; matrix products, arithmetic and copies ran while one was open for 9% -> 11% of each run, Pallas kernels for 16% -> 19%
where the time goes in v2:
time: 135 us
  waiting for transfers between devices  36.8 us (27%)
  starting transfers between devices  32.7 us (24%)
  Pallas kernels  25.4 us (19%)
  between operations  14.2 us (11%)
  other arithmetic  12.9 us (10%)
  local copies, waits for them, and re-layouts  12.7 us (9%)
    ppermute x20, waiting for transfers between devices, shift(): return lax.ppermute(value, AXES, pairs)  36.1 us
    ppermute x20, starting transfers between devices, shift(): return lax.ppermute(value, AXES, pairs)  32.6 us
    unnamed x36, local copies, waits for them, and re-layouts  10.2 us
    pallas_call x1, Pallas kernels, near_parts(): pl.pallas_call(near_kernel, grid_spec=pltpu.PrefetchScalarGridSpec(num_sc...  5.79 us
    pallas_call x1, Pallas kernels, keys_of(): pl.pallas_call(keys_kernel, grid_spec=pltpu.PrefetchScalarGridSpec(num_sc...  4.97 us
    pallas_call x1, Pallas kernels, update(): pl.pallas_call(update_kernel, grid=(4,), in_specs=[pl.BlockSpec((2, ROWS,...  4.24 us
    add x1, other arithmetic, per_device(): rows = here.astype(F32) + up.astype(F32) + down.astype(F32)  3.83 us
    pallas_call x2, Pallas kernels, join(): pl.pallas_call(join_kernel, out_shape=jax.ShapeDtypeStruct((n, *parts[0]....  3.65 us
  transfers between devices with their start and end apart: 22, of which 8 were waited for; matrix products, arithmetic and copies ran while one was open for 11% of the time, Pallas kernels for 19%

profile of v2, /device:TPU:1, one launch (start us, length us, event | category | flops | bytes accessed | tf_op | source)
XLA Modules:
  0.0 134.7 jit_solution(17960148590372297317)
XLA Ops:
  7.2 0.0 copy-start.17
  7.2 0.0 copy-start.7
  7.2 0.0 all-gather.7.cloned.1.call-start
  7.2 0.7 all-gather.7.cloned.1.call-update
  7.9 0.0 all-gather.5.cloned.1.call-start
  8.0 0.3 copy-done.7
  8.3 3.2 %collective-permute-start = (bf16[640,512]{1,0:T(8,128)(2,1)S(1)}, bf16[640,512]{1,0:T(8,128)(2,1)S(1)}, u32[]{:S(2)}, u32[]{:S(2)}) collective-permute-start(bf16[640,512]{1,0:T(8,128)(2,1)S(1)} %bitcast.23), channel_id=1, source_target_pairs={{0,8},{1,9},{2,10},{3,11},{4,12},{5,13},{6,14},{7,15},{8,0},{9,1},... | collective-permute-start | bytes 1966088 | tf_op jit(solution)/shard_map/ppermute | solution.py:39
  11.6 0.1 concatenate.15.order
  11.7 2.5 %copy-done = bf16[512,5120]{1,0:T(8,128)(2,1)S(1)} copy-done((bf16[512,5120]{1,0:T(8,128)(2,1)S(1)}, bf16[512,5120]{1,0:T(8,128)(2,1)}, u32[]{:S(2)}) %copy-start) | copy-done | bytes 5242904
  14.2 1.4 %shard_map.100 = (bf16[2,320,512]{2,1,0:T(8,128)(2,1)S(1)}, bf16[2,320,512]{2,1,0:T(8,128)(2,1)S(1)}) custom-call(s32[25]{0:T(128)S(1)} %concatenate.15.order, bf16[512,5120]{1,0:T(8,128)(2,1)S(1)} %copy-done, bf16[512,512]{1,0:T(8,128)(2,1)S(1)} %copy-done.3), custom_call_target="tpu_custom_call" | custom-call | flops 671088640 | bytes 3145728 | tf_op jit(solution)/shard_map/pallas_call | solution.py:60
  15.6 0.1 collective-permute-start.15
  15.7 2.7 %collective-permute-start.17 = (bf16[2,320,512]{2,1,0:T(8,128)(2,1)S(1)}, bf16[2,320,512]{2,1,0:T(8,128)(2,1)}, u32[]{:S(2)}, u32[]{:S(2)}) collective-permute-start(bf16[2,320,512]{2,1,0:T(8,128)(2,1)S(1)} %get-tuple-element.34), channel_id=1, source_target_pairs={{0,6},{1,7},{2,0},{3,1},{4,2},{5,3},{6,4},{7,5},{8,14},{9,15},{10,... | collective-permute-start | bytes 1966088 | tf_op jit(solution)/shard_map/ppermute | solution.py:39
  18.4 0.8 copy-done.8
  19.2 2.7 %shard_map.93 = (f32[160,256]{1,0:T(8,128)}, bf16[160,256]{1,0:T(8,128)(2,1)}, bf16[160,256]{1,0:T(8,128)(2,1)}, bf16[160,256]{1,0:T(8,128)(2,1)}) custom-call(s32[25]{0:T(128)} %copy-done.4, f32[640,512]{1,0:T(8,128)} %g.5, bf16[640,512]{1,0:T(8,128)(2,1)} %bitcast.22, bf16[640,512]{1,0:T(8,128)(2,1)} %copy-done.8), custom_call_target="tpu_custom_call" | custom-call | tf_op jit(solution)/shard_map/pallas_call | solution.py:116
  21.9 0.0 collective-permute-start.1
  21.9 2.1 %collective-permute-start.2 = (bf16[160,256]{1,0:T(8,128)(2,1)}, bf16[160,256]{1,0:T(8,128)(2,1)S(1)}, u32[]{:S(2)}, u32[]{:S(2)}) collective-permute-start(bf16[160,256]{1,0:T(8,128)(2,1)} %get-tuple-element.22), channel_id=1, source_target_pairs={{0,32},{1,33},{2,34},{3,35},{4,36},{5,37},{6,38},{7,39},{8,40},{9,... | collective-permute-start | bytes 245768 | tf_op jit(solution)/shard_map/ppermute | solution.py:39
  24.0 1.2 collective-permute-start.3
  25.2 5.8 %shard_map.99 = (bf16[2,640,512]{2,1,0:T(8,128)(2,1)S(1)}, bf16[2,640,512]{2,1,0:T(8,128)(2,1)S(1)}, bf16[2,640,512]{2,1,0:T(8,128)(2,1)S(1)}) custom-call(s32[25]{0:T(128)S(1)} %copy-done.5, bf16[512,5120]{1,0:T(8,128)(2,1)} %tokens.2, bf16[512,512]{1,0:T(8,128)(2,1)S(1)} %copy-done.3), custom_call_target="tpu_custom_call" | custom-call | flops 2013265920 | bytes 8388608 | tf_op jit(solution)/shard_map/pallas_call | solution.py:89
  31.0 0.0 collective-permute-done.1
  31.0 0.0 collective-permute-done.2
  31.0 0.7 fusion.9
  31.7 1.6 %collective-permute-done.15 = bf16[2,320,512]{2,1,0:T(8,128)(2,1)} collective-permute-done((bf16[2,320,512]{2,1,0:T(8,128)(2,1)S(1)}, bf16[2,320,512]{2,1,0:T(8,128)(2,1)}, u32[]{:S(2)}, u32[]{:S(2)}) %collective-permute-start.15) | collective-permute-done | bytes 655392 | tf_op jit(solution)/shard_map/ppermute | solution.py:39
  33.4 1.2 slice_add_fusion.1
  34.6 1.1 pad_maximum_fusion
  35.7 0.0 collective-permute-start.16
  35.8 1.4 %fusion.10 = (bf16[2,320,512]{2,1,0:T(8,128)(2,1)S(1)}, bf16[2,320,512]{2,1,0:T(8,128)(2,1)S(1)}) fusion(bf16[2,640,512]{2,1,0:T(8,128)(2,1)S(1)} %get-tuple-element.33, bf16[2,320,512]{2,1,0:T(8,128)(2,1)} %collective-permute-done.17), kind=kLoop, calls=%fused_computation.39 | loop fusion | flops 327680 | bytes 3276800 | tf_op jit(solution)/shard_map/slice | solution.py:250
  37.1 1.1 pad_maximum_fusion.1
  38.3 2.5 %collective-permute-start.18 = (bf16[2,640,512]{2,1,0:T(8,128)(2,1)}, bf16[2,640,512]{2,1,0:T(8,128)(2,1)}, u32[]{:S(2)}, u32[]{:S(2)}) collective-permute-start(bf16[2,640,512]{2,1,0:T(8,128)(2,1)} %pad_maximum_fusion.1), channel_id=1, source_target_pairs={{0,6},{1,7},{2,0},{3,1},{4,2},{5,3},{6,4},{7,5},{8,14},{9,15},{10,... | collective-permute-start | bytes 3932168 | tf_op jit(solution)/shard_map/ppermute | solution.py:39
  40.8 1.7 %collective-permute-start.4 = (bf16[160,256]{1,0:T(8,128)(2,1)S(1)}, bf16[160,256]{1,0:T(8,128)(2,1)S(1)}, u32[]{:S(2)}, u32[]{:S(2)}) collective-permute-start(bf16[160,256]{1,0:T(8,128)(2,1)S(1)} %get-tuple-element.36), channel_id=1, source_target_pairs={{0,64},{1,65},{2,66},{3,67},{4,68},{5,69},{6,70},{7,71},{8,72},{9,... | collective-permute-start | bytes 245768 | tf_op jit(solution)/shard_map/ppermute | solution.py:39
  42.4 5.0 %collective-permute-start.5 = (bf16[160,256]{1,0:T(8,128)(2,1)S(1)}, bf16[160,256]{1,0:T(8,128)(2,1)S(1)}, u32[]{:S(2)}, u32[]{:S(2)}) collective-permute-start(bf16[160,256]{1,0:T(8,128)(2,1)S(1)} %get-tuple-element.36), channel_id=1, source_target_pairs={{0,128},{1,129},{2,130},{3,131},{4,132},{5,133},{6,134},{7,135},{8... | collective-permute-start | bytes 245768 | tf_op jit(solution)/shard_map/ppermute | solution.py:39
  47.4 2.2 %collective-permute-start.6 = (bf16[160,256]{1,0:T(8,128)(2,1)S(1)}, bf16[160,256]{1,0:T(8,128)(2,1)S(1)}, u32[]{:S(2)}, u32[]{:S(2)}) collective-permute-start(bf16[160,256]{1,0:T(8,128)(2,1)S(1)} %get-tuple-element.36), channel_id=1, source_target_pairs={{0,192},{1,193},{2,194},{3,195},{4,196},{5,197},{6,198},{7,199},{8... | collective-permute-start | bytes 245768 | tf_op jit(solution)/shard_map/ppermute | solution.py:39
  49.7 0.0 collective-permute-done.4.r1
  49.7 1.1 collective-permute-done.5.r2
  50.8 2.4 %collective-permute-done.6.r3 = bf16[160,256]{1,0:T(8,128)(2,1)S(1)} collective-permute-done((bf16[160,256]{1,0:T(8,128)(2,1)S(1)}, bf16[160,256]{1,0:T(8,128)(2,1)S(1)}, u32[]{:S(2)}, u32[]{:S(2)}) %collective-permute-start.6) | collective-permute-done | bytes 81952 | tf_op jit(solution)/shard_map/ppermute | solution.py:39
  53.2 0.6 copy-done.15
  53.8 2.6 %shard_map.94 = (f32[160,256]{1,0:T(8,128)}, bf16[160,256]{1,0:T(8,128)(2,1)}) custom-call(s32[25]{0:T(128)} %copy-done.4, f32[160,256]{1,0:T(8,128)} %get-tuple-element.37.own, bf16[160,256]{1,0:T(8,128)(2,1)} %copy-done.13, bf16[160,256]{1,0:T(8,128)(2,1)} %copy-done.14, bf16[160,256]{1,0:T(8,128)(2,1)} %copy-done.15, f32[640,512]{1,0:T(8,128)} %g.5, ...), custom_call_target="tpu_custom_call" | custom-call | tf_op jit(solution)/shard_map/pallas_call | solution.py:137
  56.4 0.0 all-gather.5.cloned.1.call-update
  56.5 1.3 collective-permute-start.7
  57.8 2.6 %collective-permute-done.7 = bf16[160,256]{1,0:T(8,128)(2,1)S(1)} collective-permute-done((bf16[160,256]{1,0:T(8,128)(2,1)}, bf16[160,256]{1,0:T(8,128)(2,1)S(1)}, u32[]{:S(2)}, u32[]{:S(2)}) %collective-permute-start.7) | collective-permute-done | bytes 81952 | tf_op jit(solution)/shard_map/ppermute | solution.py:39
  60.4 0.6 copy-done.16
  61.1 1.6 %shard_map.96.refs_0_ = bf16[2,160,256]{2,1,0:T(8,128)(2,1)} custom-call(bf16[1,160,256]{2,1,0:T(8,128)(2,1)} %bitcast.24, bf16[1,160,256]{2,1,0:T(8,128)(2,1)} %bitcast.25), custom_call_target="tpu_custom_call" | custom-call | tf_op jit(solution)/shard_map/pallas_call | solution.py:160
  62.7 0.5 collective-permute-start.10
  63.2 0.9 collective-permute-start.8
  64.2 0.5 collective-permute-start.9
  64.6 7.7 %collective-permute-done.10.refs_3_ = bf16[2,160,256]{2,1,0:T(8,128)(2,1)S(1)} collective-permute-done((bf16[2,160,256]{2,1,0:T(8,128)(2,1)}, bf16[2,160,256]{2,1,0:T(8,128)(2,1)S(1)}, u32[]{:S(2)}, u32[]{:S(2)}) %collective-permute-start.10) | collective-permute-done | bytes 163872 | tf_op jit(solution)/shard_map/ppermute | solution.py:39
  72.3 0.0 collective-permute-done.8.refs_1_
  72.3 0.6 copy-done.10
  73.0 0.1 copy-done.11
  73.0 0.7 copy-done.12
  73.7 2.0 %shard_map.97.w0 = bf16[8,160,256]{2,1,0:T(8,128)(2,1)} custom-call(bf16[2,160,256]{2,1,0:T(8,128)(2,1)} %shard_map.96.refs_0_, bf16[2,160,256]{2,1,0:T(8,128)(2,1)} %copy-done.11, bf16[2,160,256]{2,1,0:T(8,128)(2,1)} %copy-done.12, bf16[2,160,256]{2,1,0:T(8,128)(2,1)} %copy-done.10), custom_call_target="tpu_custom_call" | custom-call | tf_op jit(solution)/shard_map/pallas_call | solution.py:160
  75.7 2.9 %collective-permute-start.11 = (bf16[8,160,256]{2,1,0:T(8,128)(2,1)}, bf16[8,160,256]{2,1,0:T(8,128)(2,1)S(1)}, u32[]{:S(2)}, u32[]{:S(2)}) collective-permute-start(bf16[8,160,256]{2,1,0:T(8,128)(2,1)} %shard_map.97.w0), channel_id=1, source_target_pairs={{0,16},{1,17},{2,18},{3,19},{4,20},{5,21},{6,22},{7,23},{8,24},{9,... | collective-permute-start | bytes 1966088 | tf_op jit(solution)/shard_map/ppermute | solution.py:39
  78.7 2.4 %collective-permute-start.12 = (bf16[8,160,256]{2,1,0:T(8,128)(2,1)}, bf16[8,160,256]{2,1,0:T(8,128)(2,1)S(1)}, u32[]{:S(2)}, u32[]{:S(2)}) collective-permute-start(bf16[8,160,256]{2,1,0:T(8,128)(2,1)} %shard_map.97.w0), channel_id=1, source_target_pairs={{0,32},{1,33},{2,34},{3,35},{4,36},{5,37},{6,38},{7,39},{8,40},{9,... | collective-permute-start | bytes 1966088 | tf_op jit(solution)/shard_map/ppermute | solution.py:39
  81.1 1.2 collective-permute-start.13
  82.3 3.8 %convert_add_fusion = f32[2,640,512]{2,1,0:T(8,128)} fusion(bf16[2,640,512]{2,1,0:T(8,128)(2,1)} %collective-permute-done.18, bf16[2,640,512]{2,1,0:T(8,128)(2,1)} %collective-permute-done.16, bf16[2,640,512]{2,1,0:T(8,128)(2,1)S(1)} %get-tuple-element.29), kind=kLoop, calls=%fused_computation | loop fusion | flops 3276800 | bytes 6553600 | tf_op jit(solution)/shard_map/add | solution.py:264
  86.1 2.3 %fusion.1 = bf16[640,512]{1,0:T(8,128)(2,1)} fusion(f32[2,640,512]{2,1,0:T(8,128)} %convert_add_fusion, s32[]{:T(128)S(6)} %select_n.86), kind=kLoop, calls=%fused_computation.6 | loop fusion | bytes 1310724 | tf_op jit(solution)/shard_map/convert_element_type | solution.py:265
  88.4 3.9 %collective-permute-done.11.w1 = bf16[8,160,256]{2,1,0:T(8,128)(2,1)S(1)} collective-permute-done((bf16[8,160,256]{2,1,0:T(8,128)(2,1)}, bf16[8,160,256]{2,1,0:T(8,128)(2,1)S(1)}, u32[]{:S(2)}, u32[]{:S(2)}) %collective-permute-start.11) | collective-permute-done | bytes 655392 | tf_op jit(solution)/shard_map/ppermute | solution.py:39
  92.4 14.4 %collective-permute-done.12.w2 = bf16[8,160,256]{2,1,0:T(8,128)(2,1)S(1)} collective-permute-done((bf16[8,160,256]{2,1,0:T(8,128)(2,1)}, bf16[8,160,256]{2,1,0:T(8,128)(2,1)S(1)}, u32[]{:S(2)}, u32[]{:S(2)}) %collective-permute-start.12) | collective-permute-done | bytes 655392 | tf_op jit(solution)/shard_map/ppermute | solution.py:39
  106.8 2.2 %collective-permute-done.13.w3 = bf16[8,160,256]{2,1,0:T(8,128)(2,1)S(1)} collective-permute-done((bf16[8,160,256]{2,1,0:T(8,128)(2,1)}, bf16[8,160,256]{2,1,0:T(8,128)(2,1)S(1)}, u32[]{:S(2)}, u32[]{:S(2)}) %collective-permute-start.13) | collective-permute-done | bytes 655392 | tf_op jit(solution)/shard_map/ppermute | solution.py:39
  109.0 4.0 %copy-done.1 = bf16[1024,5120]{1,0:T(8,128)(2,1)S(1)} copy-done((bf16[1024,5120]{1,0:T(8,128)(2,1)S(1)}, bf16[1024,5120]{1,0:T(8,128)(2,1)}, u32[]{:S(2)}) %copy-start.1) | copy-done | bytes 10485784
  113.0 5.0 %shard_map.98 = bf16[2,512,256]{2,1,0:T(8,128)(2,1)S(1)} custom-call(s32[25]{0:T(128)S(1)} %copy-done.6, bf16[2,512,5120]{2,1,0:T(8,128)(2,1)S(1)} %bitcast.20, bf16[8,160,256]{2,1,0:T(8,128)(2,1)S(1)} %copy-done.2, bf16[8,160,256]{2,1,0:T(8,128)(2,1)S(1)} %collective-permute-done.11.w1, bf16[8,160,256]{2,1,0:T(8,128)(2,1)S(1)} %collective-permute-done.12.w2, ...), custom_call_target="tpu_custom_call" | custom-call | flops 2684354560 | bytes 14680064 | tf_op jit(solution)/shard_map/pallas_call | solution.py:201
  118.0 2.1 %collective-permute-start.14 = (bf16[512,256]{1,0:T(8,128)(2,1)S(1)}, bf16[512,256]{1,0:T(8,128)(2,1)S(1)}, u32[]{:S(2)}, u32[]{:S(2)}) collective-permute-start(bf16[512,256]{1,0:T(8,128)(2,1)S(1)} %get-tuple-element.43), channel_id=1, source_target_pairs={{0,8},{1,9},{2,10},{3,11},{4,12},{5,13},{6,14},{7,15},{8,0},{9,1},... | collective-permute-start | bytes 786440 | tf_op jit(solution)/shard_map/ppermute | solution.py:39
  120.2 2.6 %fusion.2 = bf16[1,640,512]{2,1,0:T(8,128)(2,1)} fusion(bf16[640,512]{1,0:T(8,128)(2,1)} %collective-permute-done.19, f32[2,640,512]{2,1,0:T(8,128)} %convert_add_fusion, s32[]{:T(128)S(6)} %select_n.85), kind=kLoop, calls=%fused_computation.7 | loop fusion | flops 983040 | bytes 2621444 | tf_op jit(solution)/shard_map/broadcast_in_dim | solution.py:266
  122.7 4.2 %shard_map.95 = (f32[640,512]{1,0:T(8,128)}, f32[640,512]{1,0:T(8,128)}) custom-call(f32[8,160,256]{2,1,0:T(8,128)} %bitcast.21, f32[640,512]{1,0:T(8,128)} %g.5, f32[640,512]{1,0:T(8,128)} %m.3), custom_call_target="tpu_custom_call" | custom-call | tf_op jit(solution)/shard_map/pallas_call | solution.py:176
  127.0 0.9 maximum_select_fusion
  (40 shorter events, 0.1 us)
Async XLA Ops:
  7.2 4.4 %copy-start.17 = (s32[4]{0:T(128)S(1)}, s32[4]{0:T(128)}, u32[]{:S(2)}) copy-start(s32[4]{0:T(128)} %constant.105.clone) | copy-start | bytes 52
  7.2 1.1 copy-start.7
  7.2 4.5 %copy-start.3 = (bf16[512,512]{1,0:T(8,128)(2,1)S(1)}, bf16[512,512]{1,0:T(8,128)(2,1)}, u32[]{:S(2)}) copy-start(bf16[512,512]{1,0:T(8,128)(2,1)} %key_grad.3) | copy-start | bytes 1572868
  7.2 101.8 %all-gather.7.cloned.1.call-start = ((), (), s32[]{:S(2)}) async-start(), calls=%async_computation.1 | async-start | bytes 15728640 | tf_op jit(solution)/shard_map/all_gather | solution.py:234
  7.9 114.8 %all-gather.5.cloned.1.call-start = ((), (), s32[]{:S(2)}) async-start(), calls=%async_computation | async-start | bytes 1474560 | tf_op jit(solution)/shard_map/all_gather | solution.py:259
  8.3 10.1 %collective-permute-start = (bf16[640,512]{1,0:T(8,128)(2,1)S(1)}, bf16[640,512]{1,0:T(8,128)(2,1)S(1)}, u32[]{:S(2)}, u32[]{:S(2)}) collective-permute-start(bf16[640,512]{1,0:T(8,128)(2,1)S(1)} %bitcast.23), channel_id=1, source_target_pairs={{0,8},{1,9},{2,10},{3,11},{4,12},{5,13},{6,14},{7,15},{8,0},{9,1},... | collective-permute-start | bytes 1966088 | tf_op jit(solution)/shard_map/ppermute | solution.py:39
  11.7 2.5 %copy-start = (bf16[512,5120]{1,0:T(8,128)(2,1)S(1)}, bf16[512,5120]{1,0:T(8,128)(2,1)}, u32[]{:S(2)}) copy-start(bf16[512,5120]{1,0:T(8,128)(2,1)} %tokens.2) | copy-start | bytes 15728644
  14.2 1.4 %copy-start.4 = (s32[25]{0:T(128)}, s32[25]{0:T(128)S(1)}, u32[]{:S(2)}) copy-start(s32[25]{0:T(128)S(1)} %concatenate.15.order) | copy-start | bytes 304
  15.6 17.8 %collective-permute-start.15 = (bf16[2,320,512]{2,1,0:T(8,128)(2,1)S(1)}, bf16[2,320,512]{2,1,0:T(8,128)(2,1)}, u32[]{:S(2)}, u32[]{:S(2)}) collective-permute-start(bf16[2,320,512]{2,1,0:T(8,128)(2,1)S(1)} %get-tuple-element.31), channel_id=1, source_target_pairs={{0,2},{1,3},{2,4},{3,5},{4,6},{5,7},{6,0},{7,1},{8,10},{9,11},{10,... | collective-permute-start | bytes 1966088 | tf_op jit(solution)/shard_map/ppermute | solution.py:39
  15.7 9.5 %copy-start.5 = (s32[25]{0:T(128)S(1)}, s32[25]{0:T(128)}, u32[]{:S(2)}) copy-start(s32[25]{0:T(128)} %copy-done.4) | copy-start | bytes 304
  15.7 20.0 %collective-permute-start.17 = (bf16[2,320,512]{2,1,0:T(8,128)(2,1)S(1)}, bf16[2,320,512]{2,1,0:T(8,128)(2,1)}, u32[]{:S(2)}, u32[]{:S(2)}) collective-permute-start(bf16[2,320,512]{2,1,0:T(8,128)(2,1)S(1)} %get-tuple-element.34), channel_id=1, source_target_pairs={{0,6},{1,7},{2,0},{3,1},{4,2},{5,3},{6,4},{7,5},{8,14},{9,15},{10,... | collective-permute-start | bytes 1966088 | tf_op jit(solution)/shard_map/ppermute | solution.py:39
  18.4 0.8 copy-start.8
  21.9 9.1 %collective-permute-start.1 = (bf16[160,256]{1,0:T(8,128)(2,1)}, bf16[160,256]{1,0:T(8,128)(2,1)S(1)}, u32[]{:S(2)}, u32[]{:S(2)}) collective-permute-start(bf16[160,256]{1,0:T(8,128)(2,1)} %get-tuple-element.21), channel_id=1, source_target_pairs={{0,16},{1,17},{2,18},{3,19},{4,20},{5,21},{6,22},{7,23},{8,24},{9,... | collective-permute-start | bytes 245768 | tf_op jit(solution)/shard_map/ppermute | solution.py:39
  21.9 9.1 %collective-permute-start.2 = (bf16[160,256]{1,0:T(8,128)(2,1)}, bf16[160,256]{1,0:T(8,128)(2,1)S(1)}, u32[]{:S(2)}, u32[]{:S(2)}) collective-permute-start(bf16[160,256]{1,0:T(8,128)(2,1)} %get-tuple-element.22), channel_id=1, source_target_pairs={{0,32},{1,33},{2,34},{3,35},{4,36},{5,37},{6,38},{7,39},{8,40},{9,... | collective-permute-start | bytes 245768 | tf_op jit(solution)/shard_map/ppermute | solution.py:39
  24.0 7.0 %copy-start.9 = (f32[160,256]{1,0:T(8,128)S(1)}, f32[160,256]{1,0:T(8,128)}, u32[]{:S(2)}) copy-start(f32[160,256]{1,0:T(8,128)} %get-tuple-element.20) | copy-start | bytes 491524
  24.0 7.0 %collective-permute-start.3 = (bf16[160,256]{1,0:T(8,128)(2,1)}, bf16[160,256]{1,0:T(8,128)(2,1)S(1)}, u32[]{:S(2)}, u32[]{:S(2)}) collective-permute-start(bf16[160,256]{1,0:T(8,128)(2,1)} %get-tuple-element.23), channel_id=1, source_target_pairs={{0,48},{1,49},{2,50},{3,51},{4,52},{5,53},{6,54},{7,55},{8,56},{9,... | collective-permute-start | bytes 245768 | tf_op jit(solution)/shard_map/ppermute | solution.py:39
  35.7 46.5 %collective-permute-start.16 = (bf16[2,640,512]{2,1,0:T(8,128)(2,1)}, bf16[2,640,512]{2,1,0:T(8,128)(2,1)}, u32[]{:S(2)}, u32[]{:S(2)}) collective-permute-start(bf16[2,640,512]{2,1,0:T(8,128)(2,1)} %pad_maximum_fusion), channel_id=1, source_target_pairs={{0,2},{1,3},{2,4},{3,5},{4,6},{5,7},{6,0},{7,1},{8,10},{9,11},{10,... | collective-permute-start | bytes 3932168 | tf_op jit(solution)/shard_map/ppermute | solution.py:39
  38.3 44.0 %collective-permute-start.18 = (bf16[2,640,512]{2,1,0:T(8,128)(2,1)}, bf16[2,640,512]{2,1,0:T(8,128)(2,1)}, u32[]{:S(2)}, u32[]{:S(2)}) collective-permute-start(bf16[2,640,512]{2,1,0:T(8,128)(2,1)} %pad_maximum_fusion.1), channel_id=1, source_target_pairs={{0,6},{1,7},{2,0},{3,1},{4,2},{5,3},{6,4},{7,5},{8,14},{9,15},{10,... | collective-permute-start | bytes 3932168 | tf_op jit(solution)/shard_map/ppermute | solution.py:39
  40.8 8.9 %collective-permute-start.4 = (bf16[160,256]{1,0:T(8,128)(2,1)S(1)}, bf16[160,256]{1,0:T(8,128)(2,1)S(1)}, u32[]{:S(2)}, u32[]{:S(2)}) collective-permute-start(bf16[160,256]{1,0:T(8,128)(2,1)S(1)} %get-tuple-element.36), channel_id=1, source_target_pairs={{0,64},{1,65},{2,66},{3,67},{4,68},{5,69},{6,70},{7,71},{8,72},{9,... | collective-permute-start | bytes 245768 | tf_op jit(solution)/shard_map/ppermute | solution.py:39
  42.4 8.4 %collective-permute-start.5 = (bf16[160,256]{1,0:T(8,128)(2,1)S(1)}, bf16[160,256]{1,0:T(8,128)(2,1)S(1)}, u32[]{:S(2)}, u32[]{:S(2)}) collective-permute-start(bf16[160,256]{1,0:T(8,128)(2,1)S(1)} %get-tuple-element.36), channel_id=1, source_target_pairs={{0,128},{1,129},{2,130},{3,131},{4,132},{5,133},{6,134},{7,135},{8... | collective-permute-start | bytes 245768 | tf_op jit(solution)/shard_map/ppermute | solution.py:39
  47.4 5.8 %collective-permute-start.6 = (bf16[160,256]{1,0:T(8,128)(2,1)S(1)}, bf16[160,256]{1,0:T(8,128)(2,1)S(1)}, u32[]{:S(2)}, u32[]{:S(2)}) collective-permute-start(bf16[160,256]{1,0:T(8,128)(2,1)S(1)} %get-tuple-element.36), channel_id=1, source_target_pairs={{0,192},{1,193},{2,194},{3,195},{4,196},{5,197},{6,198},{7,199},{8... | collective-permute-start | bytes 245768 | tf_op jit(solution)/shard_map/ppermute | solution.py:39
  49.7 3.5 %copy-start.13 = (bf16[160,256]{1,0:T(8,128)(2,1)}, bf16[160,256]{1,0:T(8,128)(2,1)S(1)}, u32[]{:S(2)}) copy-start(bf16[160,256]{1,0:T(8,128)(2,1)S(1)} %collective-permute-done.4.r1) | copy-start | bytes 245764
  50.8 2.4 %copy-start.14 = (bf16[160,256]{1,0:T(8,128)(2,1)}, bf16[160,256]{1,0:T(8,128)(2,1)S(1)}, u32[]{:S(2)}) copy-start(bf16[160,256]{1,0:T(8,128)(2,1)S(1)} %collective-permute-done.5.r2) | copy-start | bytes 245764
  53.2 0.6 copy-start.15
  56.5 4.0 %collective-permute-start.7 = (bf16[160,256]{1,0:T(8,128)(2,1)}, bf16[160,256]{1,0:T(8,128)(2,1)S(1)}, u32[]{:S(2)}, u32[]{:S(2)}) collective-permute-start(bf16[160,256]{1,0:T(8,128)(2,1)} %get-tuple-element.27), channel_id=1, source_target_pairs={{0,1},{1,0},{2,3},{3,2},{4,5},{5,4},{6,7},{7,6},{8,9},{9,8},{10,11... | collective-permute-start | bytes 245768 | tf_op jit(solution)/shard_map/ppermute | solution.py:39
  60.4 0.6 copy-start.16
  62.7 9.6 %collective-permute-start.10 = (bf16[2,160,256]{2,1,0:T(8,128)(2,1)}, bf16[2,160,256]{2,1,0:T(8,128)(2,1)S(1)}, u32[]{:S(2)}, u32[]{:S(2)}) collective-permute-start(bf16[2,160,256]{2,1,0:T(8,128)(2,1)} %shard_map.96.refs_0_), channel_id=1, source_target_pairs={{0,6},{1,7},{2,0},{3,1},{4,2},{5,3},{6,4},{7,5},{8,14},{9,15},{10,... | collective-permute-start | bytes 491528 | tf_op jit(solution)/shard_map/ppermute | solution.py:39
  63.2 9.1 %collective-permute-start.8 = (bf16[2,160,256]{2,1,0:T(8,128)(2,1)}, bf16[2,160,256]{2,1,0:T(8,128)(2,1)S(1)}, u32[]{:S(2)}, u32[]{:S(2)}) collective-permute-start(bf16[2,160,256]{2,1,0:T(8,128)(2,1)} %shard_map.96.refs_0_), channel_id=1, source_target_pairs={{0,2},{1,3},{2,4},{3,5},{4,6},{5,7},{6,0},{7,1},{8,10},{9,11},{10,... | collective-permute-start | bytes 491528 | tf_op jit(solution)/shard_map/ppermute | solution.py:39
  64.2 8.2 %collective-permute-start.9 = (bf16[2,160,256]{2,1,0:T(8,128)(2,1)}, bf16[2,160,256]{2,1,0:T(8,128)(2,1)S(1)}, u32[]{:S(2)}, u32[]{:S(2)}) collective-permute-start(bf16[2,160,256]{2,1,0:T(8,128)(2,1)} %shard_map.96.refs_0_), channel_id=1, source_target_pairs={{0,4},{1,5},{2,6},{3,7},{4,0},{5,1},{6,2},{7,3},{8,12},{9,13},{10,... | collective-permute-start | bytes 491528 | tf_op jit(solution)/shard_map/ppermute | solution.py:39
  72.3 0.7 copy-start.10
  72.3 0.7 copy-start.11
  73.0 0.7 copy-start.12
  75.7 16.6 %collective-permute-start.11 = (bf16[8,160,256]{2,1,0:T(8,128)(2,1)}, bf16[8,160,256]{2,1,0:T(8,128)(2,1)S(1)}, u32[]{:S(2)}, u32[]{:S(2)}) collective-permute-start(bf16[8,160,256]{2,1,0:T(8,128)(2,1)} %shard_map.97.w0), channel_id=1, source_target_pairs={{0,16},{1,17},{2,18},{3,19},{4,20},{5,21},{6,22},{7,23},{8,24},{9,... | collective-permute-start | bytes 1966088 | tf_op jit(solution)/shard_map/ppermute | solution.py:39
  78.7 28.2 %collective-permute-start.12 = (bf16[8,160,256]{2,1,0:T(8,128)(2,1)}, bf16[8,160,256]{2,1,0:T(8,128)(2,1)S(1)}, u32[]{:S(2)}, u32[]{:S(2)}) collective-permute-start(bf16[8,160,256]{2,1,0:T(8,128)(2,1)} %shard_map.97.w0), channel_id=1, source_target_pairs={{0,32},{1,33},{2,34},{3,35},{4,36},{5,37},{6,38},{7,39},{8,40},{9,... | collective-permute-start | bytes 1966088 | tf_op jit(solution)/shard_map/ppermute | solution.py:39
  81.1 27.9 %collective-permute-start.13 = (bf16[8,160,256]{2,1,0:T(8,128)(2,1)}, bf16[8,160,256]{2,1,0:T(8,128)(2,1)S(1)}, u32[]{:S(2)}, u32[]{:S(2)}) collective-permute-start(bf16[8,160,256]{2,1,0:T(8,128)(2,1)} %shard_map.97.w0), channel_id=1, source_target_pairs={{0,48},{1,49},{2,50},{3,51},{4,52},{5,53},{6,54},{7,55},{8,56},{9,... | collective-permute-start | bytes 1966088 | tf_op jit(solution)/shard_map/ppermute | solution.py:39
  86.1 22.9 %copy-start.2 = (bf16[8,160,256]{2,1,0:T(8,128)(2,1)S(1)}, bf16[8,160,256]{2,1,0:T(8,128)(2,1)}, u32[]{:S(2)}) copy-start(bf16[8,160,256]{2,1,0:T(8,128)(2,1)} %shard_map.97.w0) | copy-start | bytes 1966084
  86.1 22.9 %copy-start.6 = (s32[25]{0:T(128)S(1)}, s32[25]{0:T(128)}, u32[]{:S(2)}) copy-start(s32[25]{0:T(128)} %copy-done.4) | copy-start | bytes 304
  88.4 31.7 %collective-permute-start.19 = (bf16[640,512]{1,0:T(8,128)(2,1)}, bf16[640,512]{1,0:T(8,128)(2,1)}, u32[]{:S(2)}, u32[]{:S(2)}) collective-permute-start(bf16[640,512]{1,0:T(8,128)(2,1)} %fusion.1), channel_id=1, source_target_pairs={{0,1},{1,0},{2,3},{3,2},{4,5},{5,4},{6,7},{7,6},{8,9},{9,8},{10,11... | collective-permute-start | bytes 1966088 | tf_op jit(solution)/shard_map/ppermute | solution.py:39
  109.0 4.0 %copy-start.1 = (bf16[1024,5120]{1,0:T(8,128)(2,1)S(1)}, bf16[1024,5120]{1,0:T(8,128)(2,1)}, u32[]{:S(2)}) copy-start(bf16[1024,5120]{1,0:T(8,128)(2,1)} %all-gather.7.cloned.1.call-done) | copy-start | bytes 31457284
  118.0 8.9 %collective-permute-start.14 = (bf16[512,256]{1,0:T(8,128)(2,1)S(1)}, bf16[512,256]{1,0:T(8,128)(2,1)S(1)}, u32[]{:S(2)}, u32[]{:S(2)}) collective-permute-start(bf16[512,256]{1,0:T(8,128)(2,1)S(1)} %get-tuple-element.43), channel_id=1, source_target_pairs={{0,8},{1,9},{2,10},{3,11},{4,12},{5,13},{6,14},{7,15},{8,0},{9,1},... | collective-permute-start | bytes 786440 | tf_op jit(solution)/shard_map/ppermute | solution.py:39
Sparse Core Ops, SparseCore 0:
  9.8 32.7 all-gather.6
  56.6 27.2 all-gather.4

commit v3 on v2

v3 whole, which is shorter than its diff:
```python
import functools

import jax
import jax.numpy as jnp
from jax import lax
from jax.experimental import pallas as pl
from jax.experimental.pallas import tpu as pltpu
from jax.sharding import PartitionSpec as P

momentum_rate = 0.9
outer_rate = 0.7

F32, BF16 = jnp.float32, jnp.bfloat16
AXES = ("rep", "fsdp")
SIZES = (4, 4, 2, 4, 2)
REPLICAS = 32
D, KW, SHARD = 5120, 512, 640
TOK = 512
ROWS, COLS = 160, 256


def shift(value, zh=0, x=0, core=0, y=0, zl=0, both_ways=False):
    steps = (zh, x, core, y, zl)

    def index(place):
        n = 0
        for p, size in zip(place, SIZES):
            n = n * size + p
        return n

    pairs = []
    for a in range(4):
        for b in range(4):
            for c in range(2):
                for d in range(4):
                    for e in range(2):
                        place = (a, b, c, d, e)
                        sign = -1 if both_ways and c == 1 else 1
                        to = tuple((p + sign * s) % n for p, s, n in zip(place, steps, SIZES))
                        pairs.append((index(place), index(to)))
    return lax.ppermute(value, AXES, pairs)


def after(value, *others):
    return lax.optimization_barrier((value, *others))[0]


def grant(mib):
    return pltpu.CompilerParams(vmem_limit_bytes=mib << 20)


def grad_kernel(at, sizes, order, tokens, key_grad, *refs):
    outs, held, sem = refs[: len(sizes)], refs[-2], refs[-1]
    copies = []
    for k, i in enumerate(at):
        columns = pl.ds(pl.multiple_of(order[i] * SHARD, SHARD), SHARD)
        copies.append(pltpu.make_async_copy(tokens.at[:, columns], held.at[k], sem.at[k]))
        copies[-1].start()
    places = [(out, j) for out, n in zip(outs, sizes) for j in range(n)]
    for k, (out, j) in enumerate(places):
        copies[k].wait()
        out[j] = lax.dot_general(
            held[k], key_grad[...], (((0,), (0,)), ((), ())), preferred_element_type=F32
        ).astype(BF16)


def grad_parts(order, at, sizes, tokens, key_grad):
    n = len(at)
    here = pl.BlockSpec(memory_space=pltpu.VMEM)
    return pl.pallas_call(
        functools.partial(grad_kernel, at, sizes),
        in_specs=[
            pl.BlockSpec(memory_space=pltpu.SMEM),
            pl.BlockSpec(memory_space=pltpu.HBM),
            here,
        ],
        out_specs=[here] * len(sizes),
        out_shape=[jax.ShapeDtypeStruct((k, SHARD, KW), BF16) for k in sizes],
        scratch_shapes=[pltpu.VMEM((n, TOK, SHARD), BF16), pltpu.SemaphoreType.DMA((n,))],
        compiler_params=grant(4 + 3 * n),
        cost_estimate=pl.CostEstimate(
            flops=2 * n * TOK * SHARD * KW, bytes_accessed=n * 1310720, transcendentals=0
        ),
    )(order, tokens, key_grad)


def pair_kernel(order, g, l0, l1, own, p1, p2, p3):
    for k, ref in enumerate((own, p1, p2, p3)):
        rows = pl.ds(pl.multiple_of(order[16 + k] * ROWS, ROWS), ROWS)
        total = 2.0 * g[rows, :] - l0[rows, :].astype(F32) - l1[rows, :].astype(F32)
        ref[...] = total.astype(ref.dtype)


def pair_sums(order, g, l0, l1):
    block = pl.BlockSpec((SHARD, COLS), lambda s, o: (0, o[24]))
    out = pl.BlockSpec((ROWS, COLS), lambda s, o: (0, 0))
    return pl.pallas_call(
        pair_kernel,
        grid_spec=pltpu.PrefetchScalarGridSpec(
            num_scalar_prefetch=1, grid=(1,), in_specs=[block] * 3, out_specs=[out] * 4
        ),
        out_shape=[jax.ShapeDtypeStruct((ROWS, COLS), F32)]
        + [jax.ShapeDtypeStruct((ROWS, COLS), BF16)] * 3,
        compiler_params=grant(6),
    )(order, g, l0, l1)


def step_kernel(order, own, r1, r2, r3, g, m, average, start):
    avg = (own[...] + r1[...].astype(F32) + r2[...].astype(F32) + r3[...].astype(F32)) / REPLICAS
    new_m = momentum_rate * m[...] + avg
    new_g = g[...] - outer_rate * (avg + momentum_rate * new_m)
    average[...] = avg
    start[...] = new_g.astype(BF16)


def outer_step(order, own, r1, r2, r3, g, m):
    here = pl.BlockSpec((ROWS, COLS), lambda s, o: (0, 0))
    block = pl.BlockSpec((ROWS, COLS), lambda s, o: (o[16], o[24]))
    return pl.pallas_call(
        step_kernel,
        grid_spec=pltpu.PrefetchScalarGridSpec(
            num_scalar_prefetch=1, grid=(1,), in_specs=[here] * 4 + [block] * 2, out_specs=[here] * 2
        ),
        out_shape=[
            jax.ShapeDtypeStruct((ROWS, COLS), F32),
            jax.ShapeDtypeStruct((ROWS, COLS), BF16),
        ],
        compiler_params=grant(4),
    )(order, own, r1, r2, r3, g, m)


def join_kernel(*refs):
    *parts, out = refs
    at = 0
    for ref in parts:
        n = ref.shape[0]
        out[at : at + n] = ref[...]
        at += n


def join(*parts):
    n = sum(p.shape[0] for p in parts)
    return pl.pallas_call(
        join_kernel,
        out_shape=jax.ShapeDtypeStruct((n, *parts[0].shape[1:]), parts[0].dtype),
        compiler_params=grant(4),
    )(*parts)


def update_kernel(order, average, g, m, new_global, new_momentum):
    for h in range(2):
        cols = slice(h * COLS, (h + 1) * COLS)
        new_m = momentum_rate * m[:, cols] + average[h]
        new_momentum[:, cols] = new_m
        new_global[:, cols] = g[:, cols] - outer_rate * (average[h] + momentum_rate * new_m)


def update(order, average, g, m):
    block = pl.BlockSpec((ROWS, KW), lambda s, o: (o[28 + s], 0))
    return pl.pallas_call(
        update_kernel,
        grid_spec=pltpu.PrefetchScalarGridSpec(
            num_scalar_prefetch=1,
            grid=(4,),
            in_specs=[pl.BlockSpec((2, ROWS, COLS), lambda s, o: (s, 0, 0)), block, block],
            out_specs=[block] * 2,
        ),
        out_shape=[jax.ShapeDtypeStruct((SHARD, KW), F32)] * 2,
        compiler_params=grant(8),
    )(order, average, g, m)


def keys_kernel(order, tokens, w0, w1, w2, w3, keys, weights, held, sem):
    places = [(h, slice(k * COLS, (k + 1) * COLS)) for h in range(2) for k in range(2)]
    copies = []
    for n, (h, rows) in enumerate(places):
        copies.append(pltpu.make_async_copy(tokens.at[h, rows], held.at[n], sem.at[n]))
        copies[-1].start()
    for d in range(4):
        for z in range(2):
            for k, ref in enumerate((w0, w1, w2, w3)):
                at = order[4 + d] * (2 * SHARD) + order[12 + z] * SHARD + order[20 + k] * ROWS
                weights[pl.ds(pl.multiple_of(at, ROWS), ROWS), :] = ref[2 * d + z]
    for n, (h, rows) in enumerate(places):
        copies[n].wait()
        keys[h, rows] = jnp.dot(held[n], weights[...], preferred_element_type=F32).astype(BF16)


def keys_of(order, tokens, blocks):
    here = pl.BlockSpec(memory_space=pltpu.VMEM)
    return pl.pallas_call(
        keys_kernel,
        in_specs=[pl.BlockSpec(memory_space=pltpu.SMEM), pl.BlockSpec(memory_space=pltpu.HBM)]
        + [here] * 4,
        out_specs=here,
        scratch_shapes=[
            pltpu.VMEM((D, COLS), BF16),
            pltpu.VMEM((4, COLS, D), BF16),
            pltpu.SemaphoreType.DMA((4,)),
        ],
        out_shape=jax.ShapeDtypeStruct((2, TOK, COLS), BF16),
        compiler_params=grant(24),
        cost_estimate=pl.CostEstimate(flops=2 * TOK * D * KW, bytes_accessed=14 << 20, transcendentals=0),
    )(order, tokens, *blocks)


def per_device(local_weights, global_weights, momentum, tokens, key_grad):
    g, m, local = global_weights, momentum, local_weights[0]
    rep, fsdp = lax.axis_index("rep"), lax.axis_index("fsdp")
    core, x, y, zl = rep % 2, rep // 2 % 4, fsdp // 2, fsdp % 2
    odd = rep // 8 % 2
    four = jnp.arange(4)
    way = 1 - 2 * core
    piece = x + 2 * odd

    def shards_of(y):
        return (y % 4) * 2 + (zl + jnp.arange(2)) % 2

    order = jnp.concatenate(
        [
            shards_of(y + 2),
            shards_of(y - way),
            (y - four) % 4,
            shards_of(y + way),
            shards_of(y),
            (zl + four) % 2,
            (piece + four) % 4,
            (piece - four) % 4,
            core + 0 * four,
            (four + 2 * odd) % 4,
        ]
    ).astype(jnp.int32)

    local_other = shift(local, core=1)
    pairs = lax.all_gather(tokens, "rep", axis_index_groups=[[2 * k, 2 * k + 1] for k in range(16)])

    (far,) = grad_parts(order, (0, 1), (2,), tokens, key_grad)
    far_got = shift(far, y=1, both_ways=True)

    local_other = after(local_other, far)
    own, p1, p2, p3 = pair_sums(order, g, local, local_other)
    r1, r2, r3 = (shift(p, x=k + 1) for k, p in enumerate((p1, p2, p3)))

    (direct,) = grad_parts(order, (2, 3), (2,), after(tokens, p1), key_grad)
    direct_got = shift(direct, y=-1, both_ways=True)

    chips = own + after(r1, direct).astype(F32) + r2.astype(F32) + r3.astype(F32)
    sent = chips.astype(BF16)
    q1, q2, q3 = (shift(sent, zh=k, x=2 * (k % 2)) for k in (1, 2, 3))

    on_own, on_other, here = grad_parts(
        order, (8, 9, 10, 11), (1, 1, 2), after(tokens, sent), key_grad
    )
    on_other = on_other[0] + far_got[1]
    on_other_got = shift(on_other, y=1, both_ways=True)

    average, start = outer_step(order, chips, after(q1, on_other, here), q2, q3, g, m)
    whole = lax.all_gather(
        average, "rep", axis_index_groups=[[8 * k + j for j in range(8)] for k in range(4)]
    )

    pair = join(start[None], shift(start, zl=1)[None])
    on_own = on_own[0] + after(far_got, pair)[0]
    on_own_got = shift(on_own, y=1, both_ways=True)
    shards = join(pair, *(shift(pair, y=k) for k in (1, 2, 3)))
    shards, pairs = lax.optimization_barrier((shards, pairs))
    blocks = [
        shards,
        shift(shards, x=1),
        shift(shards, zh=1, both_ways=True),
        shift(shards, x=-1),
    ]

    grad_sent = here[1].astype(F32) + direct_got[1].astype(F32) + on_other_got.astype(F32)
    grad_got = shift(grad_sent.astype(BF16), zl=1)

    new_global, new_momentum = update(order, after(whole, shards), g, m)

    grad_kept = here[0].astype(F32) + direct_got[0].astype(F32) + on_own_got.astype(F32)
    weight_grad = (grad_kept + grad_got.astype(F32)).astype(BF16)[None]

    *blocks, new_global, weight_grad = lax.optimization_barrier((*blocks, new_global, weight_grad))
    keys = keys_of(order, pairs, blocks)
    keys_got = shift(lax.dynamic_index_in_dim(keys, 1 - core, 0, False), core=1)
    keys = lax.dynamic_index_in_dim(keys, core, 0, False)
    inner_keys = jnp.where(
        core == 0,
        jnp.concatenate([keys, keys_got], axis=1),
        jnp.concatenate([keys_got, keys], axis=1),
    )
    return (new_global, new_momentum, inner_keys, weight_grad)


def solution(mesh):
    placed = (
        P("rep", "fsdp", None),
        P("fsdp", None),
        P("fsdp", None),
        P(("rep", "fsdp"), None),
        P(("rep", "fsdp"), None),
    )
    return jax.shard_map(
        per_device,
        mesh=mesh,
        in_specs=placed,
        out_specs=(
            P("fsdp", None),
            P("fsdp", None),
            P(("rep", "fsdp"), None),
            P("rep", "fsdp", None),
        ),
        check_vma=False,
    )
```

time: 135 us -> 117 us (0.87)
  waiting for transfers between devices: 36.8 us -> 20.6 us
  starting transfers between devices: 32.7 us -> 42.8 us
  Pallas kernels: 25.4 us -> 20.9 us
  other arithmetic: 12.9 us -> 9.08 us
  local copies, waits for them, and re-layouts: 12.7 us -> 8.97 us
    ppermute x20, waiting for transfers between devices: 36.1 us -> 19.9 us  [shift(): return lax.ppermute(value, AXES, pairs)]
    ppermute x20, starting transfers between devices: 32.6 us -> 42.7 us  [shift(): return lax.ppermute(value, AXES, pairs)]
    pallas_call x2, Pallas kernels: 3.65 us -> 0.05 us  [join(): pl.pallas_call(join_kernel, out_shape=jax.ShapeDtypeStruct((n, *parts[0]....]
    pallas_call x4 -> x5, Pallas kernels: 16.4 us -> 18.9 us  [the longest x1 8.4 us: keys_of(): pl.pallas_call(keys_kernel, in_specs=[pl.BlockSpec(memory_space=pltpu.SME...]
    convert_element_type x1 -> x0, local copies, waits for them, and re-layouts: 2.3 us -> none  [per_device(): lax.dynamic_index_in_dim(rows, 1 - zl, 0, False).astype(BF16)]
    concatenate x2 -> x0, other arithmetic: 2.28 us -> none  [the longest x1 1.14 us: per_device(): up = jnp.concatenate([up[:, :HALF] + low, up[:, HALF:]], axis=1)]
    convert_element_type x0 -> x1, other arithmetic: none -> 2.19 us  [per_device(): grad_got = shift(grad_sent.astype(BF16), zl=1)]
    add x2 -> x4, other arithmetic: 5.06 us -> 3.03 us  [the longest x1 2 us: per_device(): on_own = on_own[0] + after(far_got, pair)[0]]
  transfers between devices with their start and end apart: 22 -> 22, of which waited for: 8 -> 8; matrix products, arithmetic and copies ran while one was open for 11% -> 7% of each run, Pallas kernels for 19% -> 11%
where the time goes in v3:
time: 117 us
  starting transfers between devices  42.8 us (37%)
  Pallas kernels  20.9 us (18%)
  waiting for transfers between devices  20.6 us (18%)
  between operations  14.4 us (12%)
  other arithmetic  9.08 us (8%)
  local copies, waits for them, and re-layouts  8.97 us (8%)
    ppermute x20, starting transfers between devices, shift(): return lax.ppermute(value, AXES, pairs)  42.7 us
    ppermute x20, waiting for transfers between devices, shift(): return lax.ppermute(value, AXES, pairs)  19.9 us
    unnamed x24, local copies, waits for them, and re-layouts  8.84 us
    pallas_call x1, Pallas kernels, keys_of(): pl.pallas_call(keys_kernel, in_specs=[pl.BlockSpec(memory_space=pltpu.SME...  8.4 us
    pallas_call x3, Pallas kernels, grad_parts(): pl.pallas_call(functools.partial(grad_kernel, at, sizes), in_specs=[pl.Bl...  7.83 us
    broadcast_in_dim x1, other arithmetic, per_device(): weight_grad = (grad_kept + grad_got.astype(F32)).astype(BF16)[None]  2.87 us
    pallas_call x1, Pallas kernels, update(): pl.pallas_call(update_kernel, grid_spec=pltpu.PrefetchScalarGridSpec(num_...  2.63 us
  transfers between devices with their start and end apart: 22, of which 8 were waited for; matrix products, arithmetic and copies ran while one was open for 7% of the time, Pallas kernels for 11%

profile of v3, /device:TPU:1, one launch (start us, length us, event | category | flops | bytes accessed | tf_op | source)
XLA Modules:
  0.0 116.7 jit_solution(12815265595925761672)
XLA Ops:
  7.2 0.0 all-gather.5.cloned.1.call-start
  7.2 0.7 all-gather.5.cloned.1.call-update
  7.9 0.0 all-gather.7.cloned.1.call-start
  8.2 0.1 concatenate.9.order
  8.3 0.0 copy-start
  8.3 2.5 %copy-done = bf16[512,5120]{1,0:T(8,128)(2,1)S(1)} copy-done((bf16[512,5120]{1,0:T(8,128)(2,1)S(1)}, bf16[512,5120]{1,0:T(8,128)(2,1)}, u32[]{:S(2)}) %copy-start) | copy-done | bytes 5242904
  10.8 1.8 %shard_map.84 = bf16[2,640,512]{2,1,0:T(8,128)(2,1)S(1)} custom-call(s32[32]{0:T(128)S(1)} %concatenate.9.order, bf16[512,5120]{1,0:T(8,128)(2,1)S(1)} %copy-done, bf16[512,512]{1,0:T(8,128)(2,1)S(1)} %copy-done.4), custom_call_target="tpu_custom_call" | custom-call | flops 671088640 | bytes 2621440 | tf_op jit(solution)/shard_map/pallas_call | solution.py:70
  12.6 3.6 %collective-permute-start.5 = (bf16[2,640,512]{2,1,0:T(8,128)(2,1)S(1)}, bf16[2,640,512]{2,1,0:T(8,128)(2,1)S(1)}, u32[]{:S(2)}, u32[]{:S(2)}) collective-permute-start(bf16[2,640,512]{2,1,0:T(8,128)(2,1)S(1)} %shard_map.84), channel_id=1, source_target_pairs={{0,2},{1,3},{2,4},{3,5},{4,6},{5,7},{6,0},{7,1},{8,14},{9,15},{10,... | collective-permute-start | bytes 3932168 | tf_op jit(solution)/shard_map/ppermute | solution.py:41
  16.3 0.0 collective-permute-start
  16.3 2.1 %collective-permute-done.l1 = bf16[640,512]{1,0:T(8,128)(2,1)S(1)} collective-permute-done((bf16[640,512]{1,0:T(8,128)(2,1)S(1)}, bf16[640,512]{1,0:T(8,128)(2,1)S(1)}, u32[]{:S(2)}, u32[]{:S(2)}) %collective-permute-start) | collective-permute-done | bytes 655392 | tf_op jit(solution)/shard_map/ppermute | solution.py:41
  18.4 0.8 shard_map.85
  19.2 1.3 %collective-permute-start.1 = (bf16[160,256]{1,0:T(8,128)(2,1)S(1)}, bf16[160,256]{1,0:T(8,128)(2,1)S(1)}, u32[]{:S(2)}, u32[]{:S(2)}) collective-permute-start(bf16[160,256]{1,0:T(8,128)(2,1)S(1)} %get-tuple-element.32), channel_id=1, source_target_pairs={{0,16},{1,17},{2,18},{3,19},{4,20},{5,21},{6,22},{7,23},{8,24},{9,... | collective-permute-start | bytes 245768 | tf_op jit(solution)/shard_map/ppermute | solution.py:41
  20.4 2.5 %collective-permute-start.2 = (bf16[160,256]{1,0:T(8,128)(2,1)S(1)}, bf16[160,256]{1,0:T(8,128)(2,1)S(1)}, u32[]{:S(2)}, u32[]{:S(2)}) collective-permute-start(bf16[160,256]{1,0:T(8,128)(2,1)S(1)} %get-tuple-element.35), channel_id=1, source_target_pairs={{0,32},{1,33},{2,34},{3,35},{4,36},{5,37},{6,38},{7,39},{8,40},{9,... | collective-permute-start | bytes 245768 | tf_op jit(solution)/shard_map/ppermute | solution.py:41
  22.9 1.2 collective-permute-start.3
  24.0 2.9 %shard_map.86 = bf16[2,640,512]{2,1,0:T(8,128)(2,1)} custom-call(s32[32]{0:T(128)S(1)} %concatenate.9.order, bf16[512,5120]{1,0:T(8,128)(2,1)S(1)} %copy-done, bf16[512,512]{1,0:T(8,128)(2,1)S(1)} %copy-done.4), custom_call_target="tpu_custom_call" | custom-call | flops 671088640 | bytes 2621440 | tf_op jit(solution)/shard_map/pallas_call | solution.py:70
  26.9 0.5 collective-permute-start.15
  27.5 0.0 collective-permute-done.1
  27.5 0.0 collective-permute-done.2
  27.5 0.0 collective-permute-done.3
  27.5 4.4 %collective-permute-start.4 = (bf16[160,256]{1,0:T(8,128)(2,1)S(1)}, bf16[160,256]{1,0:T(8,128)(2,1)S(1)}, u32[]{:S(2)}, u32[]{:S(2)}) collective-permute-start(bf16[160,256]{1,0:T(8,128)(2,1)S(1)} %get-tuple-element.56), channel_id=1, source_target_pairs={{0,96},{1,97},{2,98},{3,99},{4,100},{5,101},{6,102},{7,103},{8,104... | collective-permute-start | bytes 245768 | tf_op jit(solution)/shard_map/ppermute | solution.py:41
  31.9 5.1 %collective-permute-start.6 = (bf16[160,256]{1,0:T(8,128)(2,1)S(1)}, bf16[160,256]{1,0:T(8,128)(2,1)S(1)}, u32[]{:S(2)}, u32[]{:S(2)}) collective-permute-start(bf16[160,256]{1,0:T(8,128)(2,1)S(1)} %get-tuple-element.56), channel_id=1, source_target_pairs={{0,128},{1,129},{2,130},{3,131},{4,132},{5,133},{6,134},{7,135},{8... | collective-permute-start | bytes 245768 | tf_op jit(solution)/shard_map/ppermute | solution.py:41
  37.0 3.4 %collective-permute-start.7 = (bf16[160,256]{1,0:T(8,128)(2,1)S(1)}, bf16[160,256]{1,0:T(8,128)(2,1)S(1)}, u32[]{:S(2)}, u32[]{:S(2)}) collective-permute-start(bf16[160,256]{1,0:T(8,128)(2,1)S(1)} %get-tuple-element.56), channel_id=1, source_target_pairs={{0,224},{1,225},{2,226},{3,227},{4,228},{5,229},{6,230},{7,231},{8... | collective-permute-start | bytes 245768 | tf_op jit(solution)/shard_map/ppermute | solution.py:41
  40.5 3.1 %shard_map.87 = (bf16[1,640,512]{2,1,0:T(8,128)(2,1)S(1)}, bf16[1,640,512]{2,1,0:T(8,128)(2,1)S(1)}, bf16[2,640,512]{2,1,0:T(8,128)(2,1)S(1)}) custom-call(s32[32]{0:T(128)S(1)} %concatenate.9.order, bf16[512,5120]{1,0:T(8,128)(2,1)S(1)} %bitcast.28, bf16[512,512]{1,0:T(8,128)(2,1)S(1)} %copy-done.4), custom_call_target="tpu_custom_call" | custom-call | flops 1342177280 | bytes 5242880 | tf_op jit(solution)/shard_map/pallas_call | solution.py:70
  43.6 0.0 copy-start.5
  43.6 0.0 copy-start.3
  43.6 0.0 collective-permute-done.5
  43.6 1.0 copy-done.5
  44.7 1.0 fusion.4
  45.7 0.0 collective-permute-done.4.r1
  45.7 0.0 collective-permute-done.6.r2
  45.7 0.0 collective-permute-done.7.r3
  45.7 1.2 %shard_map.88 = (f32[160,256]{1,0:T(8,128)}, bf16[160,256]{1,0:T(8,128)(2,1)S(1)}) custom-call(s32[32]{0:T(128)S(1)} %concatenate.9.order, f32[160,256]{1,0:T(8,128)S(1)} %get-tuple-element.57.own, bf16[160,256]{1,0:T(8,128)(2,1)S(1)} %collective-permute-done.4.r1, bf16[160,256]{1,0:T(8,128)(2,1)S(1)} %collective-permute-done.6.r2, ...), custom_call_target="tpu_custom_call" | custom-call | tf_op jit(solution)/shard_map/pallas_call | solution.py:119
  46.9 0.0 all-gather.7.cloned.1.call-update
  47.0 0.0 copy-start.6
  47.0 2.7 %collective-permute-start.17 = (bf16[640,512]{1,0:T(8,128)(2,1)}, bf16[640,512]{1,0:T(8,128)(2,1)S(1)}, u32[]{:S(2)}, u32[]{:S(2)}) collective-permute-start(bf16[640,512]{1,0:T(8,128)(2,1)} %fusion.4), channel_id=1, source_target_pairs={{0,2},{1,3},{2,4},{3,5},{4,6},{5,7},{6,0},{7,1},{8,14},{9,15},{10,... | collective-permute-start | bytes 1966088 | tf_op jit(solution)/shard_map/ppermute | solution.py:41
  49.7 0.3 collective-permute-start.8
  50.0 3.0 %collective-permute-done.8 = bf16[160,256]{1,0:T(8,128)(2,1)S(1)} collective-permute-done((bf16[160,256]{1,0:T(8,128)(2,1)S(1)}, bf16[160,256]{1,0:T(8,128)(2,1)S(1)}, u32[]{:S(2)}, u32[]{:S(2)}) %collective-permute-start.8) | collective-permute-done | bytes 81952 | tf_op jit(solution)/shard_map/ppermute | solution.py:41
  53.0 2.0 %add_bitcast_fusion = bf16[640,512]{1,0:T(8,128)(2,1)} fusion(bf16[1,640,512]{2,1,0:T(8,128)(2,1)S(1)} %get-tuple-element.46, bf16[2,640,512]{2,1,0:T(8,128)(2,1)} %copy-done.9), kind=kLoop, calls=%fused_computation.8 | loop fusion | flops 327680 | bytes 1966080 | tf_op jit(solution)/shard_map/add | solution.py:263
  55.0 0.1 collective-permute-start.16
  55.1 2.4 %collective-permute-done.17 = bf16[640,512]{1,0:T(8,128)(2,1)S(1)} collective-permute-done((bf16[640,512]{1,0:T(8,128)(2,1)}, bf16[640,512]{1,0:T(8,128)(2,1)S(1)}, u32[]{:S(2)}, u32[]{:S(2)}) %collective-permute-start.17) | collective-permute-done | bytes 655392 | tf_op jit(solution)/shard_map/ppermute | solution.py:41
  57.6 0.0 collective-permute-done.15
  57.6 2.2 %fusion = bf16[640,512]{1,0:T(8,128)(2,1)} fusion(bf16[640,512]{1,0:T(8,128)(2,1)S(1)} %collective-permute-done.17, bf16[2,640,512]{2,1,0:T(8,128)(2,1)} %collective-permute-done.15, bf16[2,640,512]{2,1,0:T(8,128)(2,1)S(1)} %copy-done.6), kind=kLoop, calls=%fused_computation.1 | loop fusion | flops 1966080 | bytes 2621440 | tf_op jit(solution)/shard_map/convert_element_type | solution.py:275
  59.8 0.3 collective-permute-start.18
  60.1 1.8 %collective-permute-start.10 = (bf16[2,160,256]{2,1,0:T(8,128)(2,1)S(1)}, bf16[2,160,256]{2,1,0:T(8,128)(2,1)S(1)}, u32[]{:S(2)}, u32[]{:S(2)}) collective-permute-start(bf16[2,160,256]{2,1,0:T(8,128)(2,1)S(1)} %shard_map.89.refs_0_), channel_id=1, source_target_pairs={{0,4},{1,5},{2,6},{3,7},{4,0},{5,1},{6,2},{7,3},{8,12},{9,13},{10,... | collective-permute-start | bytes 491528 | tf_op jit(solution)/shard_map/ppermute | solution.py:41
  61.9 1.4 %collective-permute-start.11 = (bf16[2,160,256]{2,1,0:T(8,128)(2,1)S(1)}, bf16[2,160,256]{2,1,0:T(8,128)(2,1)S(1)}, u32[]{:S(2)}, u32[]{:S(2)}) collective-permute-start(bf16[2,160,256]{2,1,0:T(8,128)(2,1)S(1)} %shard_map.89.refs_0_), channel_id=1, source_target_pairs={{0,6},{1,7},{2,0},{3,1},{4,2},{5,3},{6,4},{7,5},{8,14},{9,15},{10,... | collective-permute-start | bytes 491528 | tf_op jit(solution)/shard_map/ppermute | solution.py:41
  63.4 0.3 collective-permute-start.9
  63.7 3.9 %collective-permute-done.10.refs_2_ = bf16[2,160,256]{2,1,0:T(8,128)(2,1)S(1)} collective-permute-done((bf16[2,160,256]{2,1,0:T(8,128)(2,1)S(1)}, bf16[2,160,256]{2,1,0:T(8,128)(2,1)S(1)}, u32[]{:S(2)}, u32[]{:S(2)}) %collective-permute-start.10) | collective-permute-done | bytes 163872 | tf_op jit(solution)/shard_map/ppermute | solution.py:41
  67.6 2.9 %collective-permute-done.11.refs_3_ = bf16[2,160,256]{2,1,0:T(8,128)(2,1)S(1)} collective-permute-done((bf16[2,160,256]{2,1,0:T(8,128)(2,1)S(1)}, bf16[2,160,256]{2,1,0:T(8,128)(2,1)S(1)}, u32[]{:S(2)}, u32[]{:S(2)}) %collective-permute-start.11) | collective-permute-done | bytes 163872 | tf_op jit(solution)/shard_map/ppermute | solution.py:41
  70.5 0.8 collective-permute-done.9.refs_1_
  71.3 0.0 all-gather.5.cloned.1.call-done
  71.3 0.4 collective-permute-start.12
  71.7 3.2 %collective-permute-start.13 = (bf16[8,160,256]{2,1,0:T(8,128)(2,1)S(1)}, bf16[8,160,256]{2,1,0:T(8,128)(2,1)}, u32[]{:S(2)}, u32[]{:S(2)}) collective-permute-start(bf16[8,160,256]{2,1,0:T(8,128)(2,1)S(1)} %shard_map.90.w0), channel_id=1, source_target_pairs={{0,64},{1,65},{2,66},{3,67},{4,68},{5,69},{6,70},{7,71},{8,200},{9... | collective-permute-start | bytes 1966088 | tf_op jit(solution)/shard_map/ppermute | solution.py:41
  74.9 2.6 %collective-permute-start.14 = (bf16[8,160,256]{2,1,0:T(8,128)(2,1)S(1)}, bf16[8,160,256]{2,1,0:T(8,128)(2,1)}, u32[]{:S(2)}, u32[]{:S(2)}) collective-permute-start(bf16[8,160,256]{2,1,0:T(8,128)(2,1)S(1)} %shard_map.90.w0), channel_id=1, source_target_pairs={{0,48},{1,49},{2,50},{3,51},{4,52},{5,53},{6,54},{7,55},{8,56},{9,... | collective-permute-start | bytes 1966088 | tf_op jit(solution)/shard_map/ppermute | solution.py:41
  77.5 2.9 %fusion.3 = bf16[1,640,512]{2,1,0:T(8,128)(2,1)} fusion(bf16[640,512]{1,0:T(8,128)(2,1)} %collective-permute-done.18, bf16[640,512]{1,0:T(8,128)(2,1)} %collective-permute-done.16, bf16[2,640,512]{2,1,0:T(8,128)(2,1)} %collective-permute-done.15, bf16[2,640,512]{2,1,0:T(8,128)(2,1)} %copy-done.5), kind=kLoop, calls=%fused_computation.5 | loop fusion | flops 2621440 | bytes 3276800 | tf_op jit(solution)/shard_map/broadcast_in_dim | solution.py:280
  80.3 1.3 %copy-done.7 = f32[1280,256]{1,0:T(8,128)S(1)} copy-done((f32[1280,256]{1,0:T(8,128)S(1)}, f32[1280,256]{1,0:T(8,128)}, u32[]{:S(2)}) %copy-start.7) | copy-done | bytes 1310744
  81.7 2.6 %shard_map.91 = (f32[640,512]{1,0:T(8,128)}, f32[640,512]{1,0:T(8,128)}) custom-call(s32[32]{0:T(128)S(1)} %concatenate.9.order, f32[8,160,256]{2,1,0:T(8,128)S(1)} %bitcast.30, f32[640,512]{1,0:T(8,128)S(1)} %copy-done.1, f32[640,512]{1,0:T(8,128)S(1)} %copy-done.3), custom_call_target="tpu_custom_call" | custom-call | tf_op jit(solution)/shard_map/pallas_call | solution.py:160
  84.3 0.0 collective-permute-done.12.w1
  84.3 0.0 collective-permute-done.13.w2
  84.3 3.6 %collective-permute-done.14.w3 = bf16[8,160,256]{2,1,0:T(8,128)(2,1)} collective-permute-done((bf16[8,160,256]{2,1,0:T(8,128)(2,1)S(1)}, bf16[8,160,256]{2,1,0:T(8,128)(2,1)}, u32[]{:S(2)}, u32[]{:S(2)}) %collective-permute-start.14) | collective-permute-done | bytes 655392 | tf_op jit(solution)/shard_map/ppermute | solution.py:41
  87.9 4.0 %copy-done.2 = bf16[1024,5120]{1,0:T(8,128)(2,1)S(1)} copy-done((bf16[1024,5120]{1,0:T(8,128)(2,1)S(1)}, bf16[1024,5120]{1,0:T(8,128)(2,1)}, u32[]{:S(2)}) %copy-start.2) | copy-done | bytes 10485784
  91.8 8.4 %shard_map.92 = bf16[2,512,256]{2,1,0:T(8,128)(2,1)S(1)} custom-call(s32[32]{0:T(128)S(1)} %concatenate.9.order, bf16[2,512,5120]{2,1,0:T(8,128)(2,1)S(1)} %bitcast.29, bf16[8,160,256]{2,1,0:T(8,128)(2,1)S(1)} %shard_map.90.w0, bf16[8,160,256]{2,1,0:T(8,128)(2,1)} %collective-permute-done.12.w1, bf16[8,160,256]{2,1,0:T(8,128)(2,1)} %collective-permute-done.13.w2, ...), custom_call_target="tpu_custom_call" | custom-call | flops 2684354560 | bytes 14680064 | tf_op jit(solution)/shard_map/pallas_call | solution.py:191
  100.3 7.5 %collective-permute-start.19 = (bf16[512,256]{1,0:T(8,128)(2,1)S(1)}, bf16[512,256]{1,0:T(8,128)(2,1)S(1)}, u32[]{:S(2)}, u32[]{:S(2)}) collective-permute-start(bf16[512,256]{1,0:T(8,128)(2,1)S(1)} %get-tuple-element.59), channel_id=1, source_target_pairs={{0,8},{1,9},{2,10},{3,11},{4,12},{5,13},{6,14},{7,15},{8,0},{9,1},... | collective-permute-start | bytes 786440 | tf_op jit(solution)/shard_map/ppermute | solution.py:41
  107.8 1.2 collective-permute-done.19
  109.0 0.9 maximum_select_fusion
  (30 shorter events, 0.2 us)
Async XLA Ops:
  7.2 1.1 copy-start.4
  7.2 64.2 %all-gather.5.cloned.1.call-start = ((), (), s32[]{:S(2)}) async-start(), calls=%async_computation | async-start | bytes 15728640 | tf_op jit(solution)/shard_map/all_gather | solution.py:235
  7.9 72.4 %all-gather.7.cloned.1.call-start = ((), (), s32[]{:S(2)}) async-start(), calls=%async_computation.1 | async-start | bytes 1474560 | tf_op jit(solution)/shard_map/all_gather | solution.py:258
  8.3 2.5 %copy-start = (bf16[512,5120]{1,0:T(8,128)(2,1)S(1)}, bf16[512,5120]{1,0:T(8,128)(2,1)}, u32[]{:S(2)}) copy-start(bf16[512,5120]{1,0:T(8,128)(2,1)} %tokens.3) | copy-start | bytes 15728644
  10.8 5.5 %copy-start.8 = (bf16[1,640,512]{2,1,0:T(8,128)(2,1)S(1)}, bf16[1,640,512]{2,1,0:T(8,128)(2,1)}, u32[]{:S(2)}) copy-start(bf16[1,640,512]{2,1,0:T(8,128)(2,1)} %param.5) | copy-start | bytes 1966084
  10.8 7.6 %copy-start.1 = (f32[640,512]{1,0:T(8,128)S(1)}, f32[640,512]{1,0:T(8,128)}, u32[]{:S(2)}) copy-start(f32[640,512]{1,0:T(8,128)} %g.5) | copy-start | bytes 3932164
  12.6 31.0 %collective-permute-start.5 = (bf16[2,640,512]{2,1,0:T(8,128)(2,1)S(1)}, bf16[2,640,512]{2,1,0:T(8,128)(2,1)S(1)}, u32[]{:S(2)}, u32[]{:S(2)}) collective-permute-start(bf16[2,640,512]{2,1,0:T(8,128)(2,1)S(1)} %shard_map.84), channel_id=1, source_target_pairs={{0,2},{1,3},{2,4},{3,5},{4,6},{5,7},{6,0},{7,1},{8,14},{9,15},{10,... | collective-permute-start | bytes 3932168 | tf_op jit(solution)/shard_map/ppermute | solution.py:41
  16.3 2.1 %collective-permute-start = (bf16[640,512]{1,0:T(8,128)(2,1)S(1)}, bf16[640,512]{1,0:T(8,128)(2,1)S(1)}, u32[]{:S(2)}, u32[]{:S(2)}) collective-permute-start(bf16[640,512]{1,0:T(8,128)(2,1)S(1)} %bitcast.31), channel_id=1, source_target_pairs={{0,8},{1,9},{2,10},{3,11},{4,12},{5,13},{6,14},{7,15},{8,0},{9,1},... | collective-permute-start | bytes 1966088 | tf_op jit(solution)/shard_map/ppermute | solution.py:41
  18.4 22.1 %slice-start = ((s8[5242880]{0:T(1024)(128)(4,1)}), s8[4194304]{0:T(1024)(128)(4,1)S(1)}, s32[]{:S(2)}) async-start(s8[5242880]{0:T(1024)(128)(4,1)} %bitcast.27), calls=%async_computation.2 | async-start | bytes 8388608
  19.2 8.3 %collective-permute-start.1 = (bf16[160,256]{1,0:T(8,128)(2,1)S(1)}, bf16[160,256]{1,0:T(8,128)(2,1)S(1)}, u32[]{:S(2)}, u32[]{:S(2)}) collective-permute-start(bf16[160,256]{1,0:T(8,128)(2,1)S(1)} %get-tuple-element.32), channel_id=1, source_target_pairs={{0,16},{1,17},{2,18},{3,19},{4,20},{5,21},{6,22},{7,23},{8,24},{9,... | collective-permute-start | bytes 245768 | tf_op jit(solution)/shard_map/ppermute | solution.py:41
  20.4 7.0 %collective-permute-start.2 = (bf16[160,256]{1,0:T(8,128)(2,1)S(1)}, bf16[160,256]{1,0:T(8,128)(2,1)S(1)}, u32[]{:S(2)}, u32[]{:S(2)}) collective-permute-start(bf16[160,256]{1,0:T(8,128)(2,1)S(1)} %get-tuple-element.35), channel_id=1, source_target_pairs={{0,32},{1,33},{2,34},{3,35},{4,36},{5,37},{6,38},{7,39},{8,40},{9,... | collective-permute-start | bytes 245768 | tf_op jit(solution)/shard_map/ppermute | solution.py:41
  22.9 17.6 %slice-start.1 = ((s8[5242880]{0:T(1024)(128)(4,1)}), s8[1048576]{0:T(1024)(128)(4,1)S(1)}, s32[]{:S(2)}) async-start(s8[5242880]{0:T(1024)(128)(4,1)} %bitcast.27), calls=%async_computation.3 | async-start | bytes 2097152
  22.9 4.6 %collective-permute-start.3 = (bf16[160,256]{1,0:T(8,128)(2,1)S(1)}, bf16[160,256]{1,0:T(8,128)(2,1)S(1)}, u32[]{:S(2)}, u32[]{:S(2)}) collective-permute-start(bf16[160,256]{1,0:T(8,128)(2,1)S(1)} %get-tuple-element.36), channel_id=1, source_target_pairs={{0,48},{1,49},{2,50},{3,51},{4,52},{5,53},{6,54},{7,55},{8,56},{9,... | collective-permute-start | bytes 245768 | tf_op jit(solution)/shard_map/ppermute | solution.py:41
  26.9 30.6 %collective-permute-start.15 = (bf16[2,640,512]{2,1,0:T(8,128)(2,1)}, bf16[2,640,512]{2,1,0:T(8,128)(2,1)}, u32[]{:S(2)}, u32[]{:S(2)}) collective-permute-start(bf16[2,640,512]{2,1,0:T(8,128)(2,1)} %shard_map.86), channel_id=1, source_target_pairs={{0,6},{1,7},{2,0},{3,1},{4,2},{5,3},{6,4},{7,5},{8,10},{9,11},{10,... | collective-permute-start | bytes 3932168 | tf_op jit(solution)/shard_map/ppermute | solution.py:41
  27.5 18.2 %collective-permute-start.4 = (bf16[160,256]{1,0:T(8,128)(2,1)S(1)}, bf16[160,256]{1,0:T(8,128)(2,1)S(1)}, u32[]{:S(2)}, u32[]{:S(2)}) collective-permute-start(bf16[160,256]{1,0:T(8,128)(2,1)S(1)} %get-tuple-element.56), channel_id=1, source_target_pairs={{0,96},{1,97},{2,98},{3,99},{4,100},{5,101},{6,102},{7,103},{8,104... | collective-permute-start | bytes 245768 | tf_op jit(solution)/shard_map/ppermute | solution.py:41
  31.9 13.7 %collective-permute-start.6 = (bf16[160,256]{1,0:T(8,128)(2,1)S(1)}, bf16[160,256]{1,0:T(8,128)(2,1)S(1)}, u32[]{:S(2)}, u32[]{:S(2)}) collective-permute-start(bf16[160,256]{1,0:T(8,128)(2,1)S(1)} %get-tuple-element.56), channel_id=1, source_target_pairs={{0,128},{1,129},{2,130},{3,131},{4,132},{5,133},{6,134},{7,135},{8... | collective-permute-start | bytes 245768 | tf_op jit(solution)/shard_map/ppermute | solution.py:41
  37.0 8.6 %collective-permute-start.7 = (bf16[160,256]{1,0:T(8,128)(2,1)S(1)}, bf16[160,256]{1,0:T(8,128)(2,1)S(1)}, u32[]{:S(2)}, u32[]{:S(2)}) collective-permute-start(bf16[160,256]{1,0:T(8,128)(2,1)S(1)} %get-tuple-element.56), channel_id=1, source_target_pairs={{0,224},{1,225},{2,226},{3,227},{4,228},{5,229},{6,230},{7,231},{8... | collective-permute-start | bytes 245768 | tf_op jit(solution)/shard_map/ppermute | solution.py:41
  43.6 1.1 copy-start.5
  43.6 2.1 %copy-start.3 = (f32[640,512]{1,0:T(8,128)S(1)}, f32[640,512]{1,0:T(8,128)}, u32[]{:S(2)}) copy-start(f32[640,512]{1,0:T(8,128)} %m.3) | copy-start | bytes 3932164
  44.7 2.3 %copy-start.9 = (bf16[2,640,512]{2,1,0:T(8,128)(2,1)}, bf16[2,640,512]{2,1,0:T(8,128)(2,1)S(1)}, u32[]{:S(2)}) copy-start(bf16[2,640,512]{2,1,0:T(8,128)(2,1)S(1)} %collective-permute-done.5) | copy-start | bytes 3932164
  47.0 10.6 %copy-start.6 = (bf16[2,640,512]{2,1,0:T(8,128)(2,1)S(1)}, bf16[2,640,512]{2,1,0:T(8,128)(2,1)}, u32[]{:S(2)}) copy-start(bf16[2,640,512]{2,1,0:T(8,128)(2,1)} %copy-done.5) | copy-start | bytes 3932164
  47.0 10.6 %collective-permute-start.17 = (bf16[640,512]{1,0:T(8,128)(2,1)}, bf16[640,512]{1,0:T(8,128)(2,1)S(1)}, u32[]{:S(2)}, u32[]{:S(2)}) collective-permute-start(bf16[640,512]{1,0:T(8,128)(2,1)} %fusion.4), channel_id=1, source_target_pairs={{0,2},{1,3},{2,4},{3,5},{4,6},{5,7},{6,0},{7,1},{8,14},{9,15},{10,... | collective-permute-start | bytes 1966088 | tf_op jit(solution)/shard_map/ppermute | solution.py:41
  49.7 3.3 %collective-permute-start.8 = (bf16[160,256]{1,0:T(8,128)(2,1)S(1)}, bf16[160,256]{1,0:T(8,128)(2,1)S(1)}, u32[]{:S(2)}, u32[]{:S(2)}) collective-permute-start(bf16[160,256]{1,0:T(8,128)(2,1)S(1)} %get-tuple-element.41), channel_id=1, source_target_pairs={{0,1},{1,0},{2,3},{3,2},{4,5},{5,4},{6,7},{7,6},{8,9},{9,8},{10,11... | collective-permute-start | bytes 245768 | tf_op jit(solution)/shard_map/ppermute | solution.py:41
  55.0 22.4 %collective-permute-start.16 = (bf16[640,512]{1,0:T(8,128)(2,1)}, bf16[640,512]{1,0:T(8,128)(2,1)}, u32[]{:S(2)}, u32[]{:S(2)}) collective-permute-start(bf16[640,512]{1,0:T(8,128)(2,1)} %add_bitcast_fusion), channel_id=1, source_target_pairs={{0,2},{1,3},{2,4},{3,5},{4,6},{5,7},{6,0},{7,1},{8,14},{9,15},{10,... | collective-permute-start | bytes 1966088 | tf_op jit(solution)/shard_map/ppermute | solution.py:41
  59.8 17.7 %collective-permute-start.18 = (bf16[640,512]{1,0:T(8,128)(2,1)}, bf16[640,512]{1,0:T(8,128)(2,1)}, u32[]{:S(2)}, u32[]{:S(2)}) collective-permute-start(bf16[640,512]{1,0:T(8,128)(2,1)} %fusion), channel_id=1, source_target_pairs={{0,1},{1,0},{2,3},{3,2},{4,5},{5,4},{6,7},{7,6},{8,9},{9,8},{10,11... | collective-permute-start | bytes 1966088 | tf_op jit(solution)/shard_map/ppermute | solution.py:41
  60.1 7.5 %collective-permute-start.10 = (bf16[2,160,256]{2,1,0:T(8,128)(2,1)S(1)}, bf16[2,160,256]{2,1,0:T(8,128)(2,1)S(1)}, u32[]{:S(2)}, u32[]{:S(2)}) collective-permute-start(bf16[2,160,256]{2,1,0:T(8,128)(2,1)S(1)} %shard_map.89.refs_0_), channel_id=1, source_target_pairs={{0,4},{1,5},{2,6},{3,7},{4,0},{5,1},{6,2},{7,3},{8,12},{9,13},{10,... | collective-permute-start | bytes 491528 | tf_op jit(solution)/shard_map/ppermute | solution.py:41
  61.9 8.6 %collective-permute-start.11 = (bf16[2,160,256]{2,1,0:T(8,128)(2,1)S(1)}, bf16[2,160,256]{2,1,0:T(8,128)(2,1)S(1)}, u32[]{:S(2)}, u32[]{:S(2)}) collective-permute-start(bf16[2,160,256]{2,1,0:T(8,128)(2,1)S(1)} %shard_map.89.refs_0_), channel_id=1, source_target_pairs={{0,6},{1,7},{2,0},{3,1},{4,2},{5,3},{6,4},{7,5},{8,14},{9,15},{10,... | collective-permute-start | bytes 491528 | tf_op jit(solution)/shard_map/ppermute | solution.py:41
  63.4 7.9 %collective-permute-start.9 = (bf16[2,160,256]{2,1,0:T(8,128)(2,1)S(1)}, bf16[2,160,256]{2,1,0:T(8,128)(2,1)S(1)}, u32[]{:S(2)}, u32[]{:S(2)}) collective-permute-start(bf16[2,160,256]{2,1,0:T(8,128)(2,1)S(1)} %shard_map.89.refs_0_), channel_id=1, source_target_pairs={{0,2},{1,3},{2,4},{3,5},{4,6},{5,7},{6,0},{7,1},{8,10},{9,11},{10,... | collective-permute-start | bytes 491528 | tf_op jit(solution)/shard_map/ppermute | solution.py:41
  71.3 12.9 %collective-permute-start.12 = (bf16[8,160,256]{2,1,0:T(8,128)(2,1)S(1)}, bf16[8,160,256]{2,1,0:T(8,128)(2,1)}, u32[]{:S(2)}, u32[]{:S(2)}) collective-permute-start(bf16[8,160,256]{2,1,0:T(8,128)(2,1)S(1)} %shard_map.90.w0), channel_id=1, source_target_pairs={{0,16},{1,17},{2,18},{3,19},{4,20},{5,21},{6,22},{7,23},{8,24},{9,... | collective-permute-start | bytes 1966088 | tf_op jit(solution)/shard_map/ppermute | solution.py:41
  71.7 12.6 %collective-permute-start.13 = (bf16[8,160,256]{2,1,0:T(8,128)(2,1)S(1)}, bf16[8,160,256]{2,1,0:T(8,128)(2,1)}, u32[]{:S(2)}, u32[]{:S(2)}) collective-permute-start(bf16[8,160,256]{2,1,0:T(8,128)(2,1)S(1)} %shard_map.90.w0), channel_id=1, source_target_pairs={{0,64},{1,65},{2,66},{3,67},{4,68},{5,69},{6,70},{7,71},{8,200},{9... | collective-permute-start | bytes 1966088 | tf_op jit(solution)/shard_map/ppermute | solution.py:41
  74.9 13.0 %collective-permute-start.14 = (bf16[8,160,256]{2,1,0:T(8,128)(2,1)S(1)}, bf16[8,160,256]{2,1,0:T(8,128)(2,1)}, u32[]{:S(2)}, u32[]{:S(2)}) collective-permute-start(bf16[8,160,256]{2,1,0:T(8,128)(2,1)S(1)} %shard_map.90.w0), channel_id=1, source_target_pairs={{0,48},{1,49},{2,50},{3,51},{4,52},{5,53},{6,54},{7,55},{8,56},{9,... | collective-permute-start | bytes 1966088 | tf_op jit(solution)/shard_map/ppermute | solution.py:41
  80.3 1.3 %copy-start.7 = (f32[1280,256]{1,0:T(8,128)S(1)}, f32[1280,256]{1,0:T(8,128)}, u32[]{:S(2)}) copy-start(f32[1280,256]{1,0:T(8,128)} %all-gather.7.cloned.1.call-done) | copy-start | bytes 3932164
  87.9 4.0 %copy-start.2 = (bf16[1024,5120]{1,0:T(8,128)(2,1)S(1)}, bf16[1024,5120]{1,0:T(8,128)(2,1)}, u32[]{:S(2)}) copy-start(bf16[1024,5120]{1,0:T(8,128)(2,1)} %all-gather.5.cloned.1.call-done) | copy-start | bytes 31457284
  100.3 8.7 %collective-permute-start.19 = (bf16[512,256]{1,0:T(8,128)(2,1)S(1)}, bf16[512,256]{1,0:T(8,128)(2,1)S(1)}, u32[]{:S(2)}, u32[]{:S(2)}) collective-permute-start(bf16[512,256]{1,0:T(8,128)(2,1)S(1)} %get-tuple-element.59), channel_id=1, source_target_pairs={{0,8},{1,9},{2,10},{3,11},{4,12},{5,13},{6,14},{7,15},{8,0},{9,1},... | collective-permute-start | bytes 786440 | tf_op jit(solution)/shard_map/ppermute | solution.py:41
Sparse Core Ops, SparseCore 0:
  9.8 32.7 all-gather.4
  47.1 25.2 all-gather.6

commit v4 on v3

v4 whole, which is shorter than its diff:
```python
import functools
import itertools

import jax
import jax.numpy as jnp
from jax import lax
from jax.experimental import pallas as pl
from jax.experimental.pallas import tpu as pltpu
from jax.sharding import PartitionSpec as P

momentum_rate = 0.9
outer_rate = 0.7

F32, BF16 = jnp.float32, jnp.bfloat16
AXES = ("rep", "fsdp")
SIZES = (4, 4, 2, 4, 2)
REPLICAS = 32
D, KW, SHARD = 5120, 512, 640
TOK = 512
ROWS, COLS = 160, 256


def send(value, target):
    pairs = []
    for place in itertools.product(*map(range, SIZES)):
        index = [0, 0]
        for k, where in enumerate((place, target(*place))):
            for p, size in zip(where, SIZES):
                index[k] = index[k] * size + p % size
        pairs.append(tuple(index))
    return lax.ppermute(value, AXES, pairs)


def shift(value, zh=0, x=0, core=0, y=0, zl=0, both_ways=False):
    def target(a, b, c, d, e):
        sign = -1 if both_ways and c == 1 else 1
        return a + sign * zh, b + sign * x, c + core, d + sign * y, e + zl

    return send(value, target)


def across(value):
    return send(value, lambda a, b, c, d, e: (a - 1 if e == 0 else a + 1, b, c, d, 1 - e))


def after(value, *others):
    return lax.optimization_barrier((value, *others))[0]


def grant(mib):
    return pltpu.CompilerParams(vmem_limit_bytes=mib << 20)


def grad_kernel(at, sizes, order, tokens, key_grad, *refs):
    outs, held, sem = refs[: len(sizes)], refs[-2], refs[-1]
    copies = []
    for k, i in enumerate(at):
        columns = pl.ds(pl.multiple_of(order[i] * SHARD, SHARD), SHARD)
        copies.append(pltpu.make_async_copy(tokens.at[:, columns], held.at[k], sem.at[k]))
        copies[-1].start()
    places = [(out, j) for out, n in zip(outs, sizes) for j in range(n)]
    for k, (out, j) in enumerate(places):
        copies[k].wait()
        out[j] = lax.dot_general(
            held[k], key_grad[...], (((0,), (0,)), ((), ())), preferred_element_type=F32
        ).astype(BF16)


def grad_parts(order, at, sizes, tokens, key_grad):
    n = len(at)
    here = pl.BlockSpec(memory_space=pltpu.VMEM)
    return pl.pallas_call(
        functools.partial(grad_kernel, at, sizes),
        in_specs=[
            pl.BlockSpec(memory_space=pltpu.SMEM),
            pl.BlockSpec(memory_space=pltpu.HBM),
            here,
        ],
        out_specs=[here] * len(sizes),
        out_shape=[jax.ShapeDtypeStruct((k, SHARD, KW), BF16) for k in sizes],
        scratch_shapes=[pltpu.VMEM((n, TOK, SHARD), BF16), pltpu.SemaphoreType.DMA((n,))],
        compiler_params=grant(4 + 3 * n),
        cost_estimate=pl.CostEstimate(
            flops=2 * n * TOK * SHARD * KW, bytes_accessed=n * 1310720, transcendentals=0
        ),
    )(order, tokens, key_grad)


def base_kernel(order, g, l, base):
    base[...] = 2.0 * g[...] - l[...].astype(F32)


def base_of(order, g, l):
    block = pl.BlockSpec((SHARD, COLS), lambda s, o: (0, o[24]))
    return pl.pallas_call(
        base_kernel,
        grid_spec=pltpu.PrefetchScalarGridSpec(
            num_scalar_prefetch=1,
            grid=(1,),
            in_specs=[block] * 2,
            out_specs=pl.BlockSpec((SHARD, COLS), lambda s, o: (0, 0)),
        ),
        out_shape=jax.ShapeDtypeStruct((SHARD, COLS), F32),
        compiler_params=grant(6),
    )(order, g, l)


def pair_kernel(order, base, l1, own, p1, p2, p3):
    for k, ref in enumerate((own, p1, p2, p3)):
        rows = pl.ds(pl.multiple_of(order[16 + k] * ROWS, ROWS), ROWS)
        ref[...] = (base[rows, :] - l1[rows, :].astype(F32)).astype(ref.dtype)


def pair_sums(order, base, l1):
    whole = pl.BlockSpec((SHARD, COLS), lambda s, o: (0, 0))
    block = pl.BlockSpec((SHARD, COLS), lambda s, o: (0, o[24]))
    out = pl.BlockSpec((ROWS, COLS), lambda s, o: (0, 0))
    return pl.pallas_call(
        pair_kernel,
        grid_spec=pltpu.PrefetchScalarGridSpec(
            num_scalar_prefetch=1, grid=(1,), in_specs=[whole, block], out_specs=[out] * 4
        ),
        out_shape=[jax.ShapeDtypeStruct((ROWS, COLS), F32)]
        + [jax.ShapeDtypeStruct((ROWS, COLS), BF16)] * 3,
        compiler_params=grant(6),
    )(order, base, l1)


def step_kernel(order, own, r1, r2, r3, g, m, average, start):
    avg = (own[...] + r1[...].astype(F32) + r2[...].astype(F32) + r3[...].astype(F32)) / REPLICAS
    new_m = momentum_rate * m[...] + avg
    new_g = g[...] - outer_rate * (avg + momentum_rate * new_m)
    average[...] = avg
    start[...] = new_g.astype(BF16)


def outer_step(order, own, r1, r2, r3, g, m):
    here = pl.BlockSpec((ROWS, COLS), lambda s, o: (0, 0))
    block = pl.BlockSpec((ROWS, COLS), lambda s, o: (o[16], o[24]))
    return pl.pallas_call(
        step_kernel,
        grid_spec=pltpu.PrefetchScalarGridSpec(
            num_scalar_prefetch=1, grid=(1,), in_specs=[here] * 4 + [block] * 2, out_specs=[here] * 2
        ),
        out_shape=[
            jax.ShapeDtypeStruct((ROWS, COLS), F32),
            jax.ShapeDtypeStruct((ROWS, COLS), BF16),
        ],
        compiler_params=grant(4),
    )(order, own, r1, r2, r3, g, m)


def join_kernel(*refs):
    *parts, out = refs
    at = 0
    for ref in parts:
        n = ref.shape[0]
        out[at : at + n] = ref[...]
        at += n


def join(*parts):
    n = sum(p.shape[0] for p in parts)
    return pl.pallas_call(
        join_kernel,
        out_shape=jax.ShapeDtypeStruct((n, *parts[0].shape[1:]), parts[0].dtype),
        compiler_params=grant(4),
    )(*parts)


def update_kernel(order, average, average_other, g, m, new_global, new_momentum):
    mine = order[24] == 0
    for h in range(2):
        cols = slice(h * COLS, (h + 1) * COLS)
        avg = jnp.where(mine == (h == 0), average[0], average_other[0])
        new_m = momentum_rate * m[:, cols] + avg
        new_momentum[:, cols] = new_m
        new_global[:, cols] = g[:, cols] - outer_rate * (avg + momentum_rate * new_m)


def update(order, average, average_other, g, m):
    block = pl.BlockSpec((ROWS, KW), lambda s, o: (o[28 + s], 0))
    part = pl.BlockSpec((1, ROWS, COLS), lambda s, o: (s, 0, 0))
    return pl.pallas_call(
        update_kernel,
        grid_spec=pltpu.PrefetchScalarGridSpec(
            num_scalar_prefetch=1,
            grid=(4,),
            in_specs=[part, part, block, block],
            out_specs=[block] * 2,
        ),
        out_shape=[jax.ShapeDtypeStruct((SHARD, KW), F32)] * 2,
        compiler_params=grant(8),
    )(order, average, average_other, g, m)


def hold_kernel(a, b, a_held, b_held, sem):
    copies = []
    for k, (src, dst) in enumerate(((a, a_held), (b, b_held))):
        for h in range(2):
            rows = pl.ds(h * COLS, COLS)
            copies.append(pltpu.make_async_copy(src.at[rows], dst.at[rows], sem.at[2 * k + h]))
            copies[-1].start()
    for copy in copies:
        copy.wait()


def hold(a, b):
    return pl.pallas_call(
        hold_kernel,
        in_specs=[pl.BlockSpec(memory_space=pl.ANY)] * 2,
        out_specs=[pl.BlockSpec(memory_space=pltpu.VMEM)] * 2,
        out_shape=[pltpu.VMEM((TOK, D), BF16)] * 2,
        scratch_shapes=[pltpu.SemaphoreType.DMA((4,))],
        compiler_params=grant(1),
    )(a, b)


def keys_kernel(order, tokens, tokens_other, w0, w1, w2, w3, keys, keys_other, weights):
    for d in range(4):
        for z in range(2):
            for k, ref in enumerate((w0, w1, w2, w3)):
                zl = order[12 + (z + (k == 2)) % 2]
                at = order[4 + d] * (2 * SHARD) + zl * SHARD + order[20 + k] * ROWS
                weights[pl.ds(pl.multiple_of(at, ROWS), ROWS), :] = ref[2 * d + z]
    for src, out in ((tokens_other, keys_other), (tokens, keys)):
        out[...] = jnp.dot(src[...], weights[...], preferred_element_type=F32).astype(BF16)


def keys_of(order, tokens, tokens_other, blocks):
    here = pl.BlockSpec(memory_space=pltpu.VMEM)
    return pl.pallas_call(
        keys_kernel,
        in_specs=[pl.BlockSpec(memory_space=pltpu.SMEM)] + [here] * 6,
        out_specs=[here] * 2,
        scratch_shapes=[pltpu.VMEM((D, COLS), BF16)],
        out_shape=[jax.ShapeDtypeStruct((TOK, COLS), BF16)] * 2,
        compiler_params=grant(24),
        cost_estimate=pl.CostEstimate(flops=20 * TOK * D * KW, bytes_accessed=14 << 20, transcendentals=0),
    )(order, tokens, tokens_other, *blocks)


def per_device(local_weights, global_weights, momentum, tokens, key_grad):
    g, m, local = global_weights, momentum, local_weights[0]
    rep, fsdp = lax.axis_index("rep"), lax.axis_index("fsdp")
    core, x, y, zl = rep % 2, rep // 2 % 4, fsdp // 2, fsdp % 2
    four = jnp.arange(4)
    way = 1 - 2 * core
    piece = x ^ (2 * zl)

    def shards_of(y):
        return (y % 4) * 2 + (zl + jnp.arange(2)) % 2

    order = jnp.concatenate(
        [
            shards_of(y + 2),
            shards_of(y - way),
            (y - four) % 4,
            shards_of(y + way),
            shards_of(y),
            (zl + four) % 2,
            (piece + four) % 4,
            (piece - four) % 4,
            core + 0 * four,
            piece ^ four,
        ]
    ).astype(jnp.int32)

    local_other = shift(local, core=1)
    base = base_of(order, g, local)
    local_other = after(local_other, base)
    tokens_other = shift(after(tokens, local_other), core=1)

    own, p1, p2, p3 = pair_sums(order, base, local_other)
    r1, r2, r3 = (shift(p, x=k + 1) for k, p in enumerate((p1, p2, p3)))

    (direct,) = grad_parts(order, (2, 3), (2,), after(tokens, p1), key_grad)
    direct_got = shift(direct, y=-1, both_ways=True)

    chips = own + after(r1, direct).astype(F32) + r2.astype(F32) + r3.astype(F32)
    sent = chips.astype(BF16)
    q1, q2, q3 = (shift(sent, zh=k) for k in (1, 2, 3))

    (far,) = grad_parts(order, (0, 1), (2,), after(tokens, sent), key_grad)
    far_got = shift(far, y=1, both_ways=True)
    on_own, on_other, here = grad_parts(
        order, (8, 9, 10, 11), (1, 1, 2), after(tokens, far), key_grad
    )

    q1, tokens_other = lax.optimization_barrier((after(q1, here), tokens_other))
    average, start = outer_step(order, chips, q1, q2, q3, g, m)

    start_other = shift(start, zl=1, x=2)
    average_1 = send(after(average, start), lambda a, b, c, d, e: (a, b ^ 1, c, d, e))
    pair = join(start[None], after(start_other, average_1)[None])
    average_1 = join(average[None], average_1[None])
    average_2 = send(after(average_1, pair), lambda a, b, c, d, e: (a, b ^ 2, c, d, e))
    shards = join(after(pair, average_2), *(shift(pair, y=k) for k in (1, 2, 3)))
    blocks = [shards, shift(shards, x=1), across(shards), shift(shards, x=-1)]

    on_other = on_other[0] + after(far_got, shards)[1]
    on_other_got = shift(on_other, y=1, both_ways=True)
    on_own = on_own[0] + far_got[0]
    on_own_got = shift(after(on_own, on_other), y=1, both_ways=True)

    average_2 = join(average_1, average_2)
    new_global, new_momentum = update(order, average_2, shift(average_2, core=1), g, m)

    grad_sent = here[1].astype(F32) + direct_got[1].astype(F32) + on_other_got.astype(F32)
    grad_got = shift(grad_sent.astype(BF16), zl=1)

    tokens, tokens_other = hold(after(tokens, shards), tokens_other)

    grad_kept = here[0].astype(F32) + direct_got[0].astype(F32) + on_own_got.astype(F32)
    weight_grad = (grad_kept + grad_got.astype(F32)).astype(BF16)[None]

    *blocks, new_global, tokens = lax.optimization_barrier((*blocks, new_global, tokens))
    keys, keys_other = keys_of(order, tokens, tokens_other, blocks)
    keys_got = shift(keys_other, core=1)
    inner_keys = jnp.where(
        core == 0,
        jnp.concatenate([keys, keys_got], axis=1),
        jnp.concatenate([keys_got, keys], axis=1),
    )
    return (new_global, new_momentum, inner_keys, weight_grad)


def solution(mesh):
    placed = (
        P("rep", "fsdp", None),
        P("fsdp", None),
        P("fsdp", None),
        P(("rep", "fsdp"), None),
        P(("rep", "fsdp"), None),
    )
    return jax.shard_map(
        per_device,
        mesh=mesh,
        in_specs=placed,
        out_specs=(
            P("fsdp", None),
            P("fsdp", None),
            P(("rep", "fsdp"), None),
            P("rep", "fsdp", None),
        ),
        check_vma=False,
    )
```

time: 117 us -> 94.5 us (0.81)
  between operations: 14.4 us -> 0.86 us
  starting transfers between devices: 42.8 us -> 52.3 us
  waiting for transfers between devices: 20.6 us -> 14 us
  Pallas kernels: 20.9 us -> 15.8 us
  other arithmetic: 9.08 us -> 5.66 us
  local copies, waits for them, and re-layouts: 8.97 us -> 5.56 us
    ppermute x20 -> x24, starting transfers between devices: 42.7 us -> 52.3 us  [send(): return lax.ppermute(value, AXES, pairs)]
    ppermute x20 -> x24, waiting for transfers between devices: 19.9 us -> 14 us  [send(): return lax.ppermute(value, AXES, pairs)]
    pallas_call x1, Pallas kernels: 8.4 us -> 3.58 us  [keys_of(): pl.pallas_call(keys_kernel, in_specs=[pl.BlockSpec(memory_space=pltpu.SME...]
    unnamed x24 -> x14, local copies, waits for them, and re-layouts: 8.84 us -> 5.47 us
    add x2, other arithmetic: 2.99 us -> 1.06 us  [the longest x1 0.97 us: per_device(): on_own = on_own[0] + far_got[0]]
    pallas_call x0 -> x2, Pallas kernels: none -> 1.37 us  [the longest x1 0.74 us: hold(): pl.pallas_call(hold_kernel, in_specs=[pl.BlockSpec(memory_space=pl.ANY)]...]
  transfers between devices with their start and end apart: 22 -> 24, of which waited for: 8 -> 12; matrix products, arithmetic and copies ran while one was open for 7% -> 3% of each run, Pallas kernels for 11% -> 17%
where the time goes in v4:
time: 94.5 us; the launch traced here: 94.2 us
  starting transfers between devices  52.3 us (55%)
  Pallas kernels  15.8 us (17%)
  waiting for transfers between devices  14 us (15%)
  other arithmetic  5.66 us (6%)
  local copies, waits for them, and re-layouts  5.56 us (6%)
    ppermute x24, starting transfers between devices, send(): return lax.ppermute(value, AXES, pairs)  52.3 us
    ppermute x24, waiting for transfers between devices, send(): return lax.ppermute(value, AXES, pairs)  14 us
    pallas_call x3, Pallas kernels, grad_parts(): pl.pallas_call(functools.partial(grad_kernel, at, sizes), in_specs=[pl.Bl...  6.81 us
    unnamed x14, local copies, waits for them, and re-layouts  5.47 us
    pallas_call x1, Pallas kernels, keys_of(): pl.pallas_call(keys_kernel, in_specs=[pl.BlockSpec(memory_space=pltpu.SME...  3.58 us
    pallas_call x1, Pallas kernels, update(): pl.pallas_call(update_kernel, grid_spec=pltpu.PrefetchScalarGridSpec(num_...  2.66 us
    broadcast_in_dim x1, other arithmetic, per_device(): weight_grad = (grad_kept + grad_got.astype(F32)).astype(BF16)[None]  2.46 us
  transfers between devices with their start and end apart: 24, of which 12 were waited for; matrix products, arithmetic and copies ran while one was open for 3% of the time, Pallas kernels for 17%

profile of v4, /device:TPU:1, one launch (start us, length us, event | category | flops | bytes accessed | tf_op | source)
XLA Modules:
  0.0 94.2 jit_solution(14918242177647209946)
XLA Ops:
  0.6 3.3 %collective-permute-start = (bf16[640,512]{1,0:T(8,128)(2,1)}, bf16[640,512]{1,0:T(8,128)(2,1)S(1)}, u32[]{:S(2)}, u32[]{:S(2)}) collective-permute-start(bf16[640,512]{1,0:T(8,128)(2,1)} %bitcast.23), channel_id=1, source_target_pairs={{0,8},{1,9},{2,10},{3,11},{4,12},{5,13},{6,14},{7,15},{8,0},{9,1},... | collective-permute-start | bytes 1966088 | tf_op jit(solution)/shard_map/ppermute | solution.py:31
  4.0 0.1 concatenate.9.order
  4.1 1.3 %copy-done.2 = f32[640,512]{1,0:T(8,128)S(1)} copy-done((f32[640,512]{1,0:T(8,128)S(1)}, f32[640,512]{1,0:T(8,128)}, u32[]{:S(2)}) %copy-start.2) | copy-done | bytes 1310744
  5.4 1.1 %copy-done.6 = bf16[1,640,512]{2,1,0:T(8,128)(2,1)S(1)} copy-done((bf16[1,640,512]{2,1,0:T(8,128)(2,1)S(1)}, bf16[1,640,512]{2,1,0:T(8,128)(2,1)}, u32[]{:S(2)}) %copy-start.6) | copy-done | bytes 655384
  6.5 0.6 shard_map.84.base
  7.2 0.0 copy-start.5
  7.2 0.0 collective-permute-done.l1
  7.2 0.2 collective-permute-start.5
  7.4 0.6 shard_map.85
  8.0 0.1 collective-permute-start.1
  8.1 1.9 %collective-permute-start.2 = (bf16[160,256]{1,0:T(8,128)(2,1)S(1)}, bf16[160,256]{1,0:T(8,128)(2,1)S(1)}, u32[]{:S(2)}, u32[]{:S(2)}) collective-permute-start(bf16[160,256]{1,0:T(8,128)(2,1)S(1)} %get-tuple-element.46), channel_id=1, source_target_pairs={{0,32},{1,33},{2,34},{3,35},{4,36},{5,37},{6,38},{7,39},{8,40},{9,... | collective-permute-start | bytes 245768 | tf_op jit(solution)/shard_map/ppermute | solution.py:31
  10.0 1.2 %collective-permute-start.3 = (bf16[160,256]{1,0:T(8,128)(2,1)S(1)}, bf16[160,256]{1,0:T(8,128)(2,1)S(1)}, u32[]{:S(2)}, u32[]{:S(2)}) collective-permute-start(bf16[160,256]{1,0:T(8,128)(2,1)S(1)} %get-tuple-element.47), channel_id=1, source_target_pairs={{0,48},{1,49},{2,50},{3,51},{4,52},{5,53},{6,54},{7,55},{8,56},{9,... | collective-permute-start | bytes 245768 | tf_op jit(solution)/shard_map/ppermute | solution.py:31
  11.2 2.5 %copy-done = bf16[512,5120]{1,0:T(8,128)(2,1)S(1)} copy-done((bf16[512,5120]{1,0:T(8,128)(2,1)S(1)}, bf16[512,5120]{1,0:T(8,128)(2,1)}, u32[]{:S(2)}) %copy-start) | copy-done | bytes 5242904
  13.7 1.8 %shard_map.86 = bf16[2,640,512]{2,1,0:T(8,128)(2,1)S(1)} custom-call(s32[32]{0:T(128)S(1)} %concatenate.9.order, bf16[512,5120]{1,0:T(8,128)(2,1)S(1)} %copy-done, bf16[512,512]{1,0:T(8,128)(2,1)S(1)} %copy-done.5), custom_call_target="tpu_custom_call" | custom-call | flops 671088640 | bytes 2621440 | tf_op jit(solution)/shard_map/pallas_call | solution.py:72
  15.5 0.0 collective-permute-done.1
  15.5 0.0 collective-permute-done.2
  15.6 0.0 collective-permute-done.3
  15.6 0.6 copy-done.1
  16.2 1.8 %shard_map.87 = bf16[2,640,512]{2,1,0:T(8,128)(2,1)S(1)} custom-call(s32[32]{0:T(128)S(1)} %concatenate.9.order, bf16[512,5120]{1,0:T(8,128)(2,1)S(1)} %copy-done.1, bf16[512,512]{1,0:T(8,128)(2,1)S(1)} %copy-done.5), custom_call_target="tpu_custom_call" | custom-call | flops 671088640 | bytes 2621440 | tf_op jit(solution)/shard_map/pallas_call | solution.py:72
  18.0 0.0 copy-start.3
  18.0 0.0 copy-start.4
  18.0 2.8 %collective-permute-start.20 = (bf16[2,640,512]{2,1,0:T(8,128)(2,1)S(1)}, bf16[2,640,512]{2,1,0:T(8,128)(2,1)S(1)}, u32[]{:S(2)}, u32[]{:S(2)}) collective-permute-start(bf16[2,640,512]{2,1,0:T(8,128)(2,1)S(1)} %shard_map.87), channel_id=1, source_target_pairs={{0,2},{1,3},{2,4},{3,5},{4,6},{5,7},{6,0},{7,1},{8,14},{9,15},{10,... | collective-permute-start | bytes 3932168 | tf_op jit(solution)/shard_map/ppermute | solution.py:31
  20.9 3.0 %collective-permute-start.4 = (bf16[160,256]{1,0:T(8,128)(2,1)S(1)}, bf16[160,256]{1,0:T(8,128)(2,1)S(1)}, u32[]{:S(2)}, u32[]{:S(2)}) collective-permute-start(bf16[160,256]{1,0:T(8,128)(2,1)S(1)} %get-tuple-element.77), channel_id=1, source_target_pairs={{0,64},{1,65},{2,66},{3,67},{4,68},{5,69},{6,70},{7,71},{8,72},{9,... | collective-permute-start | bytes 245768 | tf_op jit(solution)/shard_map/ppermute | solution.py:31
  23.8 5.1 %collective-permute-start.6 = (bf16[160,256]{1,0:T(8,128)(2,1)S(1)}, bf16[160,256]{1,0:T(8,128)(2,1)S(1)}, u32[]{:S(2)}, u32[]{:S(2)}) collective-permute-start(bf16[160,256]{1,0:T(8,128)(2,1)S(1)} %get-tuple-element.77), channel_id=1, source_target_pairs={{0,128},{1,129},{2,130},{3,131},{4,132},{5,133},{6,134},{7,135},{8... | collective-permute-start | bytes 245768 | tf_op jit(solution)/shard_map/ppermute | solution.py:31
  29.0 0.7 collective-permute-done.4.r1
  29.7 2.2 %collective-permute-start.7 = (bf16[160,256]{1,0:T(8,128)(2,1)S(1)}, bf16[160,256]{1,0:T(8,128)(2,1)S(1)}, u32[]{:S(2)}, u32[]{:S(2)}) collective-permute-start(bf16[160,256]{1,0:T(8,128)(2,1)S(1)} %get-tuple-element.77), channel_id=1, source_target_pairs={{0,192},{1,193},{2,194},{3,195},{4,196},{5,197},{6,198},{7,199},{8... | collective-permute-start | bytes 245768 | tf_op jit(solution)/shard_map/ppermute | solution.py:31
  31.8 3.1 %shard_map.88 = (bf16[1,640,512]{2,1,0:T(8,128)(2,1)S(1)}, bf16[1,640,512]{2,1,0:T(8,128)(2,1)S(1)}, bf16[2,640,512]{2,1,0:T(8,128)(2,1)S(1)}) custom-call(s32[32]{0:T(128)S(1)} %concatenate.9.order, bf16[512,5120]{1,0:T(8,128)(2,1)S(1)} %copy-done.1, bf16[512,512]{1,0:T(8,128)(2,1)S(1)} %copy-done.5), custom_call_target="tpu_custom_call" | custom-call | flops 1342177280 | bytes 5242880 | tf_op jit(solution)/shard_map/pallas_call | solution.py:72
  35.0 0.1 collective-permute-done.6.r2
  35.1 0.2 collective-permute-done.7.r3
  35.3 0.6 shard_map.89
  35.9 0.4 collective-permute-start.9
  36.3 2.7 %collective-permute-start.8 = (bf16[160,256]{1,0:T(8,128)(2,1)S(1)}, bf16[160,256]{1,0:T(8,128)(2,1)S(1)}, u32[]{:S(2)}, u32[]{:S(2)}) collective-permute-start(bf16[160,256]{1,0:T(8,128)(2,1)S(1)} %get-tuple-element.54), channel_id=1, source_target_pairs={{0,33},{1,32},{2,35},{3,34},{4,37},{5,36},{6,39},{7,38},{8,41},{9,... | collective-permute-start | bytes 245768 | tf_op jit(solution)/shard_map/ppermute | solution.py:31
  39.0 3.0 %collective-permute-done.8 = bf16[160,256]{1,0:T(8,128)(2,1)S(1)} collective-permute-done((bf16[160,256]{1,0:T(8,128)(2,1)S(1)}, bf16[160,256]{1,0:T(8,128)(2,1)S(1)}, u32[]{:S(2)}, u32[]{:S(2)}) %collective-permute-start.8) | collective-permute-done | bytes 81952 | tf_op jit(solution)/shard_map/ppermute | solution.py:31
  42.0 1.3 %collective-permute-start.10 = (f32[2,160,256]{2,1,0:T(8,128)S(1)}, f32[2,160,256]{2,1,0:T(8,128)S(1)}, u32[]{:S(2)}, u32[]{:S(2)}) collective-permute-start(f32[2,160,256]{2,1,0:T(8,128)S(1)} %shard_map.91.refs_0_), channel_id=1, source_target_pairs={{0,32},{1,33},{2,34},{3,35},{4,36},{5,37},{6,38},{7,39},{8,40},{9,... | collective-permute-start | bytes 983048 | tf_op jit(solution)/shard_map/ppermute | solution.py:31
  43.3 6.8 %collective-permute-start.12 = (bf16[2,160,256]{2,1,0:T(8,128)(2,1)S(1)}, bf16[2,160,256]{2,1,0:T(8,128)(2,1)S(1)}, u32[]{:S(2)}, u32[]{:S(2)}) collective-permute-start(bf16[2,160,256]{2,1,0:T(8,128)(2,1)S(1)} %shard_map.90.refs_0_), channel_id=1, source_target_pairs={{0,4},{1,5},{2,6},{3,7},{4,0},{5,1},{6,2},{7,3},{8,12},{9,13},{10,... | collective-permute-start | bytes 491528 | tf_op jit(solution)/shard_map/ppermute | solution.py:31
  50.1 8.4 %collective-permute-start.13 = (bf16[2,160,256]{2,1,0:T(8,128)(2,1)S(1)}, bf16[2,160,256]{2,1,0:T(8,128)(2,1)S(1)}, u32[]{:S(2)}, u32[]{:S(2)}) collective-permute-start(bf16[2,160,256]{2,1,0:T(8,128)(2,1)S(1)} %shard_map.90.refs_0_), channel_id=1, source_target_pairs={{0,6},{1,7},{2,0},{3,1},{4,2},{5,3},{6,4},{7,5},{8,14},{9,15},{10,... | collective-permute-start | bytes 491528 | tf_op jit(solution)/shard_map/ppermute | solution.py:31
  58.5 0.9 collective-permute-done.12.refs_2_
  59.4 1.4 %collective-permute-done.13.refs_3_ = bf16[2,160,256]{2,1,0:T(8,128)(2,1)S(1)} collective-permute-done((bf16[2,160,256]{2,1,0:T(8,128)(2,1)S(1)}, bf16[2,160,256]{2,1,0:T(8,128)(2,1)S(1)}, u32[]{:S(2)}, u32[]{:S(2)}) %collective-permute-start.13) | collective-permute-done | bytes 163872 | tf_op jit(solution)/shard_map/ppermute | solution.py:31
  60.8 0.0 collective-permute-done.20
  60.8 0.1 add_bitcast_fusion
  60.9 3.2 %collective-permute-start.22 = (bf16[640,512]{1,0:T(8,128)(2,1)S(1)}, bf16[640,512]{1,0:T(8,128)(2,1)S(1)}, u32[]{:S(2)}, u32[]{:S(2)}) collective-permute-start(bf16[640,512]{1,0:T(8,128)(2,1)S(1)} %add_bitcast_fusion), channel_id=1, source_target_pairs={{0,2},{1,3},{2,4},{3,5},{4,6},{5,7},{6,0},{7,1},{8,14},{9,15},{10,... | collective-permute-start | bytes 1966088 | tf_op jit(solution)/shard_map/ppermute | solution.py:31
  64.2 0.1 collective-permute-start.17
  64.3 0.1 collective-permute-start.14
  64.4 3.3 %collective-permute-start.15 = (bf16[8,160,256]{2,1,0:T(8,128)(2,1)S(1)}, bf16[8,160,256]{2,1,0:T(8,128)(2,1)S(1)}, u32[]{:S(2)}, u32[]{:S(2)}) collective-permute-start(bf16[8,160,256]{2,1,0:T(8,128)(2,1)S(1)} %shard_map.92.w0), channel_id=1, source_target_pairs={{0,193},{1,64},{2,195},{3,66},{4,197},{5,68},{6,199},{7,70},{8,201... | collective-permute-start | bytes 1966088 | tf_op jit(solution)/shard_map/ppermute | solution.py:31
  67.7 0.0 collective-permute-done.19
  67.7 1.4 %collective-permute-start.16 = (bf16[8,160,256]{2,1,0:T(8,128)(2,1)S(1)}, bf16[8,160,256]{2,1,0:T(8,128)(2,1)S(1)}, u32[]{:S(2)}, u32[]{:S(2)}) collective-permute-start(bf16[8,160,256]{2,1,0:T(8,128)(2,1)S(1)} %shard_map.92.w0), channel_id=1, source_target_pairs={{0,48},{1,49},{2,50},{3,51},{4,52},{5,53},{6,54},{7,55},{8,56},{9,... | collective-permute-start | bytes 1966088 | tf_op jit(solution)/shard_map/ppermute | solution.py:31
  69.1 1.0 %fusion.4 = bf16[640,512]{1,0:T(8,128)(2,1)} fusion(bf16[1,640,512]{2,1,0:T(8,128)(2,1)S(1)} %get-tuple-element.73, bf16[2,640,512]{2,1,0:T(8,128)(2,1)S(1)} %collective-permute-done.20), kind=kLoop, calls=%fused_computation.7 | loop fusion | flops 327680 | bytes 1966080 | tf_op jit(solution)/shard_map/add | solution.py:303
  70.1 0.7 shard_map.95
  70.8 0.8 collective-permute-done.22
  71.7 3.4 %collective-permute-start.21 = (bf16[640,512]{1,0:T(8,128)(2,1)}, bf16[640,512]{1,0:T(8,128)(2,1)}, u32[]{:S(2)}, u32[]{:S(2)}) collective-permute-start(bf16[640,512]{1,0:T(8,128)(2,1)} %fusion.4), channel_id=1, source_target_pairs={{0,2},{1,3},{2,4},{3,5},{4,6},{5,7},{6,0},{7,1},{8,14},{9,15},{10,... | collective-permute-start | bytes 1966088 | tf_op jit(solution)/shard_map/ppermute | solution.py:31
  75.1 1.1 %fusion = bf16[640,512]{1,0:T(8,128)(2,1)} fusion(bf16[640,512]{1,0:T(8,128)(2,1)S(1)} %collective-permute-done.22, bf16[2,640,512]{2,1,0:T(8,128)(2,1)S(1)} %collective-permute-done.19, bf16[2,640,512]{2,1,0:T(8,128)(2,1)S(1)} %get-tuple-element.50), kind=kLoop, calls=%fused_computation.1 | loop fusion | flops 1966080 | bytes 2621440 | tf_op jit(solution)/shard_map/convert_element_type | solution.py:310
  76.2 0.0 collective-permute-done.17.average_other
  76.2 0.0 collective-permute-start.23
  76.2 2.7 %shard_map.94 = (f32[640,512]{1,0:T(8,128)}, f32[640,512]{1,0:T(8,128)}) custom-call(s32[32]{0:T(128)S(1)} %concatenate.9.order, f32[4,160,256]{2,1,0:T(8,128)S(1)} %shard_map.93.average, f32[4,160,256]{2,1,0:T(8,128)S(1)} %collective-permute-done.17.average_other, f32[640,512]{1,0:T(8,128)S(1)} %copy-done.3, f32[640,512]{1,0:T(8,128)S(1)} %copy-done.4), custom_call_target="tpu_custom_call" | custom-call | tf_op jit(solution)/shard_map/pallas_call | solution.py:184
  78.9 2.7 %collective-permute-done.14.w1 = bf16[8,160,256]{2,1,0:T(8,128)(2,1)S(1)} collective-permute-done((bf16[8,160,256]{2,1,0:T(8,128)(2,1)S(1)}, bf16[8,160,256]{2,1,0:T(8,128)(2,1)S(1)}, u32[]{:S(2)}, u32[]{:S(2)}) %collective-permute-start.14) | collective-permute-done | bytes 655392 | tf_op jit(solution)/shard_map/ppermute | solution.py:31
  81.6 1.1 %collective-permute-done.15.w2 = bf16[8,160,256]{2,1,0:T(8,128)(2,1)S(1)} collective-permute-done((bf16[8,160,256]{2,1,0:T(8,128)(2,1)S(1)}, bf16[8,160,256]{2,1,0:T(8,128)(2,1)S(1)}, u32[]{:S(2)}, u32[]{:S(2)}) %collective-permute-start.15) | collective-permute-done | bytes 655392 | tf_op jit(solution)/shard_map/ppermute | solution.py:31
  82.6 0.8 collective-permute-done.16.w3
  83.5 3.6 %shard_map.96 = (bf16[512,256]{1,0:T(8,128)(2,1)S(1)}, bf16[512,256]{1,0:T(8,128)(2,1)S(1)}) custom-call(s32[32]{0:T(128)S(1)} %concatenate.9.order, bf16[512,5120]{1,0:T(8,128)(2,1)S(1)} %get-tuple-element.65.tokens, bf16[512,5120]{1,0:T(8,128)(2,1)S(1)} %get-tuple-element.66.tokens_other, bf16[8,160,256]{2,1,0:T(8,128)(2,1)S(1)} %shard_map.92.w0, ...), custom_call_target="tpu_custom_call" | custom-call | flops 26843545600 | bytes 14680064 | tf_op jit(solution)/shard_map/pallas_call | solution.py:232
  87.1 1.5 %collective-permute-start.18 = (bf16[512,256]{1,0:T(8,128)(2,1)S(1)}, bf16[512,256]{1,0:T(8,128)(2,1)S(1)}, u32[]{:S(2)}, u32[]{:S(2)}) collective-permute-start(bf16[512,256]{1,0:T(8,128)(2,1)S(1)} %get-tuple-element.72), channel_id=1, source_target_pairs={{0,8},{1,9},{2,10},{3,11},{4,12},{5,13},{6,14},{7,15},{8,0},{9,1},... | collective-permute-start | bytes 786440 | tf_op jit(solution)/shard_map/ppermute | solution.py:31
  88.5 1.2 %collective-permute-done.18 = bf16[512,256]{1,0:T(8,128)(2,1)S(1)} collective-permute-done((bf16[512,256]{1,0:T(8,128)(2,1)S(1)}, bf16[512,256]{1,0:T(8,128)(2,1)S(1)}, u32[]{:S(2)}, u32[]{:S(2)}) %collective-permute-start.18) | collective-permute-done | bytes 262176 | tf_op jit(solution)/shard_map/ppermute | solution.py:31
  89.7 0.9 maximum_select_fusion
  90.6 0.0 collective-permute-done.21
  90.6 1.1 %collective-permute-done.23 = bf16[640,512]{1,0:T(8,128)(2,1)} collective-permute-done((bf16[640,512]{1,0:T(8,128)(2,1)}, bf16[640,512]{1,0:T(8,128)(2,1)}, u32[]{:S(2)}, u32[]{:S(2)}) %collective-permute-start.23) | collective-permute-done | bytes 655392 | tf_op jit(solution)/shard_map/ppermute | solution.py:31
  91.8 2.5 %fusion.3 = bf16[1,640,512]{2,1,0:T(8,128)(2,1)} fusion(bf16[640,512]{1,0:T(8,128)(2,1)} %collective-permute-done.23, bf16[640,512]{1,0:T(8,128)(2,1)} %collective-permute-done.21, bf16[2,640,512]{2,1,0:T(8,128)(2,1)S(1)} %collective-permute-done.19, bf16[2,640,512]{2,1,0:T(8,128)(2,1)S(1)} %get-tuple-element.50), kind=kLoop, calls=%fused_computation.5 | loop fusion | flops 2621440 | bytes 3276800 | tf_op jit(solution)/shard_map/broadcast_in_dim | solution.py:315
  (24 shorter events, 0.3 us)
Async XLA Ops:
  0.6 6.5 %collective-permute-start = (bf16[640,512]{1,0:T(8,128)(2,1)}, bf16[640,512]{1,0:T(8,128)(2,1)S(1)}, u32[]{:S(2)}, u32[]{:S(2)}) collective-permute-start(bf16[640,512]{1,0:T(8,128)(2,1)} %bitcast.23), channel_id=1, source_target_pairs={{0,8},{1,9},{2,10},{3,11},{4,12},{5,13},{6,14},{7,15},{8,0},{9,1},... | collective-permute-start | bytes 1966088 | tf_op jit(solution)/shard_map/ppermute | solution.py:31
  4.1 1.3 %copy-start.2 = (f32[640,512]{1,0:T(8,128)S(1)}, f32[640,512]{1,0:T(8,128)}, u32[]{:S(2)}) copy-start(f32[640,512]{1,0:T(8,128)} %g.5) | copy-start | bytes 3932164
  5.4 1.1 %copy-start.6 = (bf16[1,640,512]{2,1,0:T(8,128)(2,1)S(1)}, bf16[1,640,512]{2,1,0:T(8,128)(2,1)}, u32[]{:S(2)}) copy-start(bf16[1,640,512]{2,1,0:T(8,128)(2,1)} %param.5) | copy-start | bytes 1966084
  7.2 4.0 %copy-start.5 = (bf16[512,512]{1,0:T(8,128)(2,1)S(1)}, bf16[512,512]{1,0:T(8,128)(2,1)}, u32[]{:S(2)}) copy-start(bf16[512,512]{1,0:T(8,128)(2,1)} %key_grad.5) | copy-start | bytes 1572868
  7.2 27.8 %collective-permute-start.5 = (bf16[512,5120]{1,0:T(8,128)(2,1)}, bf16[512,5120]{1,0:T(8,128)(2,1)S(1)}, u32[]{:S(2)}, u32[]{:S(2)}) collective-permute-start(bf16[512,5120]{1,0:T(8,128)(2,1)} %a), channel_id=1, source_target_pairs={{0,8},{1,9},{2,10},{3,11},{4,12},{5,13},{6,14},{7,15},{8,0},{9,1},... | collective-permute-start | bytes 15728648 | tf_op jit(solution)/shard_map/ppermute | solution.py:31
  8.0 7.5 %collective-permute-start.1 = (bf16[160,256]{1,0:T(8,128)(2,1)S(1)}, bf16[160,256]{1,0:T(8,128)(2,1)S(1)}, u32[]{:S(2)}, u32[]{:S(2)}) collective-permute-start(bf16[160,256]{1,0:T(8,128)(2,1)S(1)} %get-tuple-element.43), channel_id=1, source_target_pairs={{0,16},{1,17},{2,18},{3,19},{4,20},{5,21},{6,22},{7,23},{8,24},{9,... | collective-permute-start | bytes 245768 | tf_op jit(solution)/shard_map/ppermute | solution.py:31
  8.1 7.4 %collective-permute-start.2 = (bf16[160,256]{1,0:T(8,128)(2,1)S(1)}, bf16[160,256]{1,0:T(8,128)(2,1)S(1)}, u32[]{:S(2)}, u32[]{:S(2)}) collective-permute-start(bf16[160,256]{1,0:T(8,128)(2,1)S(1)} %get-tuple-element.46), channel_id=1, source_target_pairs={{0,32},{1,33},{2,34},{3,35},{4,36},{5,37},{6,38},{7,39},{8,40},{9,... | collective-permute-start | bytes 245768 | tf_op jit(solution)/shard_map/ppermute | solution.py:31
  10.0 5.5 %collective-permute-start.3 = (bf16[160,256]{1,0:T(8,128)(2,1)S(1)}, bf16[160,256]{1,0:T(8,128)(2,1)S(1)}, u32[]{:S(2)}, u32[]{:S(2)}) collective-permute-start(bf16[160,256]{1,0:T(8,128)(2,1)S(1)} %get-tuple-element.47), channel_id=1, source_target_pairs={{0,48},{1,49},{2,50},{3,51},{4,52},{5,53},{6,54},{7,55},{8,56},{9,... | collective-permute-start | bytes 245768 | tf_op jit(solution)/shard_map/ppermute | solution.py:31
  11.2 2.5 %copy-start = (bf16[512,5120]{1,0:T(8,128)(2,1)S(1)}, bf16[512,5120]{1,0:T(8,128)(2,1)}, u32[]{:S(2)}) copy-start(bf16[512,5120]{1,0:T(8,128)(2,1)} %a) | copy-start | bytes 15728644
  13.7 2.5 %copy-start.1 = (bf16[512,5120]{1,0:T(8,128)(2,1)S(1)}, bf16[512,5120]{1,0:T(8,128)(2,1)}, u32[]{:S(2)}) copy-start(bf16[512,5120]{1,0:T(8,128)(2,1)} %a) | copy-start | bytes 15728644
  18.0 17.2 %copy-start.3 = (f32[640,512]{1,0:T(8,128)S(1)}, f32[640,512]{1,0:T(8,128)}, u32[]{:S(2)}) copy-start(f32[640,512]{1,0:T(8,128)} %g.5) | copy-start | bytes 3932164
  18.0 17.2 %copy-start.4 = (f32[640,512]{1,0:T(8,128)S(1)}, f32[640,512]{1,0:T(8,128)}, u32[]{:S(2)}) copy-start(f32[640,512]{1,0:T(8,128)} %m.3) | copy-start | bytes 3932164
  18.0 42.8 %collective-permute-start.20 = (bf16[2,640,512]{2,1,0:T(8,128)(2,1)S(1)}, bf16[2,640,512]{2,1,0:T(8,128)(2,1)S(1)}, u32[]{:S(2)}, u32[]{:S(2)}) collective-permute-start(bf16[2,640,512]{2,1,0:T(8,128)(2,1)S(1)} %shard_map.87), channel_id=1, source_target_pairs={{0,2},{1,3},{2,4},{3,5},{4,6},{5,7},{6,0},{7,1},{8,14},{9,15},{10,... | collective-permute-start | bytes 3932168 | tf_op jit(solution)/shard_map/ppermute | solution.py:31
  20.9 8.8 %collective-permute-start.4 = (bf16[160,256]{1,0:T(8,128)(2,1)S(1)}, bf16[160,256]{1,0:T(8,128)(2,1)S(1)}, u32[]{:S(2)}, u32[]{:S(2)}) collective-permute-start(bf16[160,256]{1,0:T(8,128)(2,1)S(1)} %get-tuple-element.77), channel_id=1, source_target_pairs={{0,64},{1,65},{2,66},{3,67},{4,68},{5,69},{6,70},{7,71},{8,72},{9,... | collective-permute-start | bytes 245768 | tf_op jit(solution)/shard_map/ppermute | solution.py:31
  23.8 43.9 %collective-permute-start.19 = (bf16[2,640,512]{2,1,0:T(8,128)(2,1)S(1)}, bf16[2,640,512]{2,1,0:T(8,128)(2,1)S(1)}, u32[]{:S(2)}, u32[]{:S(2)}) collective-permute-start(bf16[2,640,512]{2,1,0:T(8,128)(2,1)S(1)} %shard_map.86), channel_id=1, source_target_pairs={{0,6},{1,7},{2,0},{3,1},{4,2},{5,3},{6,4},{7,5},{8,10},{9,11},{10,... | collective-permute-start | bytes 3932168 | tf_op jit(solution)/shard_map/ppermute | solution.py:31
  23.8 11.2 %collective-permute-start.6 = (bf16[160,256]{1,0:T(8,128)(2,1)S(1)}, bf16[160,256]{1,0:T(8,128)(2,1)S(1)}, u32[]{:S(2)}, u32[]{:S(2)}) collective-permute-start(bf16[160,256]{1,0:T(8,128)(2,1)S(1)} %get-tuple-element.77), channel_id=1, source_target_pairs={{0,128},{1,129},{2,130},{3,131},{4,132},{5,133},{6,134},{7,135},{8... | collective-permute-start | bytes 245768 | tf_op jit(solution)/shard_map/ppermute | solution.py:31
  29.7 5.6 %collective-permute-start.7 = (bf16[160,256]{1,0:T(8,128)(2,1)S(1)}, bf16[160,256]{1,0:T(8,128)(2,1)S(1)}, u32[]{:S(2)}, u32[]{:S(2)}) collective-permute-start(bf16[160,256]{1,0:T(8,128)(2,1)S(1)} %get-tuple-element.77), channel_id=1, source_target_pairs={{0,192},{1,193},{2,194},{3,195},{4,196},{5,197},{6,198},{7,199},{8... | collective-permute-start | bytes 245768 | tf_op jit(solution)/shard_map/ppermute | solution.py:31
  35.9 6.1 %collective-permute-start.9 = (f32[160,256]{1,0:T(8,128)S(1)}, f32[160,256]{1,0:T(8,128)S(1)}, u32[]{:S(2)}, u32[]{:S(2)}) collective-permute-start(f32[160,256]{1,0:T(8,128)S(1)} %get-tuple-element.55), channel_id=1, source_target_pairs={{0,16},{1,17},{2,18},{3,19},{4,20},{5,21},{6,22},{7,23},{8,24},{9,... | collective-permute-start | bytes 491528 | tf_op jit(solution)/shard_map/ppermute | solution.py:31
  36.3 5.7 %collective-permute-start.8 = (bf16[160,256]{1,0:T(8,128)(2,1)S(1)}, bf16[160,256]{1,0:T(8,128)(2,1)S(1)}, u32[]{:S(2)}, u32[]{:S(2)}) collective-permute-start(bf16[160,256]{1,0:T(8,128)(2,1)S(1)} %get-tuple-element.54), channel_id=1, source_target_pairs={{0,33},{1,32},{2,35},{3,34},{4,37},{5,36},{6,39},{7,38},{8,41},{9,... | collective-permute-start | bytes 245768 | tf_op jit(solution)/shard_map/ppermute | solution.py:31
  42.0 8.1 %collective-permute-start.10 = (f32[2,160,256]{2,1,0:T(8,128)S(1)}, f32[2,160,256]{2,1,0:T(8,128)S(1)}, u32[]{:S(2)}, u32[]{:S(2)}) collective-permute-start(f32[2,160,256]{2,1,0:T(8,128)S(1)} %shard_map.91.refs_0_), channel_id=1, source_target_pairs={{0,32},{1,33},{2,34},{3,35},{4,36},{5,37},{6,38},{7,39},{8,40},{9,... | collective-permute-start | bytes 983048 | tf_op jit(solution)/shard_map/ppermute | solution.py:31
  43.3 15.2 %collective-permute-start.11 = (bf16[2,160,256]{2,1,0:T(8,128)(2,1)S(1)}, bf16[2,160,256]{2,1,0:T(8,128)(2,1)S(1)}, u32[]{:S(2)}, u32[]{:S(2)}) collective-permute-start(bf16[2,160,256]{2,1,0:T(8,128)(2,1)S(1)} %shard_map.90.refs_0_), channel_id=1, source_target_pairs={{0,2},{1,3},{2,4},{3,5},{4,6},{5,7},{6,0},{7,1},{8,10},{9,11},{10,... | collective-permute-start | bytes 491528 | tf_op jit(solution)/shard_map/ppermute | solution.py:31
  43.3 16.1 %collective-permute-start.12 = (bf16[2,160,256]{2,1,0:T(8,128)(2,1)S(1)}, bf16[2,160,256]{2,1,0:T(8,128)(2,1)S(1)}, u32[]{:S(2)}, u32[]{:S(2)}) collective-permute-start(bf16[2,160,256]{2,1,0:T(8,128)(2,1)S(1)} %shard_map.90.refs_0_), channel_id=1, source_target_pairs={{0,4},{1,5},{2,6},{3,7},{4,0},{5,1},{6,2},{7,3},{8,12},{9,13},{10,... | collective-permute-start | bytes 491528 | tf_op jit(solution)/shard_map/ppermute | solution.py:31
  50.1 10.7 %collective-permute-start.13 = (bf16[2,160,256]{2,1,0:T(8,128)(2,1)S(1)}, bf16[2,160,256]{2,1,0:T(8,128)(2,1)S(1)}, u32[]{:S(2)}, u32[]{:S(2)}) collective-permute-start(bf16[2,160,256]{2,1,0:T(8,128)(2,1)S(1)} %shard_map.90.refs_0_), channel_id=1, source_target_pairs={{0,6},{1,7},{2,0},{3,1},{4,2},{5,3},{6,4},{7,5},{8,14},{9,15},{10,... | collective-permute-start | bytes 491528 | tf_op jit(solution)/shard_map/ppermute | solution.py:31
  60.9 10.7 %collective-permute-start.22 = (bf16[640,512]{1,0:T(8,128)(2,1)S(1)}, bf16[640,512]{1,0:T(8,128)(2,1)S(1)}, u32[]{:S(2)}, u32[]{:S(2)}) collective-permute-start(bf16[640,512]{1,0:T(8,128)(2,1)S(1)} %add_bitcast_fusion), channel_id=1, source_target_pairs={{0,2},{1,3},{2,4},{3,5},{4,6},{5,7},{6,0},{7,1},{8,14},{9,15},{10,... | collective-permute-start | bytes 1966088 | tf_op jit(solution)/shard_map/ppermute | solution.py:31
  64.2 12.0 %collective-permute-start.17 = (f32[4,160,256]{2,1,0:T(8,128)S(1)}, f32[4,160,256]{2,1,0:T(8,128)S(1)}, u32[]{:S(2)}, u32[]{:S(2)}) collective-permute-start(f32[4,160,256]{2,1,0:T(8,128)S(1)} %shard_map.93.average), channel_id=1, source_target_pairs={{0,8},{1,9},{2,10},{3,11},{4,12},{5,13},{6,14},{7,15},{8,0},{9,1},... | collective-permute-start | bytes 1966088 | tf_op jit(solution)/shard_map/ppermute | solution.py:31
  64.3 17.3 %collective-permute-start.14 = (bf16[8,160,256]{2,1,0:T(8,128)(2,1)S(1)}, bf16[8,160,256]{2,1,0:T(8,128)(2,1)S(1)}, u32[]{:S(2)}, u32[]{:S(2)}) collective-permute-start(bf16[8,160,256]{2,1,0:T(8,128)(2,1)S(1)} %shard_map.92.w0), channel_id=1, source_target_pairs={{0,16},{1,17},{2,18},{3,19},{4,20},{5,21},{6,22},{7,23},{8,24},{9,... | collective-permute-start | bytes 1966088 | tf_op jit(solution)/shard_map/ppermute | solution.py:31
  64.4 18.3 %collective-permute-start.15 = (bf16[8,160,256]{2,1,0:T(8,128)(2,1)S(1)}, bf16[8,160,256]{2,1,0:T(8,128)(2,1)S(1)}, u32[]{:S(2)}, u32[]{:S(2)}) collective-permute-start(bf16[8,160,256]{2,1,0:T(8,128)(2,1)S(1)} %shard_map.92.w0), channel_id=1, source_target_pairs={{0,193},{1,64},{2,195},{3,66},{4,197},{5,68},{6,199},{7,70},{8,201... | collective-permute-start | bytes 1966088 | tf_op jit(solution)/shard_map/ppermute | solution.py:31
  67.7 15.8 %collective-permute-start.16 = (bf16[8,160,256]{2,1,0:T(8,128)(2,1)S(1)}, bf16[8,160,256]{2,1,0:T(8,128)(2,1)S(1)}, u32[]{:S(2)}, u32[]{:S(2)}) collective-permute-start(bf16[8,160,256]{2,1,0:T(8,128)(2,1)S(1)} %shard_map.92.w0), channel_id=1, source_target_pairs={{0,48},{1,49},{2,50},{3,51},{4,52},{5,53},{6,54},{7,55},{8,56},{9,... | collective-permute-start | bytes 1966088 | tf_op jit(solution)/shard_map/ppermute | solution.py:31
  71.7 19.0 %collective-permute-start.21 = (bf16[640,512]{1,0:T(8,128)(2,1)}, bf16[640,512]{1,0:T(8,128)(2,1)}, u32[]{:S(2)}, u32[]{:S(2)}) collective-permute-start(bf16[640,512]{1,0:T(8,128)(2,1)} %fusion.4), channel_id=1, source_target_pairs={{0,2},{1,3},{2,4},{3,5},{4,6},{5,7},{6,0},{7,1},{8,14},{9,15},{10,... | collective-permute-start | bytes 1966088 | tf_op jit(solution)/shard_map/ppermute | solution.py:31
  76.2 15.6 %collective-permute-start.23 = (bf16[640,512]{1,0:T(8,128)(2,1)}, bf16[640,512]{1,0:T(8,128)(2,1)}, u32[]{:S(2)}, u32[]{:S(2)}) collective-permute-start(bf16[640,512]{1,0:T(8,128)(2,1)} %fusion), channel_id=1, source_target_pairs={{0,1},{1,0},{2,3},{3,2},{4,5},{5,4},{6,7},{7,6},{8,9},{9,8},{10,11... | collective-permute-start | bytes 1966088 | tf_op jit(solution)/shard_map/ppermute | solution.py:31
  87.1 2.6 %collective-permute-start.18 = (bf16[512,256]{1,0:T(8,128)(2,1)S(1)}, bf16[512,256]{1,0:T(8,128)(2,1)S(1)}, u32[]{:S(2)}, u32[]{:S(2)}) collective-permute-start(bf16[512,256]{1,0:T(8,128)(2,1)S(1)} %get-tuple-element.72), channel_id=1, source_target_pairs={{0,8},{1,9},{2,10},{3,11},{4,12},{5,13},{6,14},{7,15},{8,0},{9,1},... | collective-permute-start | bytes 786440 | tf_op jit(solution)/shard_map/ppermute | solution.py:31

commit v5 on v4

--- a/solution.py
+++ b/solution.py
@@ -39,6 +39,10 @@
     return send(value, target)
 
 
+def flip(value, zh=0, x=0):
+    return send(value, lambda a, b, c, d, e: (a ^ zh, b ^ x, c, d, e))
+
+
 def across(value):
     return send(value, lambda a, b, c, d, e: (a - 1 if e == 0 else a + 1, b, c, d, 1 - e))
 
@@ -51,39 +55,46 @@
     return pltpu.CompilerParams(vmem_limit_bytes=mib << 20)
 
 
+def in_hbm(value):
+    return pltpu.with_memory_space_constraint(value, pltpu.HBM)
+
+
 def grad_kernel(at, sizes, order, tokens, key_grad, *refs):
-    outs, held, sem = refs[: len(sizes)], refs[-2], refs[-1]
-    copies = []
+    outs, held, held_grad, sem = refs[: len(sizes)], *refs[len(sizes) :]
+    copies = [pltpu.make_async_copy(key_grad, held_grad, sem.at[len(at)])]
     for k, i in enumerate(at):
         columns = pl.ds(pl.multiple_of(order[i] * SHARD, SHARD), SHARD)
         copies.append(pltpu.make_async_copy(tokens.at[:, columns], held.at[k], sem.at[k]))
-        copies[-1].start()
+    for copy in copies:
+        copy.start()
+    copies[0].wait()
     places = [(out, j) for out, n in zip(outs, sizes) for j in range(n)]
     for k, (out, j) in enumerate(places):
-        copies[k].wait()
+        copies[k + 1].wait()
         out[j] = lax.dot_general(
-            held[k], key_grad[...], (((0,), (0,)), ((), ())), preferred_element_type=F32
+            held[k], held_grad[...], (((0,), (0,)), ((), ())), preferred_element_type=F32
         ).astype(BF16)
 
 
 def grad_parts(order, at, sizes, tokens, key_grad):
     n = len(at)
     here = pl.BlockSpec(memory_space=pltpu.VMEM)
+    hbm = pl.BlockSpec(memory_space=pltpu.HBM)
     return pl.pallas_call(
         functools.partial(grad_kernel, at, sizes),
-        in_specs=[
-            pl.BlockSpec(memory_space=pltpu.SMEM),
-            pl.BlockSpec(memory_space=pltpu.HBM),
-            here,
-        ],
+        in_specs=[pl.BlockSpec(memory_space=pltpu.SMEM), hbm, hbm],
         out_specs=[here] * len(sizes),
         out_shape=[jax.ShapeDtypeStruct((k, SHARD, KW), BF16) for k in sizes],
-        scratch_shapes=[pltpu.VMEM((n, TOK, SHARD), BF16), pltpu.SemaphoreType.DMA((n,))],
-        compiler_params=grant(4 + 3 * n),
+        scratch_shapes=[
+            pltpu.VMEM((n, TOK, SHARD), BF16),
+            pltpu.VMEM((TOK, KW), BF16),
+            pltpu.SemaphoreType.DMA((n + 1,)),
+        ],
+        compiler_params=grant(5 + 3 * n),
         cost_estimate=pl.CostEstimate(
             flops=2 * n * TOK * SHARD * KW, bytes_accessed=n * 1310720, transcendentals=0
         ),
-    )(order, tokens, key_grad)
+    )(order, in_hbm(tokens), in_hbm(key_grad))
 
 
 def base_kernel(order, g, l, base):
@@ -102,7 +113,7 @@
         ),
         out_shape=jax.ShapeDtypeStruct((SHARD, COLS), F32),
         compiler_params=grant(6),
-    )(order, g, l)
+    )(order, in_hbm(g), in_hbm(l))
 
 
 def pair_kernel(order, base, l1, own, p1, p2, p3):
@@ -126,28 +137,28 @@
     )(order, base, l1)
 
 
-def step_kernel(order, own, r1, r2, r3, g, m, average, start):
-    avg = (own[...] + r1[...].astype(F32) + r2[...].astype(F32) + r3[...].astype(F32)) / REPLICAS
+def step_kernel(order, own, got, g, m, average, start):
+    avg = (own[...] + got[...].astype(F32)) / REPLICAS
     new_m = momentum_rate * m[...] + avg
     new_g = g[...] - outer_rate * (avg + momentum_rate * new_m)
     average[...] = avg
     start[...] = new_g.astype(BF16)
 
 
-def outer_step(order, own, r1, r2, r3, g, m):
+def outer_step(order, own, got, g, m):
     here = pl.BlockSpec((ROWS, COLS), lambda s, o: (0, 0))
     block = pl.BlockSpec((ROWS, COLS), lambda s, o: (o[16], o[24]))
     return pl.pallas_call(
         step_kernel,
         grid_spec=pltpu.PrefetchScalarGridSpec(
-            num_scalar_prefetch=1, grid=(1,), in_specs=[here] * 4 + [block] * 2, out_specs=[here] * 2
+            num_scalar_prefetch=1, grid=(1,), in_specs=[here] * 2 + [block] * 2, out_specs=[here] * 2
         ),
         out_shape=[
             jax.ShapeDtypeStruct((ROWS, COLS), F32),
             jax.ShapeDtypeStruct((ROWS, COLS), BF16),
         ],
         compiler_params=grant(4),
-    )(order, own, r1, r2, r3, g, m)
+    )(order, own, got, g, m)
 
 
 def join_kernel(*refs):
@@ -208,12 +219,12 @@
 def hold(a, b):
     return pl.pallas_call(
         hold_kernel,
-        in_specs=[pl.BlockSpec(memory_space=pl.ANY)] * 2,
+        in_specs=[pl.BlockSpec(memory_space=pltpu.HBM)] * 2,
         out_specs=[pl.BlockSpec(memory_space=pltpu.VMEM)] * 2,
         out_shape=[pltpu.VMEM((TOK, D), BF16)] * 2,
         scratch_shapes=[pltpu.SemaphoreType.DMA((4,))],
         compiler_params=grant(1),
-    )(a, b)
+    )(in_hbm(a), in_hbm(b))
 
 
 def keys_kernel(order, tokens, tokens_other, w0, w1, w2, w3, keys, keys_other, weights):
@@ -268,55 +279,52 @@
 
     local_other = shift(local, core=1)
     base = base_of(order, g, local)
-    local_other = after(local_other, base)
-    tokens_other = shift(after(tokens, local_other), core=1)
-
-    own, p1, p2, p3 = pair_sums(order, base, local_other)
+    own, p1, p2, p3 = pair_sums(order, base, after(local_other, base))
     r1, r2, r3 = (shift(p, x=k + 1) for k, p in enumerate((p1, p2, p3)))
 
-    (direct,) = grad_parts(order, (2, 3), (2,), after(tokens, p1), key_grad)
+    far_other, direct = grad_parts(order, (1, 2, 3), (1, 2), after(tokens, p1), key_grad)
+    far_other_got = shift(far_other, y=1, both_ways=True)
     direct_got = shift(direct, y=-1, both_ways=True)
 
-    chips = own + after(r1, direct).astype(F32) + r2.astype(F32) + r3.astype(F32)
+    chips = own + after(r1, far_other).astype(F32) + r2.astype(F32) + r3.astype(F32)
     sent = chips.astype(BF16)
-    q1, q2, q3 = (shift(sent, zh=k) for k in (1, 2, 3))
-
-    (far,) = grad_parts(order, (0, 1), (2,), after(tokens, sent), key_grad)
-    far_got = shift(far, y=1, both_ways=True)
-    on_own, on_other, here = grad_parts(
-        order, (8, 9, 10, 11), (1, 1, 2), after(tokens, far), key_grad
+    tokens_other = shift(after(tokens, sent), core=1)
+    total = chips + flip(sent, zh=1).astype(F32)
+    sent = total.astype(BF16)
+    on_other, here_other, far_own = grad_parts(
+        order, (9, 11, 0), (1, 1, 1), after(tokens, sent), key_grad
     )
-
-    q1, tokens_other = lax.optimization_barrier((after(q1, here), tokens_other))
-    average, start = outer_step(order, chips, q1, q2, q3, g, m)
+    average, start = outer_step(order, total, after(flip(sent, zh=2), far_own), g, m)
 
     start_other = shift(start, zl=1, x=2)
-    average_1 = send(after(average, start), lambda a, b, c, d, e: (a, b ^ 1, c, d, e))
+    on_other = on_other + after(far_other_got, start)
+    on_other_got = shift(on_other, y=1, both_ways=True)
+    average_1 = flip(after(average, start), x=1)
     pair = join(start[None], after(start_other, average_1)[None])
+    pair, tokens_other, direct_got = lax.optimization_barrier((pair, tokens_other, direct_got))
     average_1 = join(average[None], average_1[None])
-    average_2 = send(after(average_1, pair), lambda a, b, c, d, e: (a, b ^ 2, c, d, e))
+    average_2 = flip(after(average_1, pair), x=2)
     shards = join(after(pair, average_2), *(shift(pair, y=k) for k in (1, 2, 3)))
     blocks = [shards, shift(shards, x=1), across(shards), shift(shards, x=-1)]
 
-    on_other = on_other[0] + after(far_got, shards)[1]
-    on_other_got = shift(on_other, y=1, both_ways=True)
-    on_own = on_own[0] + far_got[0]
-    on_own_got = shift(after(on_own, on_other), y=1, both_ways=True)
-
     average_2 = join(average_1, average_2)
-    new_global, new_momentum = update(order, average_2, shift(average_2, core=1), g, m)
-
-    grad_sent = here[1].astype(F32) + direct_got[1].astype(F32) + on_other_got.astype(F32)
+    average_other = shift(average_2, core=1)
+    new_global, new_momentum = update(order, average_2, average_other, g, m)
+
+    grad_sent = here_other[0].astype(F32) + direct_got[1].astype(F32) + after(on_other_got, shards)[0].astype(F32)
     grad_got = shift(grad_sent.astype(BF16), zl=1)
+    far_own_got = shift(after(far_own, shards), y=1, both_ways=True)
+    on_own, here_own = grad_parts(order, (8, 10), (1, 1), after(tokens, average_other), key_grad)
+    on_own_got = shift(on_own + far_own_got, y=1, both_ways=True)
 
     tokens, tokens_other = hold(after(tokens, shards), tokens_other)
 
-    grad_kept = here[0].astype(F32) + direct_got[0].astype(F32) + on_own_got.astype(F32)
+    grad_kept = here_own[0].astype(F32) + direct_got[0].astype(F32) + on_own_got[0].astype(F32)
     weight_grad = (grad_kept + grad_got.astype(F32)).astype(BF16)[None]
 
     *blocks, new_global, tokens = lax.optimization_barrier((*blocks, new_global, tokens))
     keys, keys_other = keys_of(order, tokens, tokens_other, blocks)
-    keys_got = shift(keys_other, core=1)
+    keys_got = after(shift(keys_other, core=1), weight_grad)
     inner_keys = jnp.where(
         core == 0,
         jnp.concatenate([keys, keys_got], axis=1),

time: 94.5 us -> 90.9 us (0.962)
  Pallas kernels: 15.8 us -> 27.8 us
  waiting for transfers between devices: 14 us -> 7.92 us
  local copies, waits for them, and re-layouts: 5.56 us -> 0.62 us
  starting transfers between devices: 52.3 us -> 48.2 us
    ppermute x24, waiting for transfers between devices: 14 us -> 7.92 us  [send(): return lax.ppermute(value, AXES, pairs)]
    unnamed x14 -> x16, local copies, waits for them, and re-layouts: 5.47 us -> 0.53 us
    ppermute x24, starting transfers between devices: 52.3 us -> 48.2 us  [send(): return lax.ppermute(value, AXES, pairs)]
    pallas_call x3, Pallas kernels: 6.81 us -> 10.6 us  [grad_parts(): pl.pallas_call(functools.partial(grad_kernel, at, sizes), in_specs=[pl.Bl...]
    pallas_call x1, Pallas kernels: 0.74 us -> 4.23 us  [hold(): pl.pallas_call(hold_kernel, in_specs=[pl.BlockSpec(memory_space=pltpu.HBM...]
    pallas_call x1, Pallas kernels: 2.66 us -> 4.25 us  [update(): pl.pallas_call(update_kernel, grid_spec=pltpu.PrefetchScalarGridSpec(num_...]
    broadcast_in_dim x1, other arithmetic: 2.46 us -> 1.2 us  [per_device(): weight_grad = (grad_kept + grad_got.astype(F32)).astype(BF16)[None]]
    pallas_call x1, Pallas kernels: 0.63 us -> 1.78 us  [base_of(): pl.pallas_call(base_kernel, grid_spec=pltpu.PrefetchScalarGridSpec(num_sc...]
  transfers between devices with their start and end apart: 24 -> 24, of which waited for: 12 -> 5; matrix products, arithmetic and copies ran while one was open for 3% -> 5% of each run, Pallas kernels for 17% -> 30%
where the time goes in v5:
time: 90.9 us; the launch traced here: 90.5 us
  starting transfers between devices  48.2 us (53%)
  Pallas kernels  27.8 us (31%)
  waiting for transfers between devices  7.92 us (9%)
  other arithmetic  5.08 us (6%)
  between operations  0.91 us (1%)
    ppermute x24, starting transfers between devices, send(): return lax.ppermute(value, AXES, pairs)  48.2 us
    pallas_call x3, Pallas kernels, grad_parts(): pl.pallas_call(functools.partial(grad_kernel, at, sizes), in_specs=[pl.Bl...  10.6 us
    ppermute x24, waiting for transfers between devices, send(): return lax.ppermute(value, AXES, pairs)  7.92 us
    pallas_call x1, Pallas kernels, keys_of(): pl.pallas_call(keys_kernel, in_specs=[pl.BlockSpec(memory_space=pltpu.SME...  4.73 us
    pallas_call x1, Pallas kernels, update(): pl.pallas_call(update_kernel, grid_spec=pltpu.PrefetchScalarGridSpec(num_...  4.25 us
    pallas_call x1, Pallas kernels, hold(): pl.pallas_call(hold_kernel, in_specs=[pl.BlockSpec(memory_space=pltpu.HBM...  4.23 us
  transfers between devices with their start and end apart: 24, of which 5 were waited for; matrix products, arithmetic and copies ran while one was open for 5% of the time, Pallas kernels for 30%

profile of v5, /device:TPU:1, one launch (start us, length us, event | category | flops | bytes accessed | tf_op | source)
XLA Modules:
  0.0 90.5 jit_solution(6706067037354897558)
XLA Ops:
  0.6 3.3 %collective-permute-start = (bf16[640,512]{1,0:T(8,128)(2,1)}, bf16[640,512]{1,0:T(8,128)(2,1)S(1)}, u32[]{:S(2)}, u32[]{:S(2)}) collective-permute-start(bf16[640,512]{1,0:T(8,128)(2,1)} %bitcast.19), channel_id=1, source_target_pairs={{0,8},{1,9},{2,10},{3,11},{4,12},{5,13},{6,14},{7,15},{8,0},{9,1},... | collective-permute-start | bytes 1966088 | tf_op jit(solution)/shard_map/ppermute | solution.py:31
  4.0 0.1 concatenate.9.order
  4.1 1.8 %shard_map.84.base = f32[640,256]{1,0:T(8,128)S(1)} custom-call(s32[32]{0:T(128)S(1)} %concatenate.9.order, f32[640,512]{1,0:T(8,128)} %g.5, bf16[640,512]{1,0:T(8,128)(2,1)} %bitcast.20), custom_call_target="tpu_custom_call" | custom-call | tf_op jit(solution)/shard_map/pallas_call | solution.py:106
  5.9 0.0 collective-permute-done.l1
  5.9 0.6 shard_map.85
  6.6 0.1 collective-permute-start.1
  6.6 1.9 %collective-permute-start.2 = (bf16[160,256]{1,0:T(8,128)(2,1)S(1)}, bf16[160,256]{1,0:T(8,128)(2,1)S(1)}, u32[]{:S(2)}, u32[]{:S(2)}) collective-permute-start(bf16[160,256]{1,0:T(8,128)(2,1)S(1)} %get-tuple-element.54), channel_id=1, source_target_pairs={{0,32},{1,33},{2,34},{3,35},{4,36},{5,37},{6,38},{7,39},{8,40},{9,... | collective-permute-start | bytes 245768 | tf_op jit(solution)/shard_map/ppermute | solution.py:31
  8.6 1.2 %collective-permute-start.3 = (bf16[160,256]{1,0:T(8,128)(2,1)S(1)}, bf16[160,256]{1,0:T(8,128)(2,1)S(1)}, u32[]{:S(2)}, u32[]{:S(2)}) collective-permute-start(bf16[160,256]{1,0:T(8,128)(2,1)S(1)} %get-tuple-element.55), channel_id=1, source_target_pairs={{0,48},{1,49},{2,50},{3,51},{4,52},{5,53},{6,54},{7,55},{8,56},{9,... | collective-permute-start | bytes 245768 | tf_op jit(solution)/shard_map/ppermute | solution.py:31
  9.7 3.4 %shard_map.86 = (bf16[1,640,512]{2,1,0:T(8,128)(2,1)S(1)}, bf16[2,640,512]{2,1,0:T(8,128)(2,1)S(1)}) custom-call(s32[32]{0:T(128)S(1)} %concatenate.9.order, bf16[512,5120]{1,0:T(8,128)(2,1)} %tokens.2, bf16[512,512]{1,0:T(8,128)(2,1)} %key_grad.5), custom_call_target="tpu_custom_call" | custom-call | flops 1006632960 | bytes 3932160 | tf_op jit(solution)/shard_map/pallas_call | solution.py:83
  13.2 0.3 collective-permute-done.1
  13.5 0.0 collective-permute-done.2
  13.5 0.1 collective-permute-done.3
  13.6 1.6 %collective-permute-start.8 = (bf16[512,5120]{1,0:T(8,128)(2,1)S(1)}, bf16[512,5120]{1,0:T(8,128)(2,1)S(1)}, u32[]{:S(2)}, u32[]{:S(2)}) collective-permute-start(bf16[512,5120]{1,0:T(8,128)(2,1)S(1)} %copy-done.4), channel_id=1, source_target_pairs={{0,8},{1,9},{2,10},{3,11},{4,12},{5,13},{6,14},{7,15},{8,0},{9,1},... | collective-permute-start | bytes 15728648 | tf_op jit(solution)/shard_map/ppermute | solution.py:31
  15.2 0.7 collective-permute-start.9
  15.8 2.0 %collective-permute-start.21 = (bf16[1,640,512]{2,1,0:T(8,128)(2,1)S(1)}, bf16[1,640,512]{2,1,0:T(8,128)(2,1)S(1)}, u32[]{:S(2)}, u32[]{:S(2)}) collective-permute-start(bf16[1,640,512]{2,1,0:T(8,128)(2,1)S(1)} %get-tuple-element.52), channel_id=1, source_target_pairs={{0,2},{1,3},{2,4},{3,5},{4,6},{5,7},{6,0},{7,1},{8,14},{9,15},{10,... | collective-permute-start | bytes 1966088 | tf_op jit(solution)/shard_map/ppermute | solution.py:31
  17.9 2.4 %collective-permute-start.4 = (bf16[160,256]{1,0:T(8,128)(2,1)S(1)}, bf16[160,256]{1,0:T(8,128)(2,1)S(1)}, u32[]{:S(2)}, u32[]{:S(2)}) collective-permute-start(bf16[160,256]{1,0:T(8,128)(2,1)S(1)} %fusion.3), channel_id=1, source_target_pairs={{0,64},{1,65},{2,66},{3,67},{4,68},{5,69},{6,70},{7,71},{8,72},{9,... | collective-permute-start | bytes 245768 | tf_op jit(solution)/shard_map/ppermute | solution.py:31
  20.3 2.5 %collective-permute-done.4 = bf16[160,256]{1,0:T(8,128)(2,1)S(1)} collective-permute-done((bf16[160,256]{1,0:T(8,128)(2,1)S(1)}, bf16[160,256]{1,0:T(8,128)(2,1)S(1)}, u32[]{:S(2)}, u32[]{:S(2)}) %collective-permute-start.4) | collective-permute-done | bytes 81952 | tf_op jit(solution)/shard_map/ppermute | solution.py:31
  22.8 0.1 fusion.9
  22.9 0.0 copy-start
  22.9 0.0 copy-start.1
  22.9 8.1 %collective-permute-start.5 = (bf16[160,256]{1,0:T(8,128)(2,1)S(1)}, bf16[160,256]{1,0:T(8,128)(2,1)S(1)}, u32[]{:S(2)}, u32[]{:S(2)}) collective-permute-start(bf16[160,256]{1,0:T(8,128)(2,1)S(1)} %get-tuple-element.91), channel_id=1, source_target_pairs={{0,128},{1,129},{2,130},{3,131},{4,132},{5,133},{6,134},{7,135},{8... | collective-permute-start | bytes 245768 | tf_op jit(solution)/shard_map/ppermute | solution.py:31
  31.0 4.3 %shard_map.87 = (bf16[1,640,512]{2,1,0:T(8,128)(2,1)S(1)}, bf16[1,640,512]{2,1,0:T(8,128)(2,1)S(1)}, bf16[1,640,512]{2,1,0:T(8,128)(2,1)}) custom-call(s32[32]{0:T(128)S(1)} %concatenate.9.order, bf16[512,5120]{1,0:T(8,128)(2,1)} %tokens.2, bf16[512,512]{1,0:T(8,128)(2,1)} %key_grad.5), custom_call_target="tpu_custom_call" | custom-call | flops 1006632960 | bytes 3932160 | tf_op jit(solution)/shard_map/pallas_call | solution.py:83
  35.3 0.0 collective-permute-done.5.got
  35.3 0.6 shard_map.88
  35.9 0.2 copy-done.2
  36.1 0.0 collective-permute-done.21
  36.1 0.2 add.188
  36.3 0.3 collective-permute-start.22
  36.6 0.4 collective-permute-start.7
  36.9 2.5 %collective-permute-start.6 = (bf16[160,256]{1,0:T(8,128)(2,1)S(1)}, bf16[160,256]{1,0:T(8,128)(2,1)S(1)}, u32[]{:S(2)}, u32[]{:S(2)}) collective-permute-start(bf16[160,256]{1,0:T(8,128)(2,1)S(1)} %get-tuple-element.59), channel_id=1, source_target_pairs={{0,33},{1,32},{2,35},{3,34},{4,37},{5,36},{6,39},{7,38},{8,41},{9,... | collective-permute-start | bytes 245768 | tf_op jit(solution)/shard_map/ppermute | solution.py:31
  39.5 3.3 %collective-permute-done.6 = bf16[160,256]{1,0:T(8,128)(2,1)S(1)} collective-permute-done((bf16[160,256]{1,0:T(8,128)(2,1)S(1)}, bf16[160,256]{1,0:T(8,128)(2,1)S(1)}, u32[]{:S(2)}, u32[]{:S(2)}) %collective-permute-start.6) | collective-permute-done | bytes 81952 | tf_op jit(solution)/shard_map/ppermute | solution.py:31
  42.7 0.0 collective-permute-done.7
  42.8 0.0 collective-permute-done.9
  42.8 0.0 copy-start.6
  42.8 2.8 %collective-permute-start.10 = (f32[2,160,256]{2,1,0:T(8,128)S(1)}, f32[2,160,256]{2,1,0:T(8,128)S(1)}, u32[]{:S(2)}, u32[]{:S(2)}) collective-permute-start(f32[2,160,256]{2,1,0:T(8,128)S(1)} %shard_map.90.refs_0_), channel_id=1, source_target_pairs={{0,32},{1,33},{2,34},{3,35},{4,36},{5,37},{6,38},{7,39},{8,40},{9,... | collective-permute-start | bytes 983048 | tf_op jit(solution)/shard_map/ppermute | solution.py:31
  45.6 1.1 %collective-permute-start.11 = (bf16[2,160,256]{2,1,0:T(8,128)(2,1)S(1)}, bf16[2,160,256]{2,1,0:T(8,128)(2,1)S(1)}, u32[]{:S(2)}, u32[]{:S(2)}) collective-permute-start(bf16[2,160,256]{2,1,0:T(8,128)(2,1)S(1)} %shard_map.89.refs_0_), channel_id=1, source_target_pairs={{0,2},{1,3},{2,4},{3,5},{4,6},{5,7},{6,0},{7,1},{8,10},{9,11},{10,... | collective-permute-start | bytes 491528 | tf_op jit(solution)/shard_map/ppermute | solution.py:31
  46.7 1.7 %collective-permute-start.12 = (bf16[2,160,256]{2,1,0:T(8,128)(2,1)S(1)}, bf16[2,160,256]{2,1,0:T(8,128)(2,1)S(1)}, u32[]{:S(2)}, u32[]{:S(2)}) collective-permute-start(bf16[2,160,256]{2,1,0:T(8,128)(2,1)S(1)} %shard_map.89.refs_0_), channel_id=1, source_target_pairs={{0,4},{1,5},{2,6},{3,7},{4,0},{5,1},{6,2},{7,3},{8,12},{9,13},{10,... | collective-permute-start | bytes 491528 | tf_op jit(solution)/shard_map/ppermute | solution.py:31
  48.4 0.8 collective-permute-start.13
  49.2 1.7 %collective-permute-done.10.refs_1_ = f32[2,160,256]{2,1,0:T(8,128)S(1)} collective-permute-done((f32[2,160,256]{2,1,0:T(8,128)S(1)}, f32[2,160,256]{2,1,0:T(8,128)S(1)}, u32[]{:S(2)}, u32[]{:S(2)}) %collective-permute-start.10) | collective-permute-done | bytes 327712 | tf_op jit(solution)/shard_map/ppermute | solution.py:31
  51.0 3.9 %collective-permute-start.17 = (f32[4,160,256]{2,1,0:T(8,128)S(1)}, f32[4,160,256]{2,1,0:T(8,128)}, u32[]{:S(2)}, u32[]{:S(2)}) collective-permute-start(f32[4,160,256]{2,1,0:T(8,128)S(1)} %shard_map.92.average), channel_id=1, source_target_pairs={{0,8},{1,9},{2,10},{3,11},{4,12},{5,13},{6,14},{7,15},{8,0},{9,1},... | collective-permute-start | bytes 1966088 | tf_op jit(solution)/shard_map/ppermute | solution.py:31
  54.8 0.0 collective-permute-done.11.refs_1_
  54.8 0.0 collective-permute-done.12.refs_2_
  54.8 0.0 collective-permute-done.13.refs_3_
  54.8 0.9 shard_map.91.w0
  55.7 2.2 %collective-permute-start.19 = (bf16[1,640,512]{2,1,0:T(8,128)(2,1)}, bf16[1,640,512]{2,1,0:T(8,128)(2,1)}, u32[]{:S(2)}, u32[]{:S(2)}) collective-permute-start(bf16[1,640,512]{2,1,0:T(8,128)(2,1)} %get-tuple-element.85), channel_id=1, source_target_pairs={{0,2},{1,3},{2,4},{3,5},{4,6},{5,7},{6,0},{7,1},{8,14},{9,15},{10,... | collective-permute-start | bytes 1966088 | tf_op jit(solution)/shard_map/ppermute | solution.py:31
  57.9 1.0 %collective-permute-start.14 = (bf16[8,160,256]{2,1,0:T(8,128)(2,1)}, bf16[8,160,256]{2,1,0:T(8,128)(2,1)}, u32[]{:S(2)}, u32[]{:S(2)}) collective-permute-start(bf16[8,160,256]{2,1,0:T(8,128)(2,1)} %shard_map.91.w0), channel_id=1, source_target_pairs={{0,16},{1,17},{2,18},{3,19},{4,20},{5,21},{6,22},{7,23},{8,24},{9,... | collective-permute-start | bytes 1966088 | tf_op jit(solution)/shard_map/ppermute | solution.py:31
  58.9 4.9 %collective-permute-start.15 = (bf16[8,160,256]{2,1,0:T(8,128)(2,1)}, bf16[8,160,256]{2,1,0:T(8,128)(2,1)}, u32[]{:S(2)}, u32[]{:S(2)}) collective-permute-start(bf16[8,160,256]{2,1,0:T(8,128)(2,1)} %shard_map.91.w0), channel_id=1, source_target_pairs={{0,193},{1,64},{2,195},{3,66},{4,197},{5,68},{6,199},{7,70},{8,201... | collective-permute-start | bytes 1966088 | tf_op jit(solution)/shard_map/ppermute | solution.py:31
  63.8 0.0 collective-permute-done.22
  63.8 1.6 %collective-permute-start.16 = (bf16[8,160,256]{2,1,0:T(8,128)(2,1)}, bf16[8,160,256]{2,1,0:T(8,128)(2,1)}, u32[]{:S(2)}, u32[]{:S(2)}) collective-permute-start(bf16[8,160,256]{2,1,0:T(8,128)(2,1)} %shard_map.91.w0), channel_id=1, source_target_pairs={{0,48},{1,49},{2,50},{3,51},{4,52},{5,53},{6,54},{7,55},{8,56},{9,... | collective-permute-start | bytes 1966088 | tf_op jit(solution)/shard_map/ppermute | solution.py:31
  65.4 4.2 %shard_map.94 = (bf16[512,5120]{1,0:T(8,128)(2,1)S(1)}, bf16[512,5120]{1,0:T(8,128)(2,1)S(1)}) custom-call(bf16[512,5120]{1,0:T(8,128)(2,1)} %tokens.2, bf16[512,5120]{1,0:T(8,128)(2,1)} %copy-done.5), custom_call_target="tpu_custom_call" | custom-call | tf_op jit(solution)/shard_map/pallas_call | solution.py:220
  69.6 0.3 copy-done.7
  70.0 1.4 %fusion.1 = bf16[640,512]{1,0:T(8,128)(2,1)S(1)} fusion(bf16[1,640,512]{2,1,0:T(8,128)(2,1)} %collective-permute-done.22, bf16[1,640,512]{2,1,0:T(8,128)(2,1)S(1)} %copy-done.3, bf16[2,640,512]{2,1,0:T(8,128)(2,1)S(1)} %copy-done.7), kind=kLoop, calls=%fused_computation.3 | loop fusion | flops 1966080 | bytes 2621440 | tf_op jit(solution)/shard_map/convert_element_type | solution.py:315
  71.3 0.1 collective-permute-start.23
  71.4 2.9 %shard_map.96 = (bf16[1,640,512]{2,1,0:T(8,128)(2,1)S(1)}, bf16[1,640,512]{2,1,0:T(8,128)(2,1)S(1)}) custom-call(s32[32]{0:T(128)S(1)} %concatenate.9.order, bf16[512,5120]{1,0:T(8,128)(2,1)} %tokens.2, bf16[512,512]{1,0:T(8,128)(2,1)} %key_grad.5), custom_call_target="tpu_custom_call" | custom-call | flops 671088640 | bytes 2621440 | tf_op jit(solution)/shard_map/pallas_call | solution.py:83
  74.3 0.0 collective-permute-done.19
  74.4 1.3 %add.184 = bf16[1,640,512]{2,1,0:T(8,128)(2,1)S(1)} add(bf16[1,640,512]{2,1,0:T(8,128)(2,1)S(1)} %get-tuple-element.84, bf16[1,640,512]{2,1,0:T(8,128)(2,1)} %collective-permute-done.19) | non-fusion elementwise | flops 327680 | bytes 1966080 | tf_op jit(solution)/shard_map/add | solution.py:318
  75.6 0.2 collective-permute-start.20
  75.8 4.3 %shard_map.93 = (f32[640,512]{1,0:T(8,128)}, f32[640,512]{1,0:T(8,128)}) custom-call(s32[32]{0:T(128)S(1)} %concatenate.9.order, f32[4,160,256]{2,1,0:T(8,128)S(1)} %shard_map.92.average, f32[4,160,256]{2,1,0:T(8,128)} %collective-permute-done.17.average_other, f32[640,512]{1,0:T(8,128)S(1)} %copy-done, f32[640,512]{1,0:T(8,128)S(1)} %copy-done.1), custom_call_target="tpu_custom_call" | custom-call | tf_op jit(solution)/shard_map/pallas_call | solution.py:195
  80.0 0.0 collective-permute-done.14.w1
  80.1 4.7 %shard_map.95 = (bf16[512,256]{1,0:T(8,128)(2,1)S(1)}, bf16[512,256]{1,0:T(8,128)(2,1)S(1)}) custom-call(s32[32]{0:T(128)S(1)} %concatenate.9.order, bf16[512,5120]{1,0:T(8,128)(2,1)S(1)} %get-tuple-element.73.tokens, bf16[512,5120]{1,0:T(8,128)(2,1)S(1)} %get-tuple-element.74.tokens_other, bf16[8,160,256]{2,1,0:T(8,128)(2,1)} %shard_map.91.w0, ...), custom_call_target="tpu_custom_call" | custom-call | flops 26843545600 | bytes 14680064 | tf_op jit(solution)/shard_map/pallas_call | solution.py:243
  84.8 3.6 %collective-permute-start.18 = (bf16[512,256]{1,0:T(8,128)(2,1)S(1)}, bf16[512,256]{1,0:T(8,128)(2,1)S(1)}, u32[]{:S(2)}, u32[]{:S(2)}) collective-permute-start(bf16[512,256]{1,0:T(8,128)(2,1)S(1)} %get-tuple-element.80), channel_id=1, source_target_pairs={{0,8},{1,9},{2,10},{3,11},{4,12},{5,13},{6,14},{7,15},{8,0},{9,1},... | collective-permute-start | bytes 786440 | tf_op jit(solution)/shard_map/ppermute | solution.py:31
  88.4 0.0 collective-permute-done.23
  88.4 1.2 %fusion.2 = bf16[1,640,512]{2,1,0:T(8,128)(2,1)} fusion(bf16[640,512]{1,0:T(8,128)(2,1)S(1)} %collective-permute-done.23, bf16[1,640,512]{2,1,0:T(8,128)(2,1)S(1)} %collective-permute-done.20, bf16[1,640,512]{2,1,0:T(8,128)(2,1)S(1)} %get-tuple-element.82, bf16[2,640,512]{2,1,0:T(8,128)(2,1)S(1)} %copy-done.7), kind=kLoop, calls=%fused_computation.4 | loop fusion | flops 2621440 | bytes 3276800 | tf_op jit(solution)/shard_map/broadcast_in_dim | solution.py:323
  89.6 0.9 %maximum_select_fusion = bf16[512,512]{1,0:T(8,128)(2,1)} fusion(bf16[512,256]{1,0:T(8,128)(2,1)S(1)} %collective-permute-done.18, bf16[512,256]{1,0:T(8,128)(2,1)S(1)} %get-tuple-element.79, pred[]{:T(512)S(6)} %eq.21), kind=kLoop, calls=%fused_computation.5 | loop fusion | flops 2359296 | bytes 1048577 | tf_op jit(solution)/shard_map/jit(_where)/select_n | solution.py:328
  (27 shorter events, 0.2 us)
Async XLA Ops:
  0.6 5.3 %collective-permute-start = (bf16[640,512]{1,0:T(8,128)(2,1)}, bf16[640,512]{1,0:T(8,128)(2,1)S(1)}, u32[]{:S(2)}, u32[]{:S(2)}) collective-permute-start(bf16[640,512]{1,0:T(8,128)(2,1)} %bitcast.19), channel_id=1, source_target_pairs={{0,8},{1,9},{2,10},{3,11},{4,12},{5,13},{6,14},{7,15},{8,0},{9,1},... | collective-permute-start | bytes 1966088 | tf_op jit(solution)/shard_map/ppermute | solution.py:31
  6.6 6.9 %collective-permute-start.1 = (bf16[160,256]{1,0:T(8,128)(2,1)S(1)}, bf16[160,256]{1,0:T(8,128)(2,1)S(1)}, u32[]{:S(2)}, u32[]{:S(2)}) collective-permute-start(bf16[160,256]{1,0:T(8,128)(2,1)S(1)} %get-tuple-element.50), channel_id=1, source_target_pairs={{0,16},{1,17},{2,18},{3,19},{4,20},{5,21},{6,22},{7,23},{8,24},{9,... | collective-permute-start | bytes 245768 | tf_op jit(solution)/shard_map/ppermute | solution.py:31
  6.6 6.8 %collective-permute-start.2 = (bf16[160,256]{1,0:T(8,128)(2,1)S(1)}, bf16[160,256]{1,0:T(8,128)(2,1)S(1)}, u32[]{:S(2)}, u32[]{:S(2)}) collective-permute-start(bf16[160,256]{1,0:T(8,128)(2,1)S(1)} %get-tuple-element.54), channel_id=1, source_target_pairs={{0,32},{1,33},{2,34},{3,35},{4,36},{5,37},{6,38},{7,39},{8,40},{9,... | collective-permute-start | bytes 245768 | tf_op jit(solution)/shard_map/ppermute | solution.py:31
  8.6 5.0 %copy-start.4 = (bf16[512,5120]{1,0:T(8,128)(2,1)S(1)}, bf16[512,5120]{1,0:T(8,128)(2,1)}, u32[]{:S(2)}) copy-start(bf16[512,5120]{1,0:T(8,128)(2,1)} %tokens.2) | copy-start | bytes 15728644
  8.6 5.0 %collective-permute-start.3 = (bf16[160,256]{1,0:T(8,128)(2,1)S(1)}, bf16[160,256]{1,0:T(8,128)(2,1)S(1)}, u32[]{:S(2)}, u32[]{:S(2)}) collective-permute-start(bf16[160,256]{1,0:T(8,128)(2,1)S(1)} %get-tuple-element.55), channel_id=1, source_target_pairs={{0,48},{1,49},{2,50},{3,51},{4,52},{5,53},{6,54},{7,55},{8,56},{9,... | collective-permute-start | bytes 245768 | tf_op jit(solution)/shard_map/ppermute | solution.py:31
  13.6 29.2 %collective-permute-start.8 = (bf16[512,5120]{1,0:T(8,128)(2,1)S(1)}, bf16[512,5120]{1,0:T(8,128)(2,1)S(1)}, u32[]{:S(2)}, u32[]{:S(2)}) collective-permute-start(bf16[512,5120]{1,0:T(8,128)(2,1)S(1)} %copy-done.4), channel_id=1, source_target_pairs={{0,8},{1,9},{2,10},{3,11},{4,12},{5,13},{6,14},{7,15},{8,0},{9,1},... | collective-permute-start | bytes 15728648 | tf_op jit(solution)/shard_map/ppermute | solution.py:31
  15.2 27.6 %collective-permute-start.9 = (bf16[2,640,512]{2,1,0:T(8,128)(2,1)S(1)}, bf16[2,640,512]{2,1,0:T(8,128)(2,1)S(1)}, u32[]{:S(2)}, u32[]{:S(2)}) collective-permute-start(bf16[2,640,512]{2,1,0:T(8,128)(2,1)S(1)} %get-tuple-element.63), channel_id=1, source_target_pairs={{0,6},{1,7},{2,0},{3,1},{4,2},{5,3},{6,4},{7,5},{8,10},{9,11},{10,... | collective-permute-start | bytes 3932168 | tf_op jit(solution)/shard_map/ppermute | solution.py:31
  15.8 20.2 %collective-permute-start.21 = (bf16[1,640,512]{2,1,0:T(8,128)(2,1)S(1)}, bf16[1,640,512]{2,1,0:T(8,128)(2,1)S(1)}, u32[]{:S(2)}, u32[]{:S(2)}) collective-permute-start(bf16[1,640,512]{2,1,0:T(8,128)(2,1)S(1)} %get-tuple-element.52), channel_id=1, source_target_pairs={{0,2},{1,3},{2,4},{3,5},{4,6},{5,7},{6,0},{7,1},{8,14},{9,15},{10,... | collective-permute-start | bytes 1966088 | tf_op jit(solution)/shard_map/ppermute | solution.py:31
  17.9 5.0 %collective-permute-start.4 = (bf16[160,256]{1,0:T(8,128)(2,1)S(1)}, bf16[160,256]{1,0:T(8,128)(2,1)S(1)}, u32[]{:S(2)}, u32[]{:S(2)}) collective-permute-start(bf16[160,256]{1,0:T(8,128)(2,1)S(1)} %fusion.3), channel_id=1, source_target_pairs={{0,64},{1,65},{2,66},{3,67},{4,68},{5,69},{6,70},{7,71},{8,72},{9,... | collective-permute-start | bytes 245768 | tf_op jit(solution)/shard_map/ppermute | solution.py:31
  22.9 12.4 %copy-start = (f32[640,512]{1,0:T(8,128)S(1)}, f32[640,512]{1,0:T(8,128)}, u32[]{:S(2)}) copy-start(f32[640,512]{1,0:T(8,128)} %g.5) | copy-start | bytes 3932164
  22.9 12.4 %copy-start.1 = (f32[640,512]{1,0:T(8,128)S(1)}, f32[640,512]{1,0:T(8,128)}, u32[]{:S(2)}) copy-start(f32[640,512]{1,0:T(8,128)} %m.3) | copy-start | bytes 3932164
  22.9 12.4 %collective-permute-start.5 = (bf16[160,256]{1,0:T(8,128)(2,1)S(1)}, bf16[160,256]{1,0:T(8,128)(2,1)S(1)}, u32[]{:S(2)}, u32[]{:S(2)}) collective-permute-start(bf16[160,256]{1,0:T(8,128)(2,1)S(1)} %get-tuple-element.91), channel_id=1, source_target_pairs={{0,128},{1,129},{2,130},{3,131},{4,132},{5,133},{6,134},{7,135},{8... | collective-permute-start | bytes 245768 | tf_op jit(solution)/shard_map/ppermute | solution.py:31
  35.2 0.8 copy-start.2
  36.3 27.5 %collective-permute-start.22 = (bf16[1,640,512]{2,1,0:T(8,128)(2,1)S(1)}, bf16[1,640,512]{2,1,0:T(8,128)(2,1)}, u32[]{:S(2)}, u32[]{:S(2)}) collective-permute-start(bf16[1,640,512]{2,1,0:T(8,128)(2,1)S(1)} %add.188), channel_id=1, source_target_pairs={{0,2},{1,3},{2,4},{3,5},{4,6},{5,7},{6,0},{7,1},{8,14},{9,15},{10,... | collective-permute-start | bytes 1966088 | tf_op jit(solution)/shard_map/ppermute | solution.py:31
  36.6 6.2 %collective-permute-start.7 = (f32[160,256]{1,0:T(8,128)S(1)}, f32[160,256]{1,0:T(8,128)S(1)}, u32[]{:S(2)}, u32[]{:S(2)}) collective-permute-start(f32[160,256]{1,0:T(8,128)S(1)} %get-tuple-element.60), channel_id=1, source_target_pairs={{0,16},{1,17},{2,18},{3,19},{4,20},{5,21},{6,22},{7,23},{8,24},{9,... | collective-permute-start | bytes 491528 | tf_op jit(solution)/shard_map/ppermute | solution.py:31
  36.9 5.8 %collective-permute-start.6 = (bf16[160,256]{1,0:T(8,128)(2,1)S(1)}, bf16[160,256]{1,0:T(8,128)(2,1)S(1)}, u32[]{:S(2)}, u32[]{:S(2)}) collective-permute-start(bf16[160,256]{1,0:T(8,128)(2,1)S(1)} %get-tuple-element.59), channel_id=1, source_target_pairs={{0,33},{1,32},{2,35},{3,34},{4,37},{5,36},{6,39},{7,38},{8,41},{9,... | collective-permute-start | bytes 245768 | tf_op jit(solution)/shard_map/ppermute | solution.py:31
  42.8 12.9 %copy-start.6 = (bf16[2,640,512]{2,1,0:T(8,128)(2,1)}, bf16[2,640,512]{2,1,0:T(8,128)(2,1)S(1)}, u32[]{:S(2)}) copy-start(bf16[2,640,512]{2,1,0:T(8,128)(2,1)S(1)} %collective-permute-done.9) | copy-start | bytes 3932164
  42.8 12.9 %copy-start.5 = (bf16[512,5120]{1,0:T(8,128)(2,1)}, bf16[512,5120]{1,0:T(8,128)(2,1)S(1)}, u32[]{:S(2)}) copy-start(bf16[512,5120]{1,0:T(8,128)(2,1)S(1)} %collective-permute-done.8.b) | copy-start | bytes 15728644
  42.8 8.1 %collective-permute-start.10 = (f32[2,160,256]{2,1,0:T(8,128)S(1)}, f32[2,160,256]{2,1,0:T(8,128)S(1)}, u32[]{:S(2)}, u32[]{:S(2)}) collective-permute-start(f32[2,160,256]{2,1,0:T(8,128)S(1)} %shard_map.90.refs_0_), channel_id=1, source_target_pairs={{0,32},{1,33},{2,34},{3,35},{4,36},{5,37},{6,38},{7,39},{8,40},{9,... | collective-permute-start | bytes 983048 | tf_op jit(solution)/shard_map/ppermute | solution.py:31
  45.6 9.2 %collective-permute-start.11 = (bf16[2,160,256]{2,1,0:T(8,128)(2,1)S(1)}, bf16[2,160,256]{2,1,0:T(8,128)(2,1)S(1)}, u32[]{:S(2)}, u32[]{:S(2)}) collective-permute-start(bf16[2,160,256]{2,1,0:T(8,128)(2,1)S(1)} %shard_map.89.refs_0_), channel_id=1, source_target_pairs={{0,2},{1,3},{2,4},{3,5},{4,6},{5,7},{6,0},{7,1},{8,10},{9,11},{10,... | collective-permute-start | bytes 491528 | tf_op jit(solution)/shard_map/ppermute | solution.py:31
  46.7 8.1 %collective-permute-start.12 = (bf16[2,160,256]{2,1,0:T(8,128)(2,1)S(1)}, bf16[2,160,256]{2,1,0:T(8,128)(2,1)S(1)}, u32[]{:S(2)}, u32[]{:S(2)}) collective-permute-start(bf16[2,160,256]{2,1,0:T(8,128)(2,1)S(1)} %shard_map.89.refs_0_), channel_id=1, source_target_pairs={{0,4},{1,5},{2,6},{3,7},{4,0},{5,1},{6,2},{7,3},{8,12},{9,13},{10,... | collective-permute-start | bytes 491528 | tf_op jit(solution)/shard_map/ppermute | solution.py:31
  48.4 6.4 %collective-permute-start.13 = (bf16[2,160,256]{2,1,0:T(8,128)(2,1)S(1)}, bf16[2,160,256]{2,1,0:T(8,128)(2,1)S(1)}, u32[]{:S(2)}, u32[]{:S(2)}) collective-permute-start(bf16[2,160,256]{2,1,0:T(8,128)(2,1)S(1)} %shard_map.89.refs_0_), channel_id=1, source_target_pairs={{0,6},{1,7},{2,0},{3,1},{4,2},{5,3},{6,4},{7,5},{8,14},{9,15},{10,... | collective-permute-start | bytes 491528 | tf_op jit(solution)/shard_map/ppermute | solution.py:31
  51.0 20.4 %collective-permute-start.17 = (f32[4,160,256]{2,1,0:T(8,128)S(1)}, f32[4,160,256]{2,1,0:T(8,128)}, u32[]{:S(2)}, u32[]{:S(2)}) collective-permute-start(f32[4,160,256]{2,1,0:T(8,128)S(1)} %shard_map.92.average), channel_id=1, source_target_pairs={{0,8},{1,9},{2,10},{3,11},{4,12},{5,13},{6,14},{7,15},{8,0},{9,1},... | collective-permute-start | bytes 1966088 | tf_op jit(solution)/shard_map/ppermute | solution.py:31
  55.7 18.6 %collective-permute-start.19 = (bf16[1,640,512]{2,1,0:T(8,128)(2,1)}, bf16[1,640,512]{2,1,0:T(8,128)(2,1)}, u32[]{:S(2)}, u32[]{:S(2)}) collective-permute-start(bf16[1,640,512]{2,1,0:T(8,128)(2,1)} %get-tuple-element.85), channel_id=1, source_target_pairs={{0,2},{1,3},{2,4},{3,5},{4,6},{5,7},{6,0},{7,1},{8,14},{9,15},{10,... | collective-permute-start | bytes 1966088 | tf_op jit(solution)/shard_map/ppermute | solution.py:31
  57.9 22.1 %collective-permute-start.14 = (bf16[8,160,256]{2,1,0:T(8,128)(2,1)}, bf16[8,160,256]{2,1,0:T(8,128)(2,1)}, u32[]{:S(2)}, u32[]{:S(2)}) collective-permute-start(bf16[8,160,256]{2,1,0:T(8,128)(2,1)} %shard_map.91.w0), channel_id=1, source_target_pairs={{0,16},{1,17},{2,18},{3,19},{4,20},{5,21},{6,22},{7,23},{8,24},{9,... | collective-permute-start | bytes 1966088 | tf_op jit(solution)/shard_map/ppermute | solution.py:31
  58.9 21.2 %collective-permute-start.15 = (bf16[8,160,256]{2,1,0:T(8,128)(2,1)}, bf16[8,160,256]{2,1,0:T(8,128)(2,1)}, u32[]{:S(2)}, u32[]{:S(2)}) collective-permute-start(bf16[8,160,256]{2,1,0:T(8,128)(2,1)} %shard_map.91.w0), channel_id=1, source_target_pairs={{0,193},{1,64},{2,195},{3,66},{4,197},{5,68},{6,199},{7,70},{8,201... | collective-permute-start | bytes 1966088 | tf_op jit(solution)/shard_map/ppermute | solution.py:31
  63.8 16.3 %collective-permute-start.16 = (bf16[8,160,256]{2,1,0:T(8,128)(2,1)}, bf16[8,160,256]{2,1,0:T(8,128)(2,1)}, u32[]{:S(2)}, u32[]{:S(2)}) collective-permute-start(bf16[8,160,256]{2,1,0:T(8,128)(2,1)} %shard_map.91.w0), channel_id=1, source_target_pairs={{0,48},{1,49},{2,50},{3,51},{4,52},{5,53},{6,54},{7,55},{8,56},{9,... | collective-permute-start | bytes 1966088 | tf_op jit(solution)/shard_map/ppermute | solution.py:31
  65.4 4.2 %copy-start.3 = (bf16[1,640,512]{2,1,0:T(8,128)(2,1)S(1)}, bf16[1,640,512]{2,1,0:T(8,128)(2,1)}, u32[]{:S(2)}) copy-start(bf16[1,640,512]{2,1,0:T(8,128)(2,1)} %copy-done.2) | copy-start | bytes 1966084
  65.4 4.6 %copy-start.7 = (bf16[2,640,512]{2,1,0:T(8,128)(2,1)S(1)}, bf16[2,640,512]{2,1,0:T(8,128)(2,1)}, u32[]{:S(2)}) copy-start(bf16[2,640,512]{2,1,0:T(8,128)(2,1)} %copy-done.6) | copy-start | bytes 3932164
  71.3 17.0 %collective-permute-start.23 = (bf16[640,512]{1,0:T(8,128)(2,1)S(1)}, bf16[640,512]{1,0:T(8,128)(2,1)S(1)}, u32[]{:S(2)}, u32[]{:S(2)}) collective-permute-start(bf16[640,512]{1,0:T(8,128)(2,1)S(1)} %fusion.1), channel_id=1, source_target_pairs={{0,1},{1,0},{2,3},{3,2},{4,5},{5,4},{6,7},{7,6},{8,9},{9,8},{10,11... | collective-permute-start | bytes 1966088 | tf_op jit(solution)/shard_map/ppermute | solution.py:31
  75.6 12.8 %collective-permute-start.20 = (bf16[1,640,512]{2,1,0:T(8,128)(2,1)S(1)}, bf16[1,640,512]{2,1,0:T(8,128)(2,1)S(1)}, u32[]{:S(2)}, u32[]{:S(2)}) collective-permute-start(bf16[1,640,512]{2,1,0:T(8,128)(2,1)S(1)} %add.184), channel_id=1, source_target_pairs={{0,2},{1,3},{2,4},{3,5},{4,6},{5,7},{6,0},{7,1},{8,14},{9,15},{10,... | collective-permute-start | bytes 1966088 | tf_op jit(solution)/shard_map/ppermute | solution.py:31
  84.8 4.8 %collective-permute-start.18 = (bf16[512,256]{1,0:T(8,128)(2,1)S(1)}, bf16[512,256]{1,0:T(8,128)(2,1)S(1)}, u32[]{:S(2)}, u32[]{:S(2)}) collective-permute-start(bf16[512,256]{1,0:T(8,128)(2,1)S(1)} %get-tuple-element.80), channel_id=1, source_target_pairs={{0,8},{1,9},{2,10},{3,11},{4,12},{5,13},{6,14},{7,15},{8,0},{9,1},... | collective-permute-start | bytes 786440 | tf_op jit(solution)/shard_map/ppermute | solution.py:31

commit v6 on v5

--- a/solution.py
+++ b/solution.py
@@ -181,27 +181,30 @@
 
 def update_kernel(order, average, average_other, g, m, new_global, new_momentum):
     mine = order[24] == 0
-    for h in range(2):
-        cols = slice(h * COLS, (h + 1) * COLS)
-        avg = jnp.where(mine == (h == 0), average[0], average_other[0])
-        new_m = momentum_rate * m[:, cols] + avg
-        new_momentum[:, cols] = new_m
-        new_global[:, cols] = g[:, cols] - outer_rate * (avg + momentum_rate * new_m)
+    for j in range(2):
+        at = order[28 + 2 * pl.program_id(0) + j] % 2 * ROWS
+        rows = pl.ds(pl.multiple_of(at, ROWS), ROWS)
+        for h in range(2):
+            cols = slice(h * COLS, (h + 1) * COLS)
+            avg = jnp.where(mine == (h == 0), average[j], average_other[j])
+            new_m = momentum_rate * m[rows, cols] + avg
+            new_momentum[rows, cols] = new_m
+            new_global[rows, cols] = g[rows, cols] - outer_rate * (avg + momentum_rate * new_m)
 
 
 def update(order, average, average_other, g, m):
-    block = pl.BlockSpec((ROWS, KW), lambda s, o: (o[28 + s], 0))
-    part = pl.BlockSpec((1, ROWS, COLS), lambda s, o: (s, 0, 0))
+    block = pl.BlockSpec((2 * ROWS, KW), lambda s, o: (o[28 + 2 * s] // 2, 0))
+    part = pl.BlockSpec((2, ROWS, COLS), lambda s, o: (s, 0, 0))
     return pl.pallas_call(
         update_kernel,
         grid_spec=pltpu.PrefetchScalarGridSpec(
             num_scalar_prefetch=1,
-            grid=(4,),
+            grid=(2,),
             in_specs=[part, part, block, block],
             out_specs=[block] * 2,
         ),
         out_shape=[jax.ShapeDtypeStruct((SHARD, KW), F32)] * 2,
-        compiler_params=grant(8),
+        compiler_params=grant(10),
     )(order, average, average_other, g, m)
 
 

time: 90.9 us -> 90.7 us (level)
  Pallas kernels: 27.8 us -> 26.8 us
    pallas_call x1, Pallas kernels: 4.25 us -> 3.22 us  [update(): pl.pallas_call(update_kernel, grid_spec=pltpu.PrefetchScalarGridSpec(num_...]
  transfers between devices with their start and end apart: 24 -> 24, of which waited for: 5 -> 6; matrix products, arithmetic and copies ran while one was open for 5% -> 5% of each run, Pallas kernels for 30% -> 29%
where the time goes in v6:
time: 90.7 us; the launch traced here: 89.5 us
  starting transfers between devices  47.7 us (53%)
  Pallas kernels  26.8 us (30%)
  waiting for transfers between devices  8.39 us (9%)
  other arithmetic  5.08 us (6%)
  between operations  0.91 us (1%)
    ppermute x24, starting transfers between devices, send(): return lax.ppermute(value, AXES, pairs)  47.7 us
    pallas_call x3, Pallas kernels, grad_parts(): pl.pallas_call(functools.partial(grad_kernel, at, sizes), in_specs=[pl.Bl...  10.6 us
    ppermute x24, waiting for transfers between devices, send(): return lax.ppermute(value, AXES, pairs)  8.39 us
    pallas_call x1, Pallas kernels, keys_of(): pl.pallas_call(keys_kernel, in_specs=[pl.BlockSpec(memory_space=pltpu.SME...  4.72 us
    pallas_call x1, Pallas kernels, hold(): pl.pallas_call(hold_kernel, in_specs=[pl.BlockSpec(memory_space=pltpu.HBM...  4.23 us
    pallas_call x1, Pallas kernels, update(): pl.pallas_call(update_kernel, grid_spec=pltpu.PrefetchScalarGridSpec(num_...  3.22 us
  transfers between devices with their start and end apart: 24, of which 6 were waited for; matrix products, arithmetic and copies ran while one was open for 5% of the time, Pallas kernels for 29%

profile of v6, /device:TPU:1, one launch (start us, length us, event | category | flops | bytes accessed | tf_op | source)
XLA Modules:
  0.0 89.5 jit_solution(6466675797030042690)
XLA Ops:
  0.6 3.3 %collective-permute-start = (bf16[640,512]{1,0:T(8,128)(2,1)}, bf16[640,512]{1,0:T(8,128)(2,1)S(1)}, u32[]{:S(2)}, u32[]{:S(2)}) collective-permute-start(bf16[640,512]{1,0:T(8,128)(2,1)} %bitcast.19), channel_id=1, source_target_pairs={{0,8},{1,9},{2,10},{3,11},{4,12},{5,13},{6,14},{7,15},{8,0},{9,1},... | collective-permute-start | bytes 1966088 | tf_op jit(solution)/shard_map/ppermute | solution.py:31
  4.0 0.1 concatenate.9.order
  4.1 1.8 %shard_map.84.base = f32[640,256]{1,0:T(8,128)S(1)} custom-call(s32[32]{0:T(128)S(1)} %concatenate.9.order, f32[640,512]{1,0:T(8,128)} %g.5, bf16[640,512]{1,0:T(8,128)(2,1)} %bitcast.20), custom_call_target="tpu_custom_call" | custom-call | tf_op jit(solution)/shard_map/pallas_call | solution.py:106
  5.9 0.6 shard_map.85
  6.6 0.1 collective-permute-start.1
  6.6 1.9 %collective-permute-start.2 = (bf16[160,256]{1,0:T(8,128)(2,1)S(1)}, bf16[160,256]{1,0:T(8,128)(2,1)S(1)}, u32[]{:S(2)}, u32[]{:S(2)}) collective-permute-start(bf16[160,256]{1,0:T(8,128)(2,1)S(1)} %get-tuple-element.54), channel_id=1, source_target_pairs={{0,32},{1,33},{2,34},{3,35},{4,36},{5,37},{6,38},{7,39},{8,40},{9,... | collective-permute-start | bytes 245768 | tf_op jit(solution)/shard_map/ppermute | solution.py:31
  8.6 1.2 %collective-permute-start.3 = (bf16[160,256]{1,0:T(8,128)(2,1)S(1)}, bf16[160,256]{1,0:T(8,128)(2,1)S(1)}, u32[]{:S(2)}, u32[]{:S(2)}) collective-permute-start(bf16[160,256]{1,0:T(8,128)(2,1)S(1)} %get-tuple-element.55), channel_id=1, source_target_pairs={{0,48},{1,49},{2,50},{3,51},{4,52},{5,53},{6,54},{7,55},{8,56},{9,... | collective-permute-start | bytes 245768 | tf_op jit(solution)/shard_map/ppermute | solution.py:31
  9.7 3.4 %shard_map.86 = (bf16[1,640,512]{2,1,0:T(8,128)(2,1)S(1)}, bf16[2,640,512]{2,1,0:T(8,128)(2,1)S(1)}) custom-call(s32[32]{0:T(128)S(1)} %concatenate.9.order, bf16[512,5120]{1,0:T(8,128)(2,1)} %tokens.2, bf16[512,512]{1,0:T(8,128)(2,1)} %key_grad.5), custom_call_target="tpu_custom_call" | custom-call | flops 1006632960 | bytes 3932160 | tf_op jit(solution)/shard_map/pallas_call | solution.py:83
  13.2 0.3 collective-permute-done.1
  13.5 0.0 collective-permute-done.2
  13.5 0.1 collective-permute-done.3
  13.6 1.6 %collective-permute-start.8 = (bf16[512,5120]{1,0:T(8,128)(2,1)S(1)}, bf16[512,5120]{1,0:T(8,128)(2,1)S(1)}, u32[]{:S(2)}, u32[]{:S(2)}) collective-permute-start(bf16[512,5120]{1,0:T(8,128)(2,1)S(1)} %copy-done.4), channel_id=1, source_target_pairs={{0,8},{1,9},{2,10},{3,11},{4,12},{5,13},{6,14},{7,15},{8,0},{9,1},... | collective-permute-start | bytes 15728648 | tf_op jit(solution)/shard_map/ppermute | solution.py:31
  15.2 0.7 collective-permute-start.9
  15.8 2.0 %collective-permute-start.21 = (bf16[1,640,512]{2,1,0:T(8,128)(2,1)S(1)}, bf16[1,640,512]{2,1,0:T(8,128)(2,1)S(1)}, u32[]{:S(2)}, u32[]{:S(2)}) collective-permute-start(bf16[1,640,512]{2,1,0:T(8,128)(2,1)S(1)} %get-tuple-element.52), channel_id=1, source_target_pairs={{0,2},{1,3},{2,4},{3,5},{4,6},{5,7},{6,0},{7,1},{8,14},{9,15},{10,... | collective-permute-start | bytes 1966088 | tf_op jit(solution)/shard_map/ppermute | solution.py:31
  17.9 2.4 %collective-permute-start.4 = (bf16[160,256]{1,0:T(8,128)(2,1)S(1)}, bf16[160,256]{1,0:T(8,128)(2,1)S(1)}, u32[]{:S(2)}, u32[]{:S(2)}) collective-permute-start(bf16[160,256]{1,0:T(8,128)(2,1)S(1)} %fusion.3), channel_id=1, source_target_pairs={{0,64},{1,65},{2,66},{3,67},{4,68},{5,69},{6,70},{7,71},{8,72},{9,... | collective-permute-start | bytes 245768 | tf_op jit(solution)/shard_map/ppermute | solution.py:31
  20.3 2.5 %collective-permute-done.4 = bf16[160,256]{1,0:T(8,128)(2,1)S(1)} collective-permute-done((bf16[160,256]{1,0:T(8,128)(2,1)S(1)}, bf16[160,256]{1,0:T(8,128)(2,1)S(1)}, u32[]{:S(2)}, u32[]{:S(2)}) %collective-permute-start.4) | collective-permute-done | bytes 81952 | tf_op jit(solution)/shard_map/ppermute | solution.py:31
  22.8 0.1 fusion.9
  22.9 0.0 copy-start
  22.9 0.0 copy-start.1
  22.9 8.1 %collective-permute-start.5 = (bf16[160,256]{1,0:T(8,128)(2,1)S(1)}, bf16[160,256]{1,0:T(8,128)(2,1)S(1)}, u32[]{:S(2)}, u32[]{:S(2)}) collective-permute-start(bf16[160,256]{1,0:T(8,128)(2,1)S(1)} %get-tuple-element.91), channel_id=1, source_target_pairs={{0,128},{1,129},{2,130},{3,131},{4,132},{5,133},{6,134},{7,135},{8... | collective-permute-start | bytes 245768 | tf_op jit(solution)/shard_map/ppermute | solution.py:31
  31.0 4.3 %shard_map.87 = (bf16[1,640,512]{2,1,0:T(8,128)(2,1)S(1)}, bf16[1,640,512]{2,1,0:T(8,128)(2,1)S(1)}, bf16[1,640,512]{2,1,0:T(8,128)(2,1)}) custom-call(s32[32]{0:T(128)S(1)} %concatenate.9.order, bf16[512,5120]{1,0:T(8,128)(2,1)} %tokens.2, bf16[512,512]{1,0:T(8,128)(2,1)} %key_grad.5), custom_call_target="tpu_custom_call" | custom-call | flops 1006632960 | bytes 3932160 | tf_op jit(solution)/shard_map/pallas_call | solution.py:83
  35.3 0.0 collective-permute-done.5.got
  35.3 0.6 shard_map.88
  35.9 0.2 copy-done.2
  36.1 0.0 collective-permute-done.21
  36.1 0.2 add.188
  36.3 0.3 collective-permute-start.22
  36.6 0.4 collective-permute-start.7
  36.9 2.5 %collective-permute-start.6 = (bf16[160,256]{1,0:T(8,128)(2,1)S(1)}, bf16[160,256]{1,0:T(8,128)(2,1)S(1)}, u32[]{:S(2)}, u32[]{:S(2)}) collective-permute-start(bf16[160,256]{1,0:T(8,128)(2,1)S(1)} %get-tuple-element.59), channel_id=1, source_target_pairs={{0,33},{1,32},{2,35},{3,34},{4,37},{5,36},{6,39},{7,38},{8,41},{9,... | collective-permute-start | bytes 245768 | tf_op jit(solution)/shard_map/ppermute | solution.py:31
  39.5 3.3 %collective-permute-done.6 = bf16[160,256]{1,0:T(8,128)(2,1)S(1)} collective-permute-done((bf16[160,256]{1,0:T(8,128)(2,1)S(1)}, bf16[160,256]{1,0:T(8,128)(2,1)S(1)}, u32[]{:S(2)}, u32[]{:S(2)}) %collective-permute-start.6) | collective-permute-done | bytes 81952 | tf_op jit(solution)/shard_map/ppermute | solution.py:31
  42.8 0.0 copy-start.6
  42.8 0.0 collective-permute-done.8.b
  42.8 2.8 %collective-permute-start.10 = (f32[2,160,256]{2,1,0:T(8,128)S(1)}, f32[2,160,256]{2,1,0:T(8,128)S(1)}, u32[]{:S(2)}, u32[]{:S(2)}) collective-permute-start(f32[2,160,256]{2,1,0:T(8,128)S(1)} %shard_map.90.refs_0_), channel_id=1, source_target_pairs={{0,32},{1,33},{2,34},{3,35},{4,36},{5,37},{6,38},{7,39},{8,40},{9,... | collective-permute-start | bytes 983048 | tf_op jit(solution)/shard_map/ppermute | solution.py:31
  45.6 1.1 %collective-permute-start.11 = (bf16[2,160,256]{2,1,0:T(8,128)(2,1)S(1)}, bf16[2,160,256]{2,1,0:T(8,128)(2,1)S(1)}, u32[]{:S(2)}, u32[]{:S(2)}) collective-permute-start(bf16[2,160,256]{2,1,0:T(8,128)(2,1)S(1)} %shard_map.89.refs_0_), channel_id=1, source_target_pairs={{0,2},{1,3},{2,4},{3,5},{4,6},{5,7},{6,0},{7,1},{8,10},{9,11},{10,... | collective-permute-start | bytes 491528 | tf_op jit(solution)/shard_map/ppermute | solution.py:31
  46.7 1.7 %collective-permute-start.12 = (bf16[2,160,256]{2,1,0:T(8,128)(2,1)S(1)}, bf16[2,160,256]{2,1,0:T(8,128)(2,1)S(1)}, u32[]{:S(2)}, u32[]{:S(2)}) collective-permute-start(bf16[2,160,256]{2,1,0:T(8,128)(2,1)S(1)} %shard_map.89.refs_0_), channel_id=1, source_target_pairs={{0,4},{1,5},{2,6},{3,7},{4,0},{5,1},{6,2},{7,3},{8,12},{9,13},{10,... | collective-permute-start | bytes 491528 | tf_op jit(solution)/shard_map/ppermute | solution.py:31
  48.4 0.8 collective-permute-start.13
  49.2 1.7 %collective-permute-done.10.refs_1_ = f32[2,160,256]{2,1,0:T(8,128)S(1)} collective-permute-done((f32[2,160,256]{2,1,0:T(8,128)S(1)}, f32[2,160,256]{2,1,0:T(8,128)S(1)}, u32[]{:S(2)}, u32[]{:S(2)}) %collective-permute-start.10) | collective-permute-done | bytes 327712 | tf_op jit(solution)/shard_map/ppermute | solution.py:31
  51.0 3.9 %collective-permute-start.17 = (f32[4,160,256]{2,1,0:T(8,128)S(1)}, f32[4,160,256]{2,1,0:T(8,128)}, u32[]{:S(2)}, u32[]{:S(2)}) collective-permute-start(f32[4,160,256]{2,1,0:T(8,128)S(1)} %shard_map.92.average), channel_id=1, source_target_pairs={{0,8},{1,9},{2,10},{3,11},{4,12},{5,13},{6,14},{7,15},{8,0},{9,1},... | collective-permute-start | bytes 1966088 | tf_op jit(solution)/shard_map/ppermute | solution.py:31
  54.8 0.0 collective-permute-done.11.refs_1_
  54.8 0.0 collective-permute-done.12.refs_2_
  54.8 0.0 collective-permute-done.13.refs_3_
  54.8 0.9 shard_map.91.w0
  55.7 2.2 %collective-permute-start.19 = (bf16[1,640,512]{2,1,0:T(8,128)(2,1)}, bf16[1,640,512]{2,1,0:T(8,128)(2,1)}, u32[]{:S(2)}, u32[]{:S(2)}) collective-permute-start(bf16[1,640,512]{2,1,0:T(8,128)(2,1)} %get-tuple-element.85), channel_id=1, source_target_pairs={{0,2},{1,3},{2,4},{3,5},{4,6},{5,7},{6,0},{7,1},{8,14},{9,15},{10,... | collective-permute-start | bytes 1966088 | tf_op jit(solution)/shard_map/ppermute | solution.py:31
  57.9 1.0 %collective-permute-start.14 = (bf16[8,160,256]{2,1,0:T(8,128)(2,1)}, bf16[8,160,256]{2,1,0:T(8,128)(2,1)}, u32[]{:S(2)}, u32[]{:S(2)}) collective-permute-start(bf16[8,160,256]{2,1,0:T(8,128)(2,1)} %shard_map.91.w0), channel_id=1, source_target_pairs={{0,16},{1,17},{2,18},{3,19},{4,20},{5,21},{6,22},{7,23},{8,24},{9,... | collective-permute-start | bytes 1966088 | tf_op jit(solution)/shard_map/ppermute | solution.py:31
  58.9 4.9 %collective-permute-start.15 = (bf16[8,160,256]{2,1,0:T(8,128)(2,1)}, bf16[8,160,256]{2,1,0:T(8,128)(2,1)}, u32[]{:S(2)}, u32[]{:S(2)}) collective-permute-start(bf16[8,160,256]{2,1,0:T(8,128)(2,1)} %shard_map.91.w0), channel_id=1, source_target_pairs={{0,193},{1,64},{2,195},{3,66},{4,197},{5,68},{6,199},{7,70},{8,201... | collective-permute-start | bytes 1966088 | tf_op jit(solution)/shard_map/ppermute | solution.py:31
  63.8 0.0 collective-permute-done.22
  63.8 1.6 %collective-permute-start.16 = (bf16[8,160,256]{2,1,0:T(8,128)(2,1)}, bf16[8,160,256]{2,1,0:T(8,128)(2,1)}, u32[]{:S(2)}, u32[]{:S(2)}) collective-permute-start(bf16[8,160,256]{2,1,0:T(8,128)(2,1)} %shard_map.91.w0), channel_id=1, source_target_pairs={{0,48},{1,49},{2,50},{3,51},{4,52},{5,53},{6,54},{7,55},{8,56},{9,... | collective-permute-start | bytes 1966088 | tf_op jit(solution)/shard_map/ppermute | solution.py:31
  65.4 4.2 %shard_map.94 = (bf16[512,5120]{1,0:T(8,128)(2,1)S(1)}, bf16[512,5120]{1,0:T(8,128)(2,1)S(1)}) custom-call(bf16[512,5120]{1,0:T(8,128)(2,1)} %tokens.2, bf16[512,5120]{1,0:T(8,128)(2,1)} %copy-done.5), custom_call_target="tpu_custom_call" | custom-call | tf_op jit(solution)/shard_map/pallas_call | solution.py:223
  69.6 0.3 copy-done.7
  70.0 1.4 %fusion.1 = bf16[640,512]{1,0:T(8,128)(2,1)S(1)} fusion(bf16[1,640,512]{2,1,0:T(8,128)(2,1)} %collective-permute-done.22, bf16[1,640,512]{2,1,0:T(8,128)(2,1)S(1)} %copy-done.3, bf16[2,640,512]{2,1,0:T(8,128)(2,1)S(1)} %copy-done.7), kind=kLoop, calls=%fused_computation.3 | loop fusion | flops 1966080 | bytes 2621440 | tf_op jit(solution)/shard_map/convert_element_type | solution.py:318
  71.3 0.1 collective-permute-start.23
  71.4 2.9 %shard_map.96 = (bf16[1,640,512]{2,1,0:T(8,128)(2,1)S(1)}, bf16[1,640,512]{2,1,0:T(8,128)(2,1)S(1)}) custom-call(s32[32]{0:T(128)S(1)} %concatenate.9.order, bf16[512,5120]{1,0:T(8,128)(2,1)} %tokens.2, bf16[512,512]{1,0:T(8,128)(2,1)} %key_grad.5), custom_call_target="tpu_custom_call" | custom-call | flops 671088640 | bytes 2621440 | tf_op jit(solution)/shard_map/pallas_call | solution.py:83
  74.3 0.0 collective-permute-done.19
  74.4 1.3 %add.184 = bf16[1,640,512]{2,1,0:T(8,128)(2,1)S(1)} add(bf16[1,640,512]{2,1,0:T(8,128)(2,1)S(1)} %get-tuple-element.84, bf16[1,640,512]{2,1,0:T(8,128)(2,1)} %collective-permute-done.19) | non-fusion elementwise | flops 327680 | bytes 1966080 | tf_op jit(solution)/shard_map/add | solution.py:321
  75.6 0.2 collective-permute-start.20
  75.8 3.2 %shard_map.93 = (f32[640,512]{1,0:T(8,128)}, f32[640,512]{1,0:T(8,128)}) custom-call(s32[32]{0:T(128)S(1)} %concatenate.9.order, f32[4,160,256]{2,1,0:T(8,128)S(1)} %shard_map.92.average, f32[4,160,256]{2,1,0:T(8,128)} %collective-permute-done.17.average_other, f32[640,512]{1,0:T(8,128)S(1)} %copy-done, f32[640,512]{1,0:T(8,128)S(1)} %copy-done.1), custom_call_target="tpu_custom_call" | custom-call | tf_op jit(solution)/shard_map/pallas_call | solution.py:198
  79.0 0.0 collective-permute-done.14.w1
  79.0 0.0 collective-permute-done.15.w2
  79.0 0.5 collective-permute-done.16.w3
  79.5 4.7 %shard_map.95 = (bf16[512,256]{1,0:T(8,128)(2,1)S(1)}, bf16[512,256]{1,0:T(8,128)(2,1)S(1)}) custom-call(s32[32]{0:T(128)S(1)} %concatenate.9.order, bf16[512,5120]{1,0:T(8,128)(2,1)S(1)} %get-tuple-element.73.tokens, bf16[512,5120]{1,0:T(8,128)(2,1)S(1)} %get-tuple-element.74.tokens_other, bf16[8,160,256]{2,1,0:T(8,128)(2,1)} %shard_map.91.w0, ...), custom_call_target="tpu_custom_call" | custom-call | flops 26843545600 | bytes 14680064 | tf_op jit(solution)/shard_map/pallas_call | solution.py:246
  84.2 3.1 %collective-permute-start.18 = (bf16[512,256]{1,0:T(8,128)(2,1)S(1)}, bf16[512,256]{1,0:T(8,128)(2,1)S(1)}, u32[]{:S(2)}, u32[]{:S(2)}) collective-permute-start(bf16[512,256]{1,0:T(8,128)(2,1)S(1)} %get-tuple-element.80), channel_id=1, source_target_pairs={{0,8},{1,9},{2,10},{3,11},{4,12},{5,13},{6,14},{7,15},{8,0},{9,1},... | collective-permute-start | bytes 786440 | tf_op jit(solution)/shard_map/ppermute | solution.py:31
  87.3 0.0 collective-permute-done.23
  87.3 1.2 %fusion.2 = bf16[1,640,512]{2,1,0:T(8,128)(2,1)} fusion(bf16[640,512]{1,0:T(8,128)(2,1)S(1)} %collective-permute-done.23, bf16[1,640,512]{2,1,0:T(8,128)(2,1)S(1)} %collective-permute-done.20, bf16[1,640,512]{2,1,0:T(8,128)(2,1)S(1)} %get-tuple-element.82, bf16[2,640,512]{2,1,0:T(8,128)(2,1)S(1)} %copy-done.7), kind=kLoop, calls=%fused_computation.4 | loop fusion | flops 2621440 | bytes 3276800 | tf_op jit(solution)/shard_map/broadcast_in_dim | solution.py:326
  88.6 0.9 %maximum_select_fusion = bf16[512,512]{1,0:T(8,128)(2,1)} fusion(bf16[512,256]{1,0:T(8,128)(2,1)S(1)} %collective-permute-done.18, bf16[512,256]{1,0:T(8,128)(2,1)S(1)} %get-tuple-element.79, pred[]{:T(512)S(6)} %eq.21), kind=kLoop, calls=%fused_computation.5 | loop fusion | flops 2359296 | bytes 1048577 | tf_op jit(solution)/shard_map/jit(_where)/select_n | solution.py:331
  (27 shorter events, 0.2 us)
Async XLA Ops:
  0.6 5.3 %collective-permute-start = (bf16[640,512]{1,0:T(8,128)(2,1)}, bf16[640,512]{1,0:T(8,128)(2,1)S(1)}, u32[]{:S(2)}, u32[]{:S(2)}) collective-permute-start(bf16[640,512]{1,0:T(8,128)(2,1)} %bitcast.19), channel_id=1, source_target_pairs={{0,8},{1,9},{2,10},{3,11},{4,12},{5,13},{6,14},{7,15},{8,0},{9,1},... | collective-permute-start | bytes 1966088 | tf_op jit(solution)/shard_map/ppermute | solution.py:31
  6.6 6.9 %collective-permute-start.1 = (bf16[160,256]{1,0:T(8,128)(2,1)S(1)}, bf16[160,256]{1,0:T(8,128)(2,1)S(1)}, u32[]{:S(2)}, u32[]{:S(2)}) collective-permute-start(bf16[160,256]{1,0:T(8,128)(2,1)S(1)} %get-tuple-element.50), channel_id=1, source_target_pairs={{0,16},{1,17},{2,18},{3,19},{4,20},{5,21},{6,22},{7,23},{8,24},{9,... | collective-permute-start | bytes 245768 | tf_op jit(solution)/shard_map/ppermute | solution.py:31
  6.6 6.8 %collective-permute-start.2 = (bf16[160,256]{1,0:T(8,128)(2,1)S(1)}, bf16[160,256]{1,0:T(8,128)(2,1)S(1)}, u32[]{:S(2)}, u32[]{:S(2)}) collective-permute-start(bf16[160,256]{1,0:T(8,128)(2,1)S(1)} %get-tuple-element.54), channel_id=1, source_target_pairs={{0,32},{1,33},{2,34},{3,35},{4,36},{5,37},{6,38},{7,39},{8,40},{9,... | collective-permute-start | bytes 245768 | tf_op jit(solution)/shard_map/ppermute | solution.py:31
  8.6 5.0 %copy-start.4 = (bf16[512,5120]{1,0:T(8,128)(2,1)S(1)}, bf16[512,5120]{1,0:T(8,128)(2,1)}, u32[]{:S(2)}) copy-start(bf16[512,5120]{1,0:T(8,128)(2,1)} %tokens.2) | copy-start | bytes 15728644
  8.6 5.0 %collective-permute-start.3 = (bf16[160,256]{1,0:T(8,128)(2,1)S(1)}, bf16[160,256]{1,0:T(8,128)(2,1)S(1)}, u32[]{:S(2)}, u32[]{:S(2)}) collective-permute-start(bf16[160,256]{1,0:T(8,128)(2,1)S(1)} %get-tuple-element.55), channel_id=1, source_target_pairs={{0,48},{1,49},{2,50},{3,51},{4,52},{5,53},{6,54},{7,55},{8,56},{9,... | collective-permute-start | bytes 245768 | tf_op jit(solution)/shard_map/ppermute | solution.py:31
  13.6 29.2 %collective-permute-start.8 = (bf16[512,5120]{1,0:T(8,128)(2,1)S(1)}, bf16[512,5120]{1,0:T(8,128)(2,1)S(1)}, u32[]{:S(2)}, u32[]{:S(2)}) collective-permute-start(bf16[512,5120]{1,0:T(8,128)(2,1)S(1)} %copy-done.4), channel_id=1, source_target_pairs={{0,8},{1,9},{2,10},{3,11},{4,12},{5,13},{6,14},{7,15},{8,0},{9,1},... | collective-permute-start | bytes 15728648 | tf_op jit(solution)/shard_map/ppermute | solution.py:31
  15.2 27.6 %collective-permute-start.9 = (bf16[2,640,512]{2,1,0:T(8,128)(2,1)S(1)}, bf16[2,640,512]{2,1,0:T(8,128)(2,1)S(1)}, u32[]{:S(2)}, u32[]{:S(2)}) collective-permute-start(bf16[2,640,512]{2,1,0:T(8,128)(2,1)S(1)} %get-tuple-element.63), channel_id=1, source_target_pairs={{0,6},{1,7},{2,0},{3,1},{4,2},{5,3},{6,4},{7,5},{8,10},{9,11},{10,... | collective-permute-start | bytes 3932168 | tf_op jit(solution)/shard_map/ppermute | solution.py:31
  15.8 20.2 %collective-permute-start.21 = (bf16[1,640,512]{2,1,0:T(8,128)(2,1)S(1)}, bf16[1,640,512]{2,1,0:T(8,128)(2,1)S(1)}, u32[]{:S(2)}, u32[]{:S(2)}) collective-permute-start(bf16[1,640,512]{2,1,0:T(8,128)(2,1)S(1)} %get-tuple-element.52), channel_id=1, source_target_pairs={{0,2},{1,3},{2,4},{3,5},{4,6},{5,7},{6,0},{7,1},{8,14},{9,15},{10,... | collective-permute-start | bytes 1966088 | tf_op jit(solution)/shard_map/ppermute | solution.py:31
  17.9 5.0 %collective-permute-start.4 = (bf16[160,256]{1,0:T(8,128)(2,1)S(1)}, bf16[160,256]{1,0:T(8,128)(2,1)S(1)}, u32[]{:S(2)}, u32[]{:S(2)}) collective-permute-start(bf16[160,256]{1,0:T(8,128)(2,1)S(1)} %fusion.3), channel_id=1, source_target_pairs={{0,64},{1,65},{2,66},{3,67},{4,68},{5,69},{6,70},{7,71},{8,72},{9,... | collective-permute-start | bytes 245768 | tf_op jit(solution)/shard_map/ppermute | solution.py:31
  22.9 12.4 %copy-start = (f32[640,512]{1,0:T(8,128)S(1)}, f32[640,512]{1,0:T(8,128)}, u32[]{:S(2)}) copy-start(f32[640,512]{1,0:T(8,128)} %g.5) | copy-start | bytes 3932164
  22.9 12.4 %copy-start.1 = (f32[640,512]{1,0:T(8,128)S(1)}, f32[640,512]{1,0:T(8,128)}, u32[]{:S(2)}) copy-start(f32[640,512]{1,0:T(8,128)} %m.3) | copy-start | bytes 3932164
  22.9 12.4 %collective-permute-start.5 = (bf16[160,256]{1,0:T(8,128)(2,1)S(1)}, bf16[160,256]{1,0:T(8,128)(2,1)S(1)}, u32[]{:S(2)}, u32[]{:S(2)}) collective-permute-start(bf16[160,256]{1,0:T(8,128)(2,1)S(1)} %get-tuple-element.91), channel_id=1, source_target_pairs={{0,128},{1,129},{2,130},{3,131},{4,132},{5,133},{6,134},{7,135},{8... | collective-permute-start | bytes 245768 | tf_op jit(solution)/shard_map/ppermute | solution.py:31
  35.2 0.8 copy-start.2
  36.3 27.5 %collective-permute-start.22 = (bf16[1,640,512]{2,1,0:T(8,128)(2,1)S(1)}, bf16[1,640,512]{2,1,0:T(8,128)(2,1)}, u32[]{:S(2)}, u32[]{:S(2)}) collective-permute-start(bf16[1,640,512]{2,1,0:T(8,128)(2,1)S(1)} %add.188), channel_id=1, source_target_pairs={{0,2},{1,3},{2,4},{3,5},{4,6},{5,7},{6,0},{7,1},{8,14},{9,15},{10,... | collective-permute-start | bytes 1966088 | tf_op jit(solution)/shard_map/ppermute | solution.py:31
  36.6 6.2 %collective-permute-start.7 = (f32[160,256]{1,0:T(8,128)S(1)}, f32[160,256]{1,0:T(8,128)S(1)}, u32[]{:S(2)}, u32[]{:S(2)}) collective-permute-start(f32[160,256]{1,0:T(8,128)S(1)} %get-tuple-element.60), channel_id=1, source_target_pairs={{0,16},{1,17},{2,18},{3,19},{4,20},{5,21},{6,22},{7,23},{8,24},{9,... | collective-permute-start | bytes 491528 | tf_op jit(solution)/shard_map/ppermute | solution.py:31
  36.9 5.8 %collective-permute-start.6 = (bf16[160,256]{1,0:T(8,128)(2,1)S(1)}, bf16[160,256]{1,0:T(8,128)(2,1)S(1)}, u32[]{:S(2)}, u32[]{:S(2)}) collective-permute-start(bf16[160,256]{1,0:T(8,128)(2,1)S(1)} %get-tuple-element.59), channel_id=1, source_target_pairs={{0,33},{1,32},{2,35},{3,34},{4,37},{5,36},{6,39},{7,38},{8,41},{9,... | collective-permute-start | bytes 245768 | tf_op jit(solution)/shard_map/ppermute | solution.py:31
  42.8 12.9 %copy-start.6 = (bf16[2,640,512]{2,1,0:T(8,128)(2,1)}, bf16[2,640,512]{2,1,0:T(8,128)(2,1)S(1)}, u32[]{:S(2)}) copy-start(bf16[2,640,512]{2,1,0:T(8,128)(2,1)S(1)} %collective-permute-done.9) | copy-start | bytes 3932164
  42.8 12.9 %copy-start.5 = (bf16[512,5120]{1,0:T(8,128)(2,1)}, bf16[512,5120]{1,0:T(8,128)(2,1)S(1)}, u32[]{:S(2)}) copy-start(bf16[512,5120]{1,0:T(8,128)(2,1)S(1)} %collective-permute-done.8.b) | copy-start | bytes 15728644
  42.8 8.1 %collective-permute-start.10 = (f32[2,160,256]{2,1,0:T(8,128)S(1)}, f32[2,160,256]{2,1,0:T(8,128)S(1)}, u32[]{:S(2)}, u32[]{:S(2)}) collective-permute-start(f32[2,160,256]{2,1,0:T(8,128)S(1)} %shard_map.90.refs_0_), channel_id=1, source_target_pairs={{0,32},{1,33},{2,34},{3,35},{4,36},{5,37},{6,38},{7,39},{8,40},{9,... | collective-permute-start | bytes 983048 | tf_op jit(solution)/shard_map/ppermute | solution.py:31
  45.6 9.2 %collective-permute-start.11 = (bf16[2,160,256]{2,1,0:T(8,128)(2,1)S(1)}, bf16[2,160,256]{2,1,0:T(8,128)(2,1)S(1)}, u32[]{:S(2)}, u32[]{:S(2)}) collective-permute-start(bf16[2,160,256]{2,1,0:T(8,128)(2,1)S(1)} %shard_map.89.refs_0_), channel_id=1, source_target_pairs={{0,2},{1,3},{2,4},{3,5},{4,6},{5,7},{6,0},{7,1},{8,10},{9,11},{10,... | collective-permute-start | bytes 491528 | tf_op jit(solution)/shard_map/ppermute | solution.py:31
  46.7 8.1 %collective-permute-start.12 = (bf16[2,160,256]{2,1,0:T(8,128)(2,1)S(1)}, bf16[2,160,256]{2,1,0:T(8,128)(2,1)S(1)}, u32[]{:S(2)}, u32[]{:S(2)}) collective-permute-start(bf16[2,160,256]{2,1,0:T(8,128)(2,1)S(1)} %shard_map.89.refs_0_), channel_id=1, source_target_pairs={{0,4},{1,5},{2,6},{3,7},{4,0},{5,1},{6,2},{7,3},{8,12},{9,13},{10,... | collective-permute-start | bytes 491528 | tf_op jit(solution)/shard_map/ppermute | solution.py:31
  48.4 6.4 %collective-permute-start.13 = (bf16[2,160,256]{2,1,0:T(8,128)(2,1)S(1)}, bf16[2,160,256]{2,1,0:T(8,128)(2,1)S(1)}, u32[]{:S(2)}, u32[]{:S(2)}) collective-permute-start(bf16[2,160,256]{2,1,0:T(8,128)(2,1)S(1)} %shard_map.89.refs_0_), channel_id=1, source_target_pairs={{0,6},{1,7},{2,0},{3,1},{4,2},{5,3},{6,4},{7,5},{8,14},{9,15},{10,... | collective-permute-start | bytes 491528 | tf_op jit(solution)/shard_map/ppermute | solution.py:31
  51.0 20.4 %collective-permute-start.17 = (f32[4,160,256]{2,1,0:T(8,128)S(1)}, f32[4,160,256]{2,1,0:T(8,128)}, u32[]{:S(2)}, u32[]{:S(2)}) collective-permute-start(f32[4,160,256]{2,1,0:T(8,128)S(1)} %shard_map.92.average), channel_id=1, source_target_pairs={{0,8},{1,9},{2,10},{3,11},{4,12},{5,13},{6,14},{7,15},{8,0},{9,1},... | collective-permute-start | bytes 1966088 | tf_op jit(solution)/shard_map/ppermute | solution.py:31
  55.7 18.6 %collective-permute-start.19 = (bf16[1,640,512]{2,1,0:T(8,128)(2,1)}, bf16[1,640,512]{2,1,0:T(8,128)(2,1)}, u32[]{:S(2)}, u32[]{:S(2)}) collective-permute-start(bf16[1,640,512]{2,1,0:T(8,128)(2,1)} %get-tuple-element.85), channel_id=1, source_target_pairs={{0,2},{1,3},{2,4},{3,5},{4,6},{5,7},{6,0},{7,1},{8,14},{9,15},{10,... | collective-permute-start | bytes 1966088 | tf_op jit(solution)/shard_map/ppermute | solution.py:31
  57.9 21.1 %collective-permute-start.14 = (bf16[8,160,256]{2,1,0:T(8,128)(2,1)}, bf16[8,160,256]{2,1,0:T(8,128)(2,1)}, u32[]{:S(2)}, u32[]{:S(2)}) collective-permute-start(bf16[8,160,256]{2,1,0:T(8,128)(2,1)} %shard_map.91.w0), channel_id=1, source_target_pairs={{0,16},{1,17},{2,18},{3,19},{4,20},{5,21},{6,22},{7,23},{8,24},{9,... | collective-permute-start | bytes 1966088 | tf_op jit(solution)/shard_map/ppermute | solution.py:31
  58.9 20.1 %collective-permute-start.15 = (bf16[8,160,256]{2,1,0:T(8,128)(2,1)}, bf16[8,160,256]{2,1,0:T(8,128)(2,1)}, u32[]{:S(2)}, u32[]{:S(2)}) collective-permute-start(bf16[8,160,256]{2,1,0:T(8,128)(2,1)} %shard_map.91.w0), channel_id=1, source_target_pairs={{0,193},{1,64},{2,195},{3,66},{4,197},{5,68},{6,199},{7,70},{8,201... | collective-permute-start | bytes 1966088 | tf_op jit(solution)/shard_map/ppermute | solution.py:31
  63.8 15.7 %collective-permute-start.16 = (bf16[8,160,256]{2,1,0:T(8,128)(2,1)}, bf16[8,160,256]{2,1,0:T(8,128)(2,1)}, u32[]{:S(2)}, u32[]{:S(2)}) collective-permute-start(bf16[8,160,256]{2,1,0:T(8,128)(2,1)} %shard_map.91.w0), channel_id=1, source_target_pairs={{0,48},{1,49},{2,50},{3,51},{4,52},{5,53},{6,54},{7,55},{8,56},{9,... | collective-permute-start | bytes 1966088 | tf_op jit(solution)/shard_map/ppermute | solution.py:31
  65.4 4.2 %copy-start.3 = (bf16[1,640,512]{2,1,0:T(8,128)(2,1)S(1)}, bf16[1,640,512]{2,1,0:T(8,128)(2,1)}, u32[]{:S(2)}) copy-start(bf16[1,640,512]{2,1,0:T(8,128)(2,1)} %copy-done.2) | copy-start | bytes 1966084
  65.4 4.6 %copy-start.7 = (bf16[2,640,512]{2,1,0:T(8,128)(2,1)S(1)}, bf16[2,640,512]{2,1,0:T(8,128)(2,1)}, u32[]{:S(2)}) copy-start(bf16[2,640,512]{2,1,0:T(8,128)(2,1)} %copy-done.6) | copy-start | bytes 3932164
  71.3 16.0 %collective-permute-start.23 = (bf16[640,512]{1,0:T(8,128)(2,1)S(1)}, bf16[640,512]{1,0:T(8,128)(2,1)S(1)}, u32[]{:S(2)}, u32[]{:S(2)}) collective-permute-start(bf16[640,512]{1,0:T(8,128)(2,1)S(1)} %fusion.1), channel_id=1, source_target_pairs={{0,1},{1,0},{2,3},{3,2},{4,5},{5,4},{6,7},{7,6},{8,9},{9,8},{10,11... | collective-permute-start | bytes 1966088 | tf_op jit(solution)/shard_map/ppermute | solution.py:31
  75.6 11.7 %collective-permute-start.20 = (bf16[1,640,512]{2,1,0:T(8,128)(2,1)S(1)}, bf16[1,640,512]{2,1,0:T(8,128)(2,1)S(1)}, u32[]{:S(2)}, u32[]{:S(2)}) collective-permute-start(bf16[1,640,512]{2,1,0:T(8,128)(2,1)S(1)} %add.184), channel_id=1, source_target_pairs={{0,2},{1,3},{2,4},{3,5},{4,6},{5,7},{6,0},{7,1},{8,14},{9,15},{10,... | collective-permute-start | bytes 1966088 | tf_op jit(solution)/shard_map/ppermute | solution.py:31
  84.2 4.3 %collective-permute-start.18 = (bf16[512,256]{1,0:T(8,128)(2,1)S(1)}, bf16[512,256]{1,0:T(8,128)(2,1)S(1)}, u32[]{:S(2)}, u32[]{:S(2)}) collective-permute-start(bf16[512,256]{1,0:T(8,128)(2,1)S(1)} %get-tuple-element.80), channel_id=1, source_target_pairs={{0,8},{1,9},{2,10},{3,11},{4,12},{5,13},{6,14},{7,15},{8,0},{9,1},... | collective-permute-start | bytes 786440 | tf_op jit(solution)/shard_map/ppermute | solution.py:31

commit v7 on v6

--- a/solution.py
+++ b/solution.py
@@ -237,8 +237,11 @@
                 zl = order[12 + (z + (k == 2)) % 2]
                 at = order[4 + d] * (2 * SHARD) + zl * SHARD + order[20 + k] * ROWS
                 weights[pl.ds(pl.multiple_of(at, ROWS), ROWS), :] = ref[2 * d + z]
-    for src, out in ((tokens_other, keys_other), (tokens, keys)):
-        out[...] = jnp.dot(src[...], weights[...], preferred_element_type=F32).astype(BF16)
+    keys_other[...] = jnp.dot(
+        tokens_other[...], weights[...], preferred_element_type=F32
+    ).astype(BF16)
+    mine = pl.ds(pl.multiple_of(order[24] * COLS, COLS), COLS)
+    keys[:, mine] = jnp.dot(tokens[...], weights[...], preferred_element_type=F32).astype(BF16)
 
 
 def keys_of(order, tokens, tokens_other, blocks):
@@ -248,7 +251,7 @@
         in_specs=[pl.BlockSpec(memory_space=pltpu.SMEM)] + [here] * 6,
         out_specs=[here] * 2,
         scratch_shapes=[pltpu.VMEM((D, COLS), BF16)],
-        out_shape=[jax.ShapeDtypeStruct((TOK, COLS), BF16)] * 2,
+        out_shape=[jax.ShapeDtypeStruct((TOK, n), BF16) for n in (KW, COLS)],
         compiler_params=grant(24),
         cost_estimate=pl.CostEstimate(flops=20 * TOK * D * KW, bytes_accessed=14 << 20, transcendentals=0),
     )(order, tokens, tokens_other, *blocks)
@@ -328,11 +331,7 @@
     *blocks, new_global, tokens = lax.optimization_barrier((*blocks, new_global, tokens))
     keys, keys_other = keys_of(order, tokens, tokens_other, blocks)
     keys_got = after(shift(keys_other, core=1), weight_grad)
-    inner_keys = jnp.where(
-        core == 0,
-        jnp.concatenate([keys, keys_got], axis=1),
-        jnp.concatenate([keys_got, keys], axis=1),
-    )
+    inner_keys = lax.dynamic_update_slice(keys, keys_got, (0, (1 - core) * COLS))
     return (new_global, new_momentum, inner_keys, weight_grad)
 
 

time: 90.7 us -> 90.6 us (level)
  other arithmetic: 5.08 us -> 4.14 us
    select_n x1 -> x0, other arithmetic: 0.93 us -> none  [per_device(): jnp.where(core == 0, jnp.concatenate([keys, keys_got], axis=1), jnp.conca...]
  transfers between devices with their start and end apart: 24 -> 24, of which waited for: 6 -> 6; matrix products, arithmetic and copies ran while one was open for 5% -> 5% of each run, Pallas kernels for 29% -> 30%
where the time goes in v7:
time: 90.6 us; the launch traced here: 90.1 us
  starting transfers between devices  47.6 us (53%)
  Pallas kernels  27.6 us (30%)
  waiting for transfers between devices  8.4 us (9%)
  other arithmetic  4.14 us (5%)
  local copies, waits for them, and re-layouts  1.44 us (2%)
  between operations  0.92 us (1%)
    ppermute x24, starting transfers between devices, send(): return lax.ppermute(value, AXES, pairs)  47.6 us
    pallas_call x3, Pallas kernels, grad_parts(): pl.pallas_call(functools.partial(grad_kernel, at, sizes), in_specs=[pl.Bl...  10.6 us
    ppermute x24, waiting for transfers between devices, send(): return lax.ppermute(value, AXES, pairs)  8.4 us
    pallas_call x1, Pallas kernels, keys_of(): pl.pallas_call(keys_kernel, in_specs=[pl.BlockSpec(memory_space=pltpu.SME...  5.52 us
    pallas_call x1, Pallas kernels, hold(): pl.pallas_call(hold_kernel, in_specs=[pl.BlockSpec(memory_space=pltpu.HBM...  4.23 us
    pallas_call x1, Pallas kernels, update(): pl.pallas_call(update_kernel, grid_spec=pltpu.PrefetchScalarGridSpec(num_...  3.22 us
  transfers between devices with their start and end apart: 24, of which 6 were waited for; matrix products, arithmetic and copies ran while one was open for 5% of the time, Pallas kernels for 30%

profile of v7, /device:TPU:1, one launch (start us, length us, event | category | flops | bytes accessed | tf_op | source)
XLA Modules:
  0.0 90.1 jit_solution(8711123589015831546)
XLA Ops:
  0.6 3.3 %collective-permute-start = (bf16[640,512]{1,0:T(8,128)(2,1)}, bf16[640,512]{1,0:T(8,128)(2,1)S(1)}, u32[]{:S(2)}, u32[]{:S(2)}) collective-permute-start(bf16[640,512]{1,0:T(8,128)(2,1)} %bitcast.19), channel_id=1, source_target_pairs={{0,8},{1,9},{2,10},{3,11},{4,12},{5,13},{6,14},{7,15},{8,0},{9,1},... | collective-permute-start | bytes 1966088 | tf_op jit(solution)/shard_map/ppermute | solution.py:31
  4.0 0.1 concatenate.3.order
  4.1 1.8 %shard_map.84.base = f32[640,256]{1,0:T(8,128)S(1)} custom-call(s32[32]{0:T(128)S(1)} %concatenate.3.order, f32[640,512]{1,0:T(8,128)} %g.5, bf16[640,512]{1,0:T(8,128)(2,1)} %bitcast.20), custom_call_target="tpu_custom_call" | custom-call | tf_op jit(solution)/shard_map/pallas_call | solution.py:106
  5.9 0.0 collective-permute-done.l1
  5.9 0.6 shard_map.85
  6.6 0.1 collective-permute-start.1
  6.6 1.9 %collective-permute-start.2 = (bf16[160,256]{1,0:T(8,128)(2,1)S(1)}, bf16[160,256]{1,0:T(8,128)(2,1)S(1)}, u32[]{:S(2)}, u32[]{:S(2)}) collective-permute-start(bf16[160,256]{1,0:T(8,128)(2,1)S(1)} %get-tuple-element.54), channel_id=1, source_target_pairs={{0,32},{1,33},{2,34},{3,35},{4,36},{5,37},{6,38},{7,39},{8,40},{9,... | collective-permute-start | bytes 245768 | tf_op jit(solution)/shard_map/ppermute | solution.py:31
  8.6 1.2 %collective-permute-start.3 = (bf16[160,256]{1,0:T(8,128)(2,1)S(1)}, bf16[160,256]{1,0:T(8,128)(2,1)S(1)}, u32[]{:S(2)}, u32[]{:S(2)}) collective-permute-start(bf16[160,256]{1,0:T(8,128)(2,1)S(1)} %get-tuple-element.55), channel_id=1, source_target_pairs={{0,48},{1,49},{2,50},{3,51},{4,52},{5,53},{6,54},{7,55},{8,56},{9,... | collective-permute-start | bytes 245768 | tf_op jit(solution)/shard_map/ppermute | solution.py:31
  9.7 3.4 %shard_map.86 = (bf16[1,640,512]{2,1,0:T(8,128)(2,1)S(1)}, bf16[2,640,512]{2,1,0:T(8,128)(2,1)S(1)}) custom-call(s32[32]{0:T(128)S(1)} %concatenate.3.order, bf16[512,5120]{1,0:T(8,128)(2,1)} %tokens.2, bf16[512,512]{1,0:T(8,128)(2,1)} %key_grad.5), custom_call_target="tpu_custom_call" | custom-call | flops 1006632960 | bytes 3932160 | tf_op jit(solution)/shard_map/pallas_call | solution.py:83
  13.2 0.3 collective-permute-done.1
  13.5 0.0 collective-permute-done.2
  13.5 0.1 collective-permute-done.3
  13.6 1.6 %collective-permute-start.8 = (bf16[512,5120]{1,0:T(8,128)(2,1)S(1)}, bf16[512,5120]{1,0:T(8,128)(2,1)S(1)}, u32[]{:S(2)}, u32[]{:S(2)}) collective-permute-start(bf16[512,5120]{1,0:T(8,128)(2,1)S(1)} %copy-done.4), channel_id=1, source_target_pairs={{0,8},{1,9},{2,10},{3,11},{4,12},{5,13},{6,14},{7,15},{8,0},{9,1},... | collective-permute-start | bytes 15728648 | tf_op jit(solution)/shard_map/ppermute | solution.py:31
  15.2 0.7 collective-permute-start.9
  15.8 2.0 %collective-permute-start.21 = (bf16[1,640,512]{2,1,0:T(8,128)(2,1)S(1)}, bf16[1,640,512]{2,1,0:T(8,128)(2,1)S(1)}, u32[]{:S(2)}, u32[]{:S(2)}) collective-permute-start(bf16[1,640,512]{2,1,0:T(8,128)(2,1)S(1)} %get-tuple-element.52), channel_id=1, source_target_pairs={{0,2},{1,3},{2,4},{3,5},{4,6},{5,7},{6,0},{7,1},{8,14},{9,15},{10,... | collective-permute-start | bytes 1966088 | tf_op jit(solution)/shard_map/ppermute | solution.py:31
  17.9 2.4 %collective-permute-start.4 = (bf16[160,256]{1,0:T(8,128)(2,1)S(1)}, bf16[160,256]{1,0:T(8,128)(2,1)S(1)}, u32[]{:S(2)}, u32[]{:S(2)}) collective-permute-start(bf16[160,256]{1,0:T(8,128)(2,1)S(1)} %fusion.3), channel_id=1, source_target_pairs={{0,64},{1,65},{2,66},{3,67},{4,68},{5,69},{6,70},{7,71},{8,72},{9,... | collective-permute-start | bytes 245768 | tf_op jit(solution)/shard_map/ppermute | solution.py:31
  20.3 2.5 %collective-permute-done.4 = bf16[160,256]{1,0:T(8,128)(2,1)S(1)} collective-permute-done((bf16[160,256]{1,0:T(8,128)(2,1)S(1)}, bf16[160,256]{1,0:T(8,128)(2,1)S(1)}, u32[]{:S(2)}, u32[]{:S(2)}) %collective-permute-start.4) | collective-permute-done | bytes 81952 | tf_op jit(solution)/shard_map/ppermute | solution.py:31
  22.8 0.1 fusion.9
  22.9 0.0 copy-start
  22.9 0.0 copy-start.1
  22.9 8.1 %collective-permute-start.5 = (bf16[160,256]{1,0:T(8,128)(2,1)S(1)}, bf16[160,256]{1,0:T(8,128)(2,1)S(1)}, u32[]{:S(2)}, u32[]{:S(2)}) collective-permute-start(bf16[160,256]{1,0:T(8,128)(2,1)S(1)} %get-tuple-element.91), channel_id=1, source_target_pairs={{0,128},{1,129},{2,130},{3,131},{4,132},{5,133},{6,134},{7,135},{8... | collective-permute-start | bytes 245768 | tf_op jit(solution)/shard_map/ppermute | solution.py:31
  31.0 4.3 %shard_map.87 = (bf16[1,640,512]{2,1,0:T(8,128)(2,1)S(1)}, bf16[1,640,512]{2,1,0:T(8,128)(2,1)S(1)}, bf16[1,640,512]{2,1,0:T(8,128)(2,1)}) custom-call(s32[32]{0:T(128)S(1)} %concatenate.3.order, bf16[512,5120]{1,0:T(8,128)(2,1)} %tokens.2, bf16[512,512]{1,0:T(8,128)(2,1)} %key_grad.5), custom_call_target="tpu_custom_call" | custom-call | flops 1006632960 | bytes 3932160 | tf_op jit(solution)/shard_map/pallas_call | solution.py:83
  35.3 0.0 collective-permute-done.5.got
  35.3 0.6 shard_map.88
  35.9 0.2 copy-done.2
  36.1 0.0 collective-permute-done.21
  36.1 0.2 add.191
  36.3 0.3 collective-permute-start.22
  36.6 0.4 collective-permute-start.7
  36.9 2.5 %collective-permute-start.6 = (bf16[160,256]{1,0:T(8,128)(2,1)S(1)}, bf16[160,256]{1,0:T(8,128)(2,1)S(1)}, u32[]{:S(2)}, u32[]{:S(2)}) collective-permute-start(bf16[160,256]{1,0:T(8,128)(2,1)S(1)} %get-tuple-element.59), channel_id=1, source_target_pairs={{0,33},{1,32},{2,35},{3,34},{4,37},{5,36},{6,39},{7,38},{8,41},{9,... | collective-permute-start | bytes 245768 | tf_op jit(solution)/shard_map/ppermute | solution.py:31
  39.5 3.3 %collective-permute-done.6 = bf16[160,256]{1,0:T(8,128)(2,1)S(1)} collective-permute-done((bf16[160,256]{1,0:T(8,128)(2,1)S(1)}, bf16[160,256]{1,0:T(8,128)(2,1)S(1)}, u32[]{:S(2)}, u32[]{:S(2)}) %collective-permute-start.6) | collective-permute-done | bytes 81952 | tf_op jit(solution)/shard_map/ppermute | solution.py:31
  42.7 0.0 collective-permute-done.7
  42.8 0.0 collective-permute-done.9
  42.8 0.0 copy-start.6
  42.8 0.0 collective-permute-done.8.b
  42.8 2.8 %collective-permute-start.10 = (f32[2,160,256]{2,1,0:T(8,128)S(1)}, f32[2,160,256]{2,1,0:T(8,128)S(1)}, u32[]{:S(2)}, u32[]{:S(2)}) collective-permute-start(f32[2,160,256]{2,1,0:T(8,128)S(1)} %shard_map.90.refs_0_), channel_id=1, source_target_pairs={{0,32},{1,33},{2,34},{3,35},{4,36},{5,37},{6,38},{7,39},{8,40},{9,... | collective-permute-start | bytes 983048 | tf_op jit(solution)/shard_map/ppermute | solution.py:31
  45.6 1.1 %collective-permute-start.11 = (bf16[2,160,256]{2,1,0:T(8,128)(2,1)S(1)}, bf16[2,160,256]{2,1,0:T(8,128)(2,1)S(1)}, u32[]{:S(2)}, u32[]{:S(2)}) collective-permute-start(bf16[2,160,256]{2,1,0:T(8,128)(2,1)S(1)} %shard_map.89.refs_0_), channel_id=1, source_target_pairs={{0,2},{1,3},{2,4},{3,5},{4,6},{5,7},{6,0},{7,1},{8,10},{9,11},{10,... | collective-permute-start | bytes 491528 | tf_op jit(solution)/shard_map/ppermute | solution.py:31
  46.7 1.7 %collective-permute-start.12 = (bf16[2,160,256]{2,1,0:T(8,128)(2,1)S(1)}, bf16[2,160,256]{2,1,0:T(8,128)(2,1)S(1)}, u32[]{:S(2)}, u32[]{:S(2)}) collective-permute-start(bf16[2,160,256]{2,1,0:T(8,128)(2,1)S(1)} %shard_map.89.refs_0_), channel_id=1, source_target_pairs={{0,4},{1,5},{2,6},{3,7},{4,0},{5,1},{6,2},{7,3},{8,12},{9,13},{10,... | collective-permute-start | bytes 491528 | tf_op jit(solution)/shard_map/ppermute | solution.py:31
  48.5 0.8 collective-permute-start.13
  49.2 1.7 %collective-permute-done.10.refs_1_ = f32[2,160,256]{2,1,0:T(8,128)S(1)} collective-permute-done((f32[2,160,256]{2,1,0:T(8,128)S(1)}, f32[2,160,256]{2,1,0:T(8,128)S(1)}, u32[]{:S(2)}, u32[]{:S(2)}) %collective-permute-start.10) | collective-permute-done | bytes 327712 | tf_op jit(solution)/shard_map/ppermute | solution.py:31
  51.0 3.9 %collective-permute-start.17 = (f32[4,160,256]{2,1,0:T(8,128)S(1)}, f32[4,160,256]{2,1,0:T(8,128)}, u32[]{:S(2)}, u32[]{:S(2)}) collective-permute-start(f32[4,160,256]{2,1,0:T(8,128)S(1)} %shard_map.92.average), channel_id=1, source_target_pairs={{0,8},{1,9},{2,10},{3,11},{4,12},{5,13},{6,14},{7,15},{8,0},{9,1},... | collective-permute-start | bytes 1966088 | tf_op jit(solution)/shard_map/ppermute | solution.py:31
  54.8 0.9 shard_map.91.w0
  55.7 2.2 %collective-permute-start.19 = (bf16[1,640,512]{2,1,0:T(8,128)(2,1)}, bf16[1,640,512]{2,1,0:T(8,128)(2,1)}, u32[]{:S(2)}, u32[]{:S(2)}) collective-permute-start(bf16[1,640,512]{2,1,0:T(8,128)(2,1)} %get-tuple-element.85), channel_id=1, source_target_pairs={{0,2},{1,3},{2,4},{3,5},{4,6},{5,7},{6,0},{7,1},{8,14},{9,15},{10,... | collective-permute-start | bytes 1966088 | tf_op jit(solution)/shard_map/ppermute | solution.py:31
  57.9 1.0 %collective-permute-start.14 = (bf16[8,160,256]{2,1,0:T(8,128)(2,1)}, bf16[8,160,256]{2,1,0:T(8,128)(2,1)}, u32[]{:S(2)}, u32[]{:S(2)}) collective-permute-start(bf16[8,160,256]{2,1,0:T(8,128)(2,1)} %shard_map.91.w0), channel_id=1, source_target_pairs={{0,16},{1,17},{2,18},{3,19},{4,20},{5,21},{6,22},{7,23},{8,24},{9,... | collective-permute-start | bytes 1966088 | tf_op jit(solution)/shard_map/ppermute | solution.py:31
  58.9 4.9 %collective-permute-start.15 = (bf16[8,160,256]{2,1,0:T(8,128)(2,1)}, bf16[8,160,256]{2,1,0:T(8,128)(2,1)}, u32[]{:S(2)}, u32[]{:S(2)}) collective-permute-start(bf16[8,160,256]{2,1,0:T(8,128)(2,1)} %shard_map.91.w0), channel_id=1, source_target_pairs={{0,193},{1,64},{2,195},{3,66},{4,197},{5,68},{6,199},{7,70},{8,201... | collective-permute-start | bytes 1966088 | tf_op jit(solution)/shard_map/ppermute | solution.py:31
  63.8 1.6 %collective-permute-start.16 = (bf16[8,160,256]{2,1,0:T(8,128)(2,1)}, bf16[8,160,256]{2,1,0:T(8,128)(2,1)}, u32[]{:S(2)}, u32[]{:S(2)}) collective-permute-start(bf16[8,160,256]{2,1,0:T(8,128)(2,1)} %shard_map.91.w0), channel_id=1, source_target_pairs={{0,48},{1,49},{2,50},{3,51},{4,52},{5,53},{6,54},{7,55},{8,56},{9,... | collective-permute-start | bytes 1966088 | tf_op jit(solution)/shard_map/ppermute | solution.py:31
  65.4 4.2 %shard_map.94 = (bf16[512,5120]{1,0:T(8,128)(2,1)S(1)}, bf16[512,5120]{1,0:T(8,128)(2,1)S(1)}) custom-call(bf16[512,5120]{1,0:T(8,128)(2,1)} %tokens.2, bf16[512,5120]{1,0:T(8,128)(2,1)} %copy-done.5), custom_call_target="tpu_custom_call" | custom-call | tf_op jit(solution)/shard_map/pallas_call | solution.py:223
  69.6 0.3 copy-done.7
  70.0 1.4 %fusion.1 = bf16[640,512]{1,0:T(8,128)(2,1)S(1)} fusion(bf16[1,640,512]{2,1,0:T(8,128)(2,1)} %collective-permute-done.22, bf16[1,640,512]{2,1,0:T(8,128)(2,1)S(1)} %copy-done.3, bf16[2,640,512]{2,1,0:T(8,128)(2,1)S(1)} %copy-done.7), kind=kLoop, calls=%fused_computation.3 | loop fusion | flops 1966080 | bytes 2621440 | tf_op jit(solution)/shard_map/convert_element_type | solution.py:321
  71.3 0.0 collective-permute-done.17.average_other
  71.3 0.1 collective-permute-start.23
  71.4 2.9 %shard_map.96 = (bf16[1,640,512]{2,1,0:T(8,128)(2,1)S(1)}, bf16[1,640,512]{2,1,0:T(8,128)(2,1)S(1)}) custom-call(s32[32]{0:T(128)S(1)} %concatenate.3.order, bf16[512,5120]{1,0:T(8,128)(2,1)} %tokens.2, bf16[512,512]{1,0:T(8,128)(2,1)} %key_grad.5), custom_call_target="tpu_custom_call" | custom-call | flops 671088640 | bytes 2621440 | tf_op jit(solution)/shard_map/pallas_call | solution.py:83
  74.3 0.0 collective-permute-done.19
  74.4 1.3 %add.187 = bf16[1,640,512]{2,1,0:T(8,128)(2,1)S(1)} add(bf16[1,640,512]{2,1,0:T(8,128)(2,1)S(1)} %get-tuple-element.84, bf16[1,640,512]{2,1,0:T(8,128)(2,1)} %collective-permute-done.19) | non-fusion elementwise | flops 327680 | bytes 1966080 | tf_op jit(solution)/shard_map/add | solution.py:324
  75.6 0.2 collective-permute-start.20
  75.8 3.2 %shard_map.93 = (f32[640,512]{1,0:T(8,128)}, f32[640,512]{1,0:T(8,128)}) custom-call(s32[32]{0:T(128)S(1)} %concatenate.3.order, f32[4,160,256]{2,1,0:T(8,128)S(1)} %shard_map.92.average, f32[4,160,256]{2,1,0:T(8,128)} %collective-permute-done.17.average_other, f32[640,512]{1,0:T(8,128)S(1)} %copy-done, f32[640,512]{1,0:T(8,128)S(1)} %copy-done.1), custom_call_target="tpu_custom_call" | custom-call | tf_op jit(solution)/shard_map/pallas_call | solution.py:198
  79.0 0.5 collective-permute-done.16.w3
  79.5 5.5 %shard_map.95 = (bf16[512,512]{1,0:T(8,128)(2,1)}, bf16[512,256]{1,0:T(8,128)(2,1)S(1)}) custom-call(s32[32]{0:T(128)S(1)} %concatenate.3.order, bf16[512,5120]{1,0:T(8,128)(2,1)S(1)} %get-tuple-element.73.tokens, bf16[512,5120]{1,0:T(8,128)(2,1)S(1)} %get-tuple-element.74.tokens_other, bf16[8,160,256]{2,1,0:T(8,128)(2,1)} %shard_map.91.w0, ...), custom_call_target="tpu_custom_call" | custom-call | flops 26843545600 | bytes 14680064 | tf_op jit(solution)/shard_map/pallas_call | solution.py:249
  85.0 3.0 %collective-permute-start.18 = (bf16[512,256]{1,0:T(8,128)(2,1)S(1)}, bf16[512,256]{1,0:T(8,128)(2,1)S(1)}, u32[]{:S(2)}, u32[]{:S(2)}) collective-permute-start(bf16[512,256]{1,0:T(8,128)(2,1)S(1)} %get-tuple-element.80), channel_id=1, source_target_pairs={{0,8},{1,9},{2,10},{3,11},{4,12},{5,13},{6,14},{7,15},{8,0},{9,1},... | collective-permute-start | bytes 786440 | tf_op jit(solution)/shard_map/ppermute | solution.py:31
  88.0 0.0 collective-permute-done.23
  88.0 0.0 collective-permute-done.20
  88.1 1.2 %fusion.2 = bf16[1,640,512]{2,1,0:T(8,128)(2,1)} fusion(bf16[640,512]{1,0:T(8,128)(2,1)S(1)} %collective-permute-done.23, bf16[1,640,512]{2,1,0:T(8,128)(2,1)S(1)} %collective-permute-done.20, bf16[1,640,512]{2,1,0:T(8,128)(2,1)S(1)} %get-tuple-element.82, bf16[2,640,512]{2,1,0:T(8,128)(2,1)S(1)} %copy-done.7), kind=kLoop, calls=%fused_computation.4 | loop fusion | flops 2621440 | bytes 3276800 | tf_op jit(solution)/shard_map/broadcast_in_dim | solution.py:329
  89.3 0.0 copy-start.9
  89.3 0.8 copy-done.9
  (31 shorter events, 0.2 us)
Async XLA Ops:
  0.6 5.3 %collective-permute-start = (bf16[640,512]{1,0:T(8,128)(2,1)}, bf16[640,512]{1,0:T(8,128)(2,1)S(1)}, u32[]{:S(2)}, u32[]{:S(2)}) collective-permute-start(bf16[640,512]{1,0:T(8,128)(2,1)} %bitcast.19), channel_id=1, source_target_pairs={{0,8},{1,9},{2,10},{3,11},{4,12},{5,13},{6,14},{7,15},{8,0},{9,1},... | collective-permute-start | bytes 1966088 | tf_op jit(solution)/shard_map/ppermute | solution.py:31
  6.6 6.9 %collective-permute-start.1 = (bf16[160,256]{1,0:T(8,128)(2,1)S(1)}, bf16[160,256]{1,0:T(8,128)(2,1)S(1)}, u32[]{:S(2)}, u32[]{:S(2)}) collective-permute-start(bf16[160,256]{1,0:T(8,128)(2,1)S(1)} %get-tuple-element.50), channel_id=1, source_target_pairs={{0,16},{1,17},{2,18},{3,19},{4,20},{5,21},{6,22},{7,23},{8,24},{9,... | collective-permute-start | bytes 245768 | tf_op jit(solution)/shard_map/ppermute | solution.py:31
  6.6 6.8 %collective-permute-start.2 = (bf16[160,256]{1,0:T(8,128)(2,1)S(1)}, bf16[160,256]{1,0:T(8,128)(2,1)S(1)}, u32[]{:S(2)}, u32[]{:S(2)}) collective-permute-start(bf16[160,256]{1,0:T(8,128)(2,1)S(1)} %get-tuple-element.54), channel_id=1, source_target_pairs={{0,32},{1,33},{2,34},{3,35},{4,36},{5,37},{6,38},{7,39},{8,40},{9,... | collective-permute-start | bytes 245768 | tf_op jit(solution)/shard_map/ppermute | solution.py:31
  8.6 5.0 %copy-start.4 = (bf16[512,5120]{1,0:T(8,128)(2,1)S(1)}, bf16[512,5120]{1,0:T(8,128)(2,1)}, u32[]{:S(2)}) copy-start(bf16[512,5120]{1,0:T(8,128)(2,1)} %tokens.2) | copy-start | bytes 15728644
  8.6 5.0 %collective-permute-start.3 = (bf16[160,256]{1,0:T(8,128)(2,1)S(1)}, bf16[160,256]{1,0:T(8,128)(2,1)S(1)}, u32[]{:S(2)}, u32[]{:S(2)}) collective-permute-start(bf16[160,256]{1,0:T(8,128)(2,1)S(1)} %get-tuple-element.55), channel_id=1, source_target_pairs={{0,48},{1,49},{2,50},{3,51},{4,52},{5,53},{6,54},{7,55},{8,56},{9,... | collective-permute-start | bytes 245768 | tf_op jit(solution)/shard_map/ppermute | solution.py:31
  13.6 29.2 %collective-permute-start.8 = (bf16[512,5120]{1,0:T(8,128)(2,1)S(1)}, bf16[512,5120]{1,0:T(8,128)(2,1)S(1)}, u32[]{:S(2)}, u32[]{:S(2)}) collective-permute-start(bf16[512,5120]{1,0:T(8,128)(2,1)S(1)} %copy-done.4), channel_id=1, source_target_pairs={{0,8},{1,9},{2,10},{3,11},{4,12},{5,13},{6,14},{7,15},{8,0},{9,1},... | collective-permute-start | bytes 15728648 | tf_op jit(solution)/shard_map/ppermute | solution.py:31
  15.2 27.6 %collective-permute-start.9 = (bf16[2,640,512]{2,1,0:T(8,128)(2,1)S(1)}, bf16[2,640,512]{2,1,0:T(8,128)(2,1)S(1)}, u32[]{:S(2)}, u32[]{:S(2)}) collective-permute-start(bf16[2,640,512]{2,1,0:T(8,128)(2,1)S(1)} %get-tuple-element.63), channel_id=1, source_target_pairs={{0,6},{1,7},{2,0},{3,1},{4,2},{5,3},{6,4},{7,5},{8,10},{9,11},{10,... | collective-permute-start | bytes 3932168 | tf_op jit(solution)/shard_map/ppermute | solution.py:31
  15.8 20.3 %collective-permute-start.21 = (bf16[1,640,512]{2,1,0:T(8,128)(2,1)S(1)}, bf16[1,640,512]{2,1,0:T(8,128)(2,1)S(1)}, u32[]{:S(2)}, u32[]{:S(2)}) collective-permute-start(bf16[1,640,512]{2,1,0:T(8,128)(2,1)S(1)} %get-tuple-element.52), channel_id=1, source_target_pairs={{0,2},{1,3},{2,4},{3,5},{4,6},{5,7},{6,0},{7,1},{8,14},{9,15},{10,... | collective-permute-start | bytes 1966088 | tf_op jit(solution)/shard_map/ppermute | solution.py:31
  17.9 5.0 %collective-permute-start.4 = (bf16[160,256]{1,0:T(8,128)(2,1)S(1)}, bf16[160,256]{1,0:T(8,128)(2,1)S(1)}, u32[]{:S(2)}, u32[]{:S(2)}) collective-permute-start(bf16[160,256]{1,0:T(8,128)(2,1)S(1)} %fusion.3), channel_id=1, source_target_pairs={{0,64},{1,65},{2,66},{3,67},{4,68},{5,69},{6,70},{7,71},{8,72},{9,... | collective-permute-start | bytes 245768 | tf_op jit(solution)/shard_map/ppermute | solution.py:31
  22.9 12.4 %copy-start = (f32[640,512]{1,0:T(8,128)S(1)}, f32[640,512]{1,0:T(8,128)}, u32[]{:S(2)}) copy-start(f32[640,512]{1,0:T(8,128)} %g.5) | copy-start | bytes 3932164
  22.9 12.4 %copy-start.1 = (f32[640,512]{1,0:T(8,128)S(1)}, f32[640,512]{1,0:T(8,128)}, u32[]{:S(2)}) copy-start(f32[640,512]{1,0:T(8,128)} %m.3) | copy-start | bytes 3932164
  22.9 12.4 %collective-permute-start.5 = (bf16[160,256]{1,0:T(8,128)(2,1)S(1)}, bf16[160,256]{1,0:T(8,128)(2,1)S(1)}, u32[]{:S(2)}, u32[]{:S(2)}) collective-permute-start(bf16[160,256]{1,0:T(8,128)(2,1)S(1)} %get-tuple-element.91), channel_id=1, source_target_pairs={{0,128},{1,129},{2,130},{3,131},{4,132},{5,133},{6,134},{7,135},{8... | collective-permute-start | bytes 245768 | tf_op jit(solution)/shard_map/ppermute | solution.py:31
  35.2 0.8 copy-start.2
  36.3 27.5 %collective-permute-start.22 = (bf16[1,640,512]{2,1,0:T(8,128)(2,1)S(1)}, bf16[1,640,512]{2,1,0:T(8,128)(2,1)}, u32[]{:S(2)}, u32[]{:S(2)}) collective-permute-start(bf16[1,640,512]{2,1,0:T(8,128)(2,1)S(1)} %add.191), channel_id=1, source_target_pairs={{0,2},{1,3},{2,4},{3,5},{4,6},{5,7},{6,0},{7,1},{8,14},{9,15},{10,... | collective-permute-start | bytes 1966088 | tf_op jit(solution)/shard_map/ppermute | solution.py:31
  36.6 6.2 %collective-permute-start.7 = (f32[160,256]{1,0:T(8,128)S(1)}, f32[160,256]{1,0:T(8,128)S(1)}, u32[]{:S(2)}, u32[]{:S(2)}) collective-permute-start(f32[160,256]{1,0:T(8,128)S(1)} %get-tuple-element.60), channel_id=1, source_target_pairs={{0,16},{1,17},{2,18},{3,19},{4,20},{5,21},{6,22},{7,23},{8,24},{9,... | collective-permute-start | bytes 491528 | tf_op jit(solution)/shard_map/ppermute | solution.py:31
  36.9 5.8 %collective-permute-start.6 = (bf16[160,256]{1,0:T(8,128)(2,1)S(1)}, bf16[160,256]{1,0:T(8,128)(2,1)S(1)}, u32[]{:S(2)}, u32[]{:S(2)}) collective-permute-start(bf16[160,256]{1,0:T(8,128)(2,1)S(1)} %get-tuple-element.59), channel_id=1, source_target_pairs={{0,33},{1,32},{2,35},{3,34},{4,37},{5,36},{6,39},{7,38},{8,41},{9,... | collective-permute-start | bytes 245768 | tf_op jit(solution)/shard_map/ppermute | solution.py:31
  42.8 12.9 %copy-start.6 = (bf16[2,640,512]{2,1,0:T(8,128)(2,1)}, bf16[2,640,512]{2,1,0:T(8,128)(2,1)S(1)}, u32[]{:S(2)}) copy-start(bf16[2,640,512]{2,1,0:T(8,128)(2,1)S(1)} %collective-permute-done.9) | copy-start | bytes 3932164
  42.8 12.9 %copy-start.5 = (bf16[512,5120]{1,0:T(8,128)(2,1)}, bf16[512,5120]{1,0:T(8,128)(2,1)S(1)}, u32[]{:S(2)}) copy-start(bf16[512,5120]{1,0:T(8,128)(2,1)S(1)} %collective-permute-done.8.b) | copy-start | bytes 15728644
  42.8 8.1 %collective-permute-start.10 = (f32[2,160,256]{2,1,0:T(8,128)S(1)}, f32[2,160,256]{2,1,0:T(8,128)S(1)}, u32[]{:S(2)}, u32[]{:S(2)}) collective-permute-start(f32[2,160,256]{2,1,0:T(8,128)S(1)} %shard_map.90.refs_0_), channel_id=1, source_target_pairs={{0,32},{1,33},{2,34},{3,35},{4,36},{5,37},{6,38},{7,39},{8,40},{9,... | collective-permute-start | bytes 983048 | tf_op jit(solution)/shard_map/ppermute | solution.py:31
  45.6 9.2 %collective-permute-start.11 = (bf16[2,160,256]{2,1,0:T(8,128)(2,1)S(1)}, bf16[2,160,256]{2,1,0:T(8,128)(2,1)S(1)}, u32[]{:S(2)}, u32[]{:S(2)}) collective-permute-start(bf16[2,160,256]{2,1,0:T(8,128)(2,1)S(1)} %shard_map.89.refs_0_), channel_id=1, source_target_pairs={{0,2},{1,3},{2,4},{3,5},{4,6},{5,7},{6,0},{7,1},{8,10},{9,11},{10,... | collective-permute-start | bytes 491528 | tf_op jit(solution)/shard_map/ppermute | solution.py:31
  46.7 8.1 %collective-permute-start.12 = (bf16[2,160,256]{2,1,0:T(8,128)(2,1)S(1)}, bf16[2,160,256]{2,1,0:T(8,128)(2,1)S(1)}, u32[]{:S(2)}, u32[]{:S(2)}) collective-permute-start(bf16[2,160,256]{2,1,0:T(8,128)(2,1)S(1)} %shard_map.89.refs_0_), channel_id=1, source_target_pairs={{0,4},{1,5},{2,6},{3,7},{4,0},{5,1},{6,2},{7,3},{8,12},{9,13},{10,... | collective-permute-start | bytes 491528 | tf_op jit(solution)/shard_map/ppermute | solution.py:31
  48.5 6.4 %collective-permute-start.13 = (bf16[2,160,256]{2,1,0:T(8,128)(2,1)S(1)}, bf16[2,160,256]{2,1,0:T(8,128)(2,1)S(1)}, u32[]{:S(2)}, u32[]{:S(2)}) collective-permute-start(bf16[2,160,256]{2,1,0:T(8,128)(2,1)S(1)} %shard_map.89.refs_0_), channel_id=1, source_target_pairs={{0,6},{1,7},{2,0},{3,1},{4,2},{5,3},{6,4},{7,5},{8,14},{9,15},{10,... | collective-permute-start | bytes 491528 | tf_op jit(solution)/shard_map/ppermute | solution.py:31
  51.0 20.4 %collective-permute-start.17 = (f32[4,160,256]{2,1,0:T(8,128)S(1)}, f32[4,160,256]{2,1,0:T(8,128)}, u32[]{:S(2)}, u32[]{:S(2)}) collective-permute-start(f32[4,160,256]{2,1,0:T(8,128)S(1)} %shard_map.92.average), channel_id=1, source_target_pairs={{0,8},{1,9},{2,10},{3,11},{4,12},{5,13},{6,14},{7,15},{8,0},{9,1},... | collective-permute-start | bytes 1966088 | tf_op jit(solution)/shard_map/ppermute | solution.py:31
  55.7 18.6 %collective-permute-start.19 = (bf16[1,640,512]{2,1,0:T(8,128)(2,1)}, bf16[1,640,512]{2,1,0:T(8,128)(2,1)}, u32[]{:S(2)}, u32[]{:S(2)}) collective-permute-start(bf16[1,640,512]{2,1,0:T(8,128)(2,1)} %get-tuple-element.85), channel_id=1, source_target_pairs={{0,2},{1,3},{2,4},{3,5},{4,6},{5,7},{6,0},{7,1},{8,14},{9,15},{10,... | collective-permute-start | bytes 1966088 | tf_op jit(solution)/shard_map/ppermute | solution.py:31
  57.9 21.1 %collective-permute-start.14 = (bf16[8,160,256]{2,1,0:T(8,128)(2,1)}, bf16[8,160,256]{2,1,0:T(8,128)(2,1)}, u32[]{:S(2)}, u32[]{:S(2)}) collective-permute-start(bf16[8,160,256]{2,1,0:T(8,128)(2,1)} %shard_map.91.w0), channel_id=1, source_target_pairs={{0,16},{1,17},{2,18},{3,19},{4,20},{5,21},{6,22},{7,23},{8,24},{9,... | collective-permute-start | bytes 1966088 | tf_op jit(solution)/shard_map/ppermute | solution.py:31
  58.9 20.1 %collective-permute-start.15 = (bf16[8,160,256]{2,1,0:T(8,128)(2,1)}, bf16[8,160,256]{2,1,0:T(8,128)(2,1)}, u32[]{:S(2)}, u32[]{:S(2)}) collective-permute-start(bf16[8,160,256]{2,1,0:T(8,128)(2,1)} %shard_map.91.w0), channel_id=1, source_target_pairs={{0,193},{1,64},{2,195},{3,66},{4,197},{5,68},{6,199},{7,70},{8,201... | collective-permute-start | bytes 1966088 | tf_op jit(solution)/shard_map/ppermute | solution.py:31
  63.8 15.7 %collective-permute-start.16 = (bf16[8,160,256]{2,1,0:T(8,128)(2,1)}, bf16[8,160,256]{2,1,0:T(8,128)(2,1)}, u32[]{:S(2)}, u32[]{:S(2)}) collective-permute-start(bf16[8,160,256]{2,1,0:T(8,128)(2,1)} %shard_map.91.w0), channel_id=1, source_target_pairs={{0,48},{1,49},{2,50},{3,51},{4,52},{5,53},{6,54},{7,55},{8,56},{9,... | collective-permute-start | bytes 1966088 | tf_op jit(solution)/shard_map/ppermute | solution.py:31
  65.4 4.2 %copy-start.3 = (bf16[1,640,512]{2,1,0:T(8,128)(2,1)S(1)}, bf16[1,640,512]{2,1,0:T(8,128)(2,1)}, u32[]{:S(2)}) copy-start(bf16[1,640,512]{2,1,0:T(8,128)(2,1)} %copy-done.2) | copy-start | bytes 1966084
  65.4 4.6 %copy-start.7 = (bf16[2,640,512]{2,1,0:T(8,128)(2,1)S(1)}, bf16[2,640,512]{2,1,0:T(8,128)(2,1)}, u32[]{:S(2)}) copy-start(bf16[2,640,512]{2,1,0:T(8,128)(2,1)} %copy-done.6) | copy-start | bytes 3932164
  71.3 16.7 %collective-permute-start.23 = (bf16[640,512]{1,0:T(8,128)(2,1)S(1)}, bf16[640,512]{1,0:T(8,128)(2,1)S(1)}, u32[]{:S(2)}, u32[]{:S(2)}) collective-permute-start(bf16[640,512]{1,0:T(8,128)(2,1)S(1)} %fusion.1), channel_id=1, source_target_pairs={{0,1},{1,0},{2,3},{3,2},{4,5},{5,4},{6,7},{7,6},{8,9},{9,8},{10,11... | collective-permute-start | bytes 1966088 | tf_op jit(solution)/shard_map/ppermute | solution.py:31
  75.6 12.4 %collective-permute-start.20 = (bf16[1,640,512]{2,1,0:T(8,128)(2,1)S(1)}, bf16[1,640,512]{2,1,0:T(8,128)(2,1)S(1)}, u32[]{:S(2)}, u32[]{:S(2)}) collective-permute-start(bf16[1,640,512]{2,1,0:T(8,128)(2,1)S(1)} %add.187), channel_id=1, source_target_pairs={{0,2},{1,3},{2,4},{3,5},{4,6},{5,7},{6,0},{7,1},{8,14},{9,15},{10,... | collective-permute-start | bytes 1966088 | tf_op jit(solution)/shard_map/ppermute | solution.py:31
  85.0 4.3 %collective-permute-start.18 = (bf16[512,256]{1,0:T(8,128)(2,1)S(1)}, bf16[512,256]{1,0:T(8,128)(2,1)S(1)}, u32[]{:S(2)}, u32[]{:S(2)}) collective-permute-start(bf16[512,256]{1,0:T(8,128)(2,1)S(1)} %get-tuple-element.80), channel_id=1, source_target_pairs={{0,8},{1,9},{2,10},{3,11},{4,12},{5,13},{6,14},{7,15},{8,0},{9,1},... | collective-permute-start | bytes 786440 | tf_op jit(solution)/shard_map/ppermute | solution.py:31
  88.1 1.2 %copy-start.8 = (bf16[512,512]{1,0:T(8,128)(2,1)S(1)}, bf16[512,512]{1,0:T(8,128)(2,1)}, u32[]{:S(2)}) copy-start(bf16[512,512]{1,0:T(8,128)(2,1)} %get-tuple-element.79) | copy-start | bytes 1572868
  89.3 0.8 copy-start.9
